TPU v7x, 32 devices: a whole 2x2x4 slice. The times are simulated.
32 devices in a mesh: aux: 4 (over x, core), pair: 8 (over z, y).
Axes of the slice: x: 2, y: 2, z: 4, core: 2. Of those that a mesh axis runs over, the one named last changes fastest.
Arguments:
- three_centre: bfloat16 [48, 32, 128, 128], P('aux', 'pair'), may hold values from -6 to 6
- occ_green: bfloat16 [1024, 1024], P('pair'), as said below
- virt_green: bfloat16 [1024, 1024], replicated, may hold values from -0.25 to 0.25
- tile_cols: int32 [8, 4], replicated, may hold values from 0 to 7, as said below
- tile_live: int32 [8], replicated, may hold values from 1 to 4, as said below
Outputs:
- polarizability: float32 [48, 48], P('pair', 'aux')
Inputs may be any that keep to these rules, and one draw needn't show every extreme that they name: occ_green is symmetric. `tile_cols`: the 4 column blocks of one block row are distinct. `tile_live`: some block row has all 4 slots live.
All inputs are finite; a program needn't handle non-finite values.
Results may differ from a plain program's by a relative error of at most 0.015.
Values may be sent and summed in bfloat16 or wider, within the bound.
No kernel may reach another device: no remote copies, remote signals or barrier semaphores. Data moves between devices by JAX's collectives and lax.ppermute only.
A program may use at most 192 MiB of HBM per device.

v0:
```python
import math

import jax
import jax.numpy as jnp
from jax import lax
from jax.sharding import PartitionSpec as P


def per_device(three_centre, occ_green, virt_green, tile_cols, tile_live):
    width = three_centre.shape[2]
    slots = three_centre.shape[1]
    local_aux = three_centre.shape[0]
    blocks = lax.axis_size("pair")
    mine = lax.axis_index("pair")
    own_cols = lax.dynamic_index_in_dim(tile_cols, mine, 0, keepdims=False)
    own_live = lax.dynamic_index_in_dim(tile_live, mine, 0, keepdims=False)
    live_mask = jnp.arange(slots, dtype=jnp.int32) < own_live
    masked = jnp.where(live_mask[None, :, None, None], three_centre, jnp.zeros_like(three_centre))
    virt_rows = jnp.take(virt_green.reshape(blocks, width, blocks * width), own_cols, axis=0)
    virt_rows = virt_rows.reshape(slots, width, blocks, width)
    half = jnp.einsum(
        "qsab,sbjc->jqac", masked, virt_rows, preferred_element_type=jnp.float32
    ).astype(jnp.bfloat16)
    flat_cols = tile_cols.reshape(-1)
    occ_rows = occ_green.reshape(width, blocks, width)
    picked = jnp.take(half, flat_cols, axis=0)
    targets = jnp.arange(lax.axis_size("pair") * slots, dtype=jnp.int32) // slots
    occ_cols = jnp.take(occ_rows, targets, axis=1)
    summed = lax.psum_scatter(
        jnp.einsum("bta,tqbc->tqac", occ_cols, picked, preferred_element_type=jnp.float32).astype(
            jnp.bfloat16
        ),
        "pair",
        scatter_dimension=0,
        tiled=True,
    )
    polar_tiles = jnp.swapaxes(summed, 0, 1)
    live_tiles = jnp.where(live_mask[None, :, None, None], polar_tiles, jnp.zeros_like(polar_tiles))
    factor = 1.0 / (width * math.sqrt(slots * blocks))
    contract = (((1,), (1,)), ((), ()))
    flat_tiles = live_tiles.reshape(local_aux, -1)
    piece = lax.all_gather(three_centre, "aux", axis=0, tiled=True)
    columns = lax.dot_general(
        piece.reshape(piece.shape[0], -1), flat_tiles, contract, preferred_element_type=jnp.float32
    )
    chi = lax.psum_scatter(columns, "pair", scatter_dimension=0, tiled=True)
    return chi * factor


def solution(mesh):
    placed = (P("aux", "pair", None, None), P("pair", None), P(), P(), P())
    return jax.shard_map(
        per_device, mesh=mesh, in_specs=placed, out_specs=P("pair", "aux"), check_vma=False
    )
```

profile of v0, /device:TPU:0, one launch (start us, length us, event | category | flops | bytes accessed | tf_op | source)
XLA Modules:
  0.0 295.4 jit_solution(1731889131639249150)
XLA Ops:
  7.4 1.0 dynamic-slice_reduce_fusion
  8.4 0.8 copy.55
  9.2 0.1 reshape.137
  9.2 0.1 reshape.135
  9.4 0.6 gather_fusion
  10.0 1.3 copy.56
  11.3 0.6 dynamic_slice.8
  11.9 0.6 iota_compare_fusion
  12.5 5.3 %fusion.8 = bf16[8,12,128,128]{2,3,1,0:T(8,128)(2,1)} fusion(bf16[12,4,128,128]{3,2,1,0:T(8,128)(2,1)} %param.5, pred[4]{0:T(512)(128)(4,1)S(1)} %iota_compare_fusion, bf16[4,128,8,128]{1,3,2,0:T(8,128)(2,1)} %bitcast.48, pred[4]{0:T(512)(128)(4,1)S(1)} %compare_and_fusion.1), kind=kOutput, calls=%fused_computation.11 | convolution fusion | flops 1613496320 | bytes 5767176 | tf_op jit(solution)/shard_map/qsab,sbjc->jqac/dot_general | solution.py:21
  17.8 4.7 %copy.59 = bf16[8,12,128,128]{3,2,1,0:T(8,128)(2,1)} copy(bf16[8,12,128,128]{2,3,1,0:T(8,128)(2,1)} %fusion.8) | data formatting | bytes 6291456 | tf_op jit(solution)/shard_map/convert_element_type | solution.py:23
  22.6 0.2 copy.60
  22.8 0.2 copy.61
  23.0 8.6 %gather_fusion.1 = bf16[32,12,128,128]{3,2,1,0:T(8,128)(2,1)} fusion(bf16[8,12,128,128]{3,2,1,0:T(8,128)(2,1)} %copy.59, s32[1024]{0:T(1024)S(1)} %pad_clamp_fusion.1), kind=kCustom, calls=%fused_computation.1 | custom fusion | bytes 25165952 | tf_op jit(solution)/shard_map/jit(_take)/gather | solution.py:26
  31.5 0.7 gather_fusion.2
  32.3 9.7 %convert_bitcast_fusion = bf16[32,12,128,128]{2,3,1,0:T(8,128)(2,1)} fusion(bf16[32,12,128,128]{3,2,1,0:T(8,128)(2,1)} %gather_fusion.1, pred[32]{0:T(512)(128)(4,1)S(1)} %get-tuple-element.6, bf16[32,128,128]{2,1,0:T(8,128)(2,1)S(1)} %gather_fusion.2, pred[32]{0:T(512)(128)(4,1)S(1)} %get-tuple-element.5), kind=kOutput, calls=%fused_computation.3 | convolution fusion | flops 1623719936 | bytes 26214464 | tf_op jit(solution)/shard_map/bta,tqbc->tqac/dot_general | solution.py:30
  42.1 0.5 all-gather.2.cloned.1.call-update
  42.7 0.6 dynamic-slice
  43.9 208.2 %reduce-scatter.3.cloned.1.call-done = bf16[4,12,128,128]{2,3,1,0:T(8,128)(2,1)} async-done(((bf16[32,12,128,128]{2,3,1,0:T(8,128)(2,1)}), bf16[4,12,128,128]{2,3,1,0:T(8,128)(2,1)}) %reduce-scatter.3.cloned.1.call-update) | async-done | bytes 1572880 | tf_op jit(solution)/shard_map/reduce_scatter | solution.py:29
  252.1 2.7 select_bitcast_fusion
  254.9 4.4 %copy.63 = bf16[12,4,128,128]{3,0,2,1:T(8,128)(2,1)} copy(bf16[12,4,128,128]{2,3,0,1:T(8,128)(2,1)} %select_bitcast_fusion) | data formatting | bytes 3145728 | tf_op jit(solution)/shard_map/jit(_where)/select_n | solution.py:38
  259.3 8.2 %fusion.12 = f32[48,12]{0,1:T(8,128)S(1)} fusion(bf16[12,4,128,128]{3,0,2,1:T(8,128)(2,1)} %copy.63, bf16[48,4,128,128]{3,2,1,0:T(8,128)(2,1)} %all-gather.2.cloned.1.call-done), kind=kOutput, calls=%fused_computation.16 | convolution fusion | flops 75497472 | bytes 7866624 | tf_op jit(solution)/shard_map/dot_general | solution.py:43
  267.4 19.7 %all-reduce = f32[48,12]{0,1:T(8,128)S(1)} all-reduce(f32[48,12]{0,1:T(8,128)S(1)} %fusion.12), channel_id=3, replica_groups=mesh['aux'=4,'pair'=8] {'pair'}, use_global_device_ids=true, to_apply=%region_1.2.clone | all-reduce | flops 576 | bytes 4608
  287.2 0.1 copy.65
  287.3 0.6 broadcast_multiply_fusion
  (21 shorter events, 0.3 us)
Async XLA Ops:
  7.4 2.0 copy-start
  7.4 3.9 %copy-start.2 = (s32[8]{0:T(128)S(1)}, s32[8]{0:T(128)}, u32[]{:S(2)}) copy-start(s32[8]{0:T(128)} %param.9) | copy-start | bytes 100
  7.4 244.8 %reduce-scatter.3.cloned.1.call-start = ((), (), s32[]{:S(2)}) async-start(), calls=%async_computation.1 | async-start | bytes 14155776 | tf_op jit(solution)/shard_map/reduce_scatter | solution.py:29
  17.8 4.7 %copy-start.1 = (bf16[128,1024]{1,0:T(8,128)(2,1)S(1)}, bf16[128,1024]{1,0:T(8,128)(2,1)}, u32[]{:S(2)}) copy-start(bf16[128,1024]{1,0:T(8,128)(2,1)} %param.6) | copy-start | bytes 786436
  42.0 0.7 copy-start.3
  42.0 217.2 %all-gather.2.cloned.1.call-start = ((), (), s32[]{:S(2)}) async-start(), calls=%async_computation.2 | async-start | bytes 7864320 | tf_op jit(solution)/shard_map/all_gather | solution.py:42
Sparse Core Ops, SparseCore 0:
  42.2 209.9 reduce-scatter.2
Sparse Core Ops, SparseCore 1:
  44.1 48.9 all-gather.1
where the time goes:
time: 296 us; the launch traced here: 295 us
  waiting for transfers between devices  209 us (71%)
  local copies, waits for them, and re-layouts  24 us (8%)
  matrix products  23.2 us (8%)
  blocking collectives  19.7 us (7%)
  between operations  15.6 us (5%)
  other arithmetic  4.04 us (1%)
    reduce_scatter x1, waiting for transfers between devices, per_device(): lax.psum_scatter(jnp.einsum('bta,tqbc->tqac', occ_cols, picked, preferred...  208 us
    unnamed x1, blocking collectives  19.7 us
    dot_general x1, matrix products, per_device(): jnp.einsum('bta,tqbc->tqac', occ_cols, picked, preferred_element_type=jnp...  9.75 us
    gather x1, local copies, waits for them, and re-layouts, per_device(): picked = jnp.take(half, flat_cols, axis=0)  8.56 us
    dot_general x1, matrix products, per_device(): lax.dot_general(piece.reshape(piece.shape[0], -1), flat_tiles, contract,...  8.15 us
  transfers between devices with their start and end apart: 2, of which 1 were waited for; matrix products, arithmetic and copies ran while one was open for 3% of the time, Pallas kernels for 0%

commit v1 on v0

v1 whole, which is shorter than its diff:
```python
import math

import jax
import jax.numpy as jnp
from jax import lax
from jax.experimental import pallas as pl
from jax.experimental.pallas import tpu as pltpu
from jax.sharding import PartitionSpec as P

F32 = jnp.float32
BF16 = jnp.bfloat16
VMEM = pl.BlockSpec(memory_space=pltpu.VMEM)
SMEM = pl.BlockSpec(memory_space=pltpu.SMEM)


def split_kernel(groups, lows, tiles_ref, *outs):
    high = lax.axis_index("pair") // lows
    for n, out in enumerate(outs):
        c, d = divmod(n, groups)
        out[...] = tiles_ref[c * groups + lax.rem(high + d, groups)]


def split(tiles, groups, lows):
    count = tiles.shape[0]
    piece = jax.ShapeDtypeStruct(tiles.shape[1:], tiles.dtype)
    return pl.pallas_call(
        lambda *refs: split_kernel(groups, lows, *refs),
        out_shape=[piece] * count,
        in_specs=[VMEM],
        out_specs=[VMEM] * count,
        name="split",
    )(tiles)


def polar_kernel(groups, lows, cols_ref, live_ref, virt_ref, *rest):
    own = rest[:groups]
    others = rest[groups : groups + lows - 1]
    occ = rest[groups + lows - 1 : 2 * groups + lows - 1]
    outs = rest[2 * groups + lows - 1 : 3 * groups + lows - 1]
    half, lhs, full = rest[3 * groups + lows - 1 :]
    slots, width = own[0].shape[0], own[0].shape[1]
    basis = virt_ref.shape[0]
    me = lax.axis_index("pair")
    high, low = me // lows, lax.rem(me, lows)

    def block(index):
        return pl.ds(pl.multiple_of(index * width, width), width)

    for e in range(lows):
        for d in range(groups):
            tiles = own[d] if e == 0 else others[e - 1].at[d]
            row = lax.rem(high + groups - d, groups) * lows + lax.rem(low + lows - e, lows)
            alive = live_ref[row]

            def term(s):
                left, right = tiles[s], virt_ref[block(cols_ref[row, s]), :]
                if s + 1 < slots:
                    second = jnp.where(s + 1 < alive, tiles[s + 1], jnp.zeros_like(left))
                    left = jnp.concatenate([left, second], axis=1)
                    right = jnp.concatenate([right, virt_ref[block(cols_ref[row, s + 1]), :]], axis=0)
                return jnp.dot(left, right, preferred_element_type=F32)

            steps = list(range(0, slots, 2))
            for n in range(len(steps)):
                here = alive > steps[n]
                if n + 1 < len(steps):
                    here = jnp.logical_and(here, alive <= steps[n + 1])

                @pl.when(here)
                def _():
                    total = term(steps[0])
                    for s in steps[1 : n + 1]:
                        total += term(s)
                    half[block(row), :] = total.astype(BF16)

    for d in range(groups):
        lhs[d * width : (d + 1) * width, :] = occ[(groups - d) % groups][...]
    wide = 2 * width
    for j in range(0, basis, wide):
        full[:, j : j + wide] = jnp.dot(
            lhs[...], half[:, j : j + wide], preferred_element_type=F32
        ).astype(BF16)
    for d in range(groups):
        row = lax.rem(high + d, groups) * lows + low
        alive = live_ref[row]
        for s in range(slots):
            tile = full[d * width : (d + 1) * width, block(cols_ref[row, s])]
            outs[d][s] = jnp.where(s < alive, tile, jnp.zeros_like(tile))


def polar(cols, live, virt, own, others, occ):
    groups, lows = len(own), len(others) + 1
    slots, width = own[0].shape[0], own[0].shape[1]
    basis = virt.shape[0]
    return pl.pallas_call(
        lambda *refs: polar_kernel(groups, lows, *refs),
        out_shape=[jax.ShapeDtypeStruct(own[0].shape, BF16)] * groups,
        in_specs=[SMEM, SMEM] + [VMEM] * (1 + len(own) + len(others) + len(occ)),
        out_specs=[VMEM] * groups,
        scratch_shapes=[
            pltpu.VMEM((basis, basis), BF16),
            pltpu.VMEM((groups * width, basis), BF16),
            pltpu.VMEM((groups * width, basis), BF16),
        ],
        compiler_params=pltpu.CompilerParams(vmem_limit_bytes=56 * 2**20),
        cost_estimate=pl.CostEstimate(
            flops=2 * basis * basis * (slots * width + groups * width),
            bytes_accessed=2 * basis * basis * 3,
            transcendentals=0,
        ),
        name="polar",
    )(cols, live, virt, *own, *others, *occ)


def chi_kernel(groups, lows, factor, all_ref, *rest):
    pieces, out = rest[:-1], rest[-1]
    count, rows, width = all_ref.shape
    high = lax.axis_index("pair") // lows
    step = 16
    total = jnp.zeros((count * step, len(pieces) * step), F32)
    for r in range(0, rows, 2 * step):

        def both(ref):
            return [ref[..., r + k * step : r + (k + 1) * step, :] for k in range(2)]

        left = jnp.concatenate([x.reshape(count * step, width) for x in both(all_ref)], axis=1)
        right = jnp.concatenate(
            [jnp.concatenate(both(ref), axis=1) for ref in pieces], axis=0
        )
        total += lax.dot_general(
            left, right, (((1,), (1,)), ((), ())), preferred_element_type=F32
        )
    row = lax.broadcasted_iota(jnp.int32, total.shape, 0) % step
    col = lax.broadcasted_iota(jnp.int32, total.shape, 1)
    total = jnp.where(row == col % step, total, 0.0).reshape(count, step, total.shape[1])
    total = jnp.sum(total, axis=1)
    group = lax.broadcasted_iota(jnp.int32, total.shape, 1) // step
    place = lax.broadcasted_iota(jnp.int32, out.shape, 1)
    result = jnp.zeros(out.shape, F32)
    for n in range(len(pieces)):
        c, d = divmod(n, groups)
        q = c * groups + lax.rem(high + groups - d, groups)
        value = jnp.sum(jnp.where(group == n, total, 0.0), axis=1, keepdims=True)
        result = jnp.where(place == q, value, result)
    out[...] = result * factor


def chi(everyone, pieces, groups, lows, factor):
    count, slots, width, _ = everyone.shape
    flat = [p.reshape(slots * width, width) for p in pieces]
    return pl.pallas_call(
        lambda *refs: chi_kernel(groups, lows, factor, *refs),
        out_shape=jax.ShapeDtypeStruct((count, len(pieces)), F32),
        in_specs=[VMEM] * (1 + len(pieces)),
        out_specs=VMEM,
        compiler_params=pltpu.CompilerParams(vmem_limit_bytes=56 * 2**20),
        cost_estimate=pl.CostEstimate(
            flops=2 * count * len(pieces) * slots * width * width,
            bytes_accessed=2 * (count + len(pieces)) * slots * width * width,
            transcendentals=0,
        ),
        name="chi",
    )(everyone.reshape(count, slots * width, width), *flat)


def per_device(three_centre, occ_green, virt_green, tile_cols, tile_live):
    local, slots, width, _ = three_centre.shape
    blocks = lax.axis_size("pair")
    groups = math.gcd(local, blocks)
    lows = blocks // groups
    chunks = local // groups

    def along_high(array, d):
        moves = [
            (h * lows + l, (h + d) % groups * lows + l) for h in range(groups) for l in range(lows)
        ]
        return lax.ppermute(array, "pair", moves)

    def along_low(array, e):
        moves = [
            (h * lows + l, h * lows + (l + e) % lows) for h in range(groups) for l in range(lows)
        ]
        return lax.ppermute(array, "pair", moves)

    pieces = split(three_centre, groups, lows)
    own = []
    for c in range(chunks):
        mine = pieces[c * groups : (c + 1) * groups]
        own.append([mine[0]] + [along_high(mine[d], d) for d in range(1, groups)])
        if c == 0:
            occ = [occ_green] + [along_high(occ_green, d) for d in range(1, groups)]
    everyone = lax.all_gather(three_centre, "aux", axis=0, tiled=True)
    back = []
    for c in range(chunks):
        stacked = jnp.stack(own[c])
        others = [along_low(stacked, e) for e in range(1, lows)]
        tiles = polar(tile_cols, tile_live, virt_green, own[c], others, occ)
        back += [tiles[0]] + [along_high(tiles[d], d) for d in range(1, groups)]
    factor = 1.0 / (width * math.sqrt(slots * blocks))
    part = chi(everyone, back, groups, lows, factor)
    part = part.reshape(blocks, -1, local)
    return jnp.sum(lax.all_to_all(part, "pair", 0, 0, tiled=True), axis=0)


def solution(mesh):
    placed = (P("aux", "pair", None, None), P("pair", None), P(), P(), P())
    return jax.shard_map(
        per_device, mesh=mesh, in_specs=placed, out_specs=P("pair", "aux"), check_vma=False
    )
```

time: 296 us -> 142 us (0.48)
  waiting for transfers between devices: 209 us -> 35.4 us
  starting transfers between devices: 0.05 us -> 46.7 us
  Pallas kernels: 0 us -> 29 us
  matrix products: 23.2 us -> 0 us
  local copies, waits for them, and re-layouts: 24 us -> 3.65 us
  blocking collectives: 19.7 us -> 10.5 us
    reduce_scatter x1 -> x0, waiting for transfers between devices: 208 us -> none  [per_device(): lax.psum_scatter(jnp.einsum('bta,tqbc->tqac', occ_cols, picked, preferred...]
    ppermute x0 -> x24, starting transfers between devices: none -> 46.7 us  [the longest x21 41.5 us: along_high(): return lax.ppermute(array, 'pair', moves)]
    ppermute x0 -> x24, waiting for transfers between devices: none -> 34.6 us  [the longest x21 34.6 us: along_high(): return lax.ppermute(array, 'pair', moves)]
    pallas_call x0 -> x5, Pallas kernels: none -> 29 us  [the longest x3 20.5 us: polar(): pl.pallas_call(lambda *refs: polar_kernel(groups, lows, *refs), out_shape...]
    dot_general x3 -> x0, matrix products: 23.2 us -> none  [the longest x1 9.75 us: per_device(): jnp.einsum('bta,tqbc->tqac', occ_cols, picked, preferred_element_type=jnp...]
    unnamed x1 -> x0, blocking collectives: 19.7 us -> none
    gather x4 -> x0, local copies, waits for them, and re-layouts: 11.2 us -> none  [the longest x1 8.56 us: per_device(): picked = jnp.take(half, flat_cols, axis=0)]
    all_to_all x0 -> x1, blocking collectives: none -> 10.5 us  [per_device(): return jnp.sum(lax.all_to_all(part, 'pair', 0, 0, tiled=True), axis=0)]
  transfers between devices with their start and end apart: 2 -> 25, of which waited for: 1 -> 8; matrix products, arithmetic and copies ran while one was open for 3% -> 2% of each run, Pallas kernels for 0% -> 16%
where the time goes in v1:
time: 142 us
  starting transfers between devices  46.7 us (33%)
  waiting for transfers between devices  35.4 us (25%)
  Pallas kernels  29 us (20%)
  between operations  13.6 us (10%)
  blocking collectives  10.5 us (7%)
  local copies, waits for them, and re-layouts  3.65 us (3%)
  other arithmetic  2.67 us (2%)
    ppermute x21, starting transfers between devices, along_high(): return lax.ppermute(array, 'pair', moves)  41.5 us
    ppermute x21, waiting for transfers between devices, along_high(): return lax.ppermute(array, 'pair', moves)  34.6 us
    pallas_call x3, Pallas kernels, polar(): pl.pallas_call(lambda *refs: polar_kernel(groups, lows, *refs), out_shape...  20.5 us
    all_to_all x1, blocking collectives, per_device(): return jnp.sum(lax.all_to_all(part, 'pair', 0, 0, tiled=True), axis=0)  10.5 us
    pallas_call x1, Pallas kernels, chi(): pl.pallas_call(lambda *refs: chi_kernel(groups, lows, factor, *refs), out...  5.79 us
    ppermute x3, starting transfers between devices, along_low(): return lax.ppermute(array, 'pair', moves)  5.25 us
    unnamed x49, local copies, waits for them, and re-layouts  2.91 us
  transfers between devices with their start and end apart: 25, of which 8 were waited for; matrix products, arithmetic and copies ran while one was open for 2% of the time, Pallas kernels for 16%

profile of v1, /device:TPU:0, one launch (start us, length us, event | category | flops | bytes accessed | tf_op | source)
XLA Modules:
  0.0 141.5 jit_solution(13944054185506794461)
XLA Ops:
  7.3 2.7 %split.1 = (bf16[4,128,128]{2,1,0:T(8,128)(2,1)}, bf16[4,128,128]{2,1,0:T(8,128)(2,1)}, bf16[4,128,128]{2,1,0:T(8,128)(2,1)}, bf16[4,128,128]{2,1,0:T(8,128)(2,1...) custom-call(bf16[12,4,128,128]{3,2,1,0:T(8,128)(2,1)} %refs_0_.4), custom_call_target="tpu_custom_call" | custom-call | tf_op jit(solution)/shard_map/split/pallas_call | solution.py:26
  9.9 3.0 %collective-permute-start.17 = (bf16[4,128,128]{2,1,0:T(8,128)(2,1)}, bf16[4,128,128]{2,1,0:T(8,128)(2,1)S(1)}, u32[]{:S(2)}, u32[]{:S(2)}) collective-permute-start(bf16[4,128,128]{2,1,0:T(8,128)(2,1)} %get-tuple-element.46), channel_id=1, source_target_pairs={{0,2},{1,3},{2,4},{3,5},{4,6},{5,7},{6,0},{7,1},{8,10},{9,11},{10,... | collective-permute-start | bytes 393224 | tf_op jit(solution)/shard_map/ppermute | solution.py:177
  13.0 2.6 %collective-permute-start.18 = (bf16[4,128,128]{2,1,0:T(8,128)(2,1)}, bf16[4,128,128]{2,1,0:T(8,128)(2,1)S(1)}, u32[]{:S(2)}, u32[]{:S(2)}) collective-permute-start(bf16[4,128,128]{2,1,0:T(8,128)(2,1)} %get-tuple-element.47), channel_id=1, source_target_pairs={{0,4},{1,5},{2,6},{3,7},{4,0},{5,1},{6,2},{7,3},{8,12},{9,13},{10,... | collective-permute-start | bytes 393224 | tf_op jit(solution)/shard_map/ppermute | solution.py:177
  17.9 1.7 %collective-permute-done.17.refs_4_ = bf16[4,128,128]{2,1,0:T(8,128)(2,1)S(1)} collective-permute-done((bf16[4,128,128]{2,1,0:T(8,128)(2,1)}, bf16[4,128,128]{2,1,0:T(8,128)(2,1)S(1)}, u32[]{:S(2)}, u32[]{:S(2)}) %collective-permute-start.17) | collective-permute-done | bytes 131104 | tf_op jit(solution)/shard_map/ppermute | solution.py:177
  19.6 2.5 %collective-permute-start.12 = (bf16[4,128,128]{2,1,0:T(8,128)(2,1)}, bf16[4,128,128]{2,1,0:T(8,128)(2,1)S(1)}, u32[]{:S(2)}, u32[]{:S(2)}) collective-permute-start(bf16[4,128,128]{2,1,0:T(8,128)(2,1)} %get-tuple-element.40), channel_id=1, source_target_pairs={{0,6},{1,7},{2,0},{3,1},{4,2},{5,3},{6,4},{7,5},{8,14},{9,15},{10,... | collective-permute-start | bytes 393224 | tf_op jit(solution)/shard_map/ppermute | solution.py:177
  22.2 3.1 %collective-permute-done.18.refs_5_ = bf16[4,128,128]{2,1,0:T(8,128)(2,1)S(1)} collective-permute-done((bf16[4,128,128]{2,1,0:T(8,128)(2,1)}, bf16[4,128,128]{2,1,0:T(8,128)(2,1)S(1)}, u32[]{:S(2)}, u32[]{:S(2)}) %collective-permute-start.18) | collective-permute-done | bytes 131104 | tf_op jit(solution)/shard_map/ppermute | solution.py:177
  25.3 2.3 %collective-permute-done.19.refs_6_ = bf16[4,128,128]{2,1,0:T(8,128)(2,1)S(1)} collective-permute-done((bf16[4,128,128]{2,1,0:T(8,128)(2,1)}, bf16[4,128,128]{2,1,0:T(8,128)(2,1)S(1)}, u32[]{:S(2)}, u32[]{:S(2)}) %collective-permute-start.19) | collective-permute-done | bytes 131104 | tf_op jit(solution)/shard_map/ppermute | solution.py:177
  28.7 3.1 %collective-permute-start.20 = (bf16[4,4,128,128]{3,2,1,0:T(8,128)(2,1)S(1)}, bf16[4,4,128,128]{3,2,1,0:T(8,128)(2,1)S(1)}, u32[]{:S(2)}, u32[]{:S(2)}) collective-permute-start(bf16[4,4,128,128]{3,2,1,0:T(8,128)(2,1)S(1)} %pad_maximum_fusion.2), channel_id=1, source_target_pairs={{0,1},{1,0},{2,3},{3,2},{4,5},{5,4},{6,7},{7,6},{8,9},{9,8},{10,11... | collective-permute-start | bytes 1572872 | tf_op jit(solution)/shard_map/ppermute | solution.py:183
  31.7 5.4 %collective-permute-start = (bf16[4,128,128]{2,1,0:T(8,128)(2,1)}, bf16[4,128,128]{2,1,0:T(8,128)(2,1)S(1)}, u32[]{:S(2)}, u32[]{:S(2)}) collective-permute-start(bf16[4,128,128]{2,1,0:T(8,128)(2,1)} %get-tuple-element.30), channel_id=1, source_target_pairs={{0,2},{1,3},{2,4},{3,5},{4,6},{5,7},{6,0},{7,1},{8,10},{9,11},{10,... | collective-permute-start | bytes 393224 | tf_op jit(solution)/shard_map/ppermute | solution.py:177
  38.9 2.8 %collective-permute-start.2 = (bf16[4,128,128]{2,1,0:T(8,128)(2,1)}, bf16[4,128,128]{2,1,0:T(8,128)(2,1)S(1)}, u32[]{:S(2)}, u32[]{:S(2)}) collective-permute-start(bf16[4,128,128]{2,1,0:T(8,128)(2,1)} %get-tuple-element.32), channel_id=1, source_target_pairs={{0,6},{1,7},{2,0},{3,1},{4,2},{5,3},{6,4},{7,5},{8,14},{9,15},{10,... | collective-permute-start | bytes 393224 | tf_op jit(solution)/shard_map/ppermute | solution.py:177
  43.6 9.1 %collective-permute-done.1.refs_5_ = bf16[4,128,128]{2,1,0:T(8,128)(2,1)S(1)} collective-permute-done((bf16[4,128,128]{2,1,0:T(8,128)(2,1)}, bf16[4,128,128]{2,1,0:T(8,128)(2,1)S(1)}, u32[]{:S(2)}, u32[]{:S(2)}) %collective-permute-start.1) | collective-permute-done | bytes 131104 | tf_op jit(solution)/shard_map/ppermute | solution.py:177
  54.4 2.8 %collective-permute-start.6 = (bf16[128,1024]{1,0:T(8,128)(2,1)S(1)}, bf16[128,1024]{1,0:T(8,128)(2,1)}, u32[]{:S(2)}, u32[]{:S(2)}) collective-permute-start(bf16[128,1024]{1,0:T(8,128)(2,1)S(1)} %copy-done.21), channel_id=1, source_target_pairs={{0,6},{1,7},{2,0},{3,1},{4,2},{5,3},{6,4},{7,5},{8,14},{9,15},{10,... | collective-permute-start | bytes 786440 | tf_op jit(solution)/shard_map/ppermute | solution.py:177
  60.0 8.5 %collective-permute-done.5.refs_10_ = bf16[128,1024]{1,0:T(8,128)(2,1)} collective-permute-done((bf16[128,1024]{1,0:T(8,128)(2,1)S(1)}, bf16[128,1024]{1,0:T(8,128)(2,1)}, u32[]{:S(2)}, u32[]{:S(2)}) %collective-permute-start.5) | collective-permute-done | bytes 262176 | tf_op jit(solution)/shard_map/ppermute | solution.py:177
  69.3 6.8 %polar.5 = (bf16[4,128,128]{2,1,0:T(8,128)(2,1)}, bf16[4,128,128]{2,1,0:T(8,128)(2,1)}, bf16[4,128,128]{2,1,0:T(8,128)(2,1)}, bf16[4,128,128]{2,1,0:T(8,128)(2,1)}) custom-call(s32[8,4]{1,0:T(8,128)} %copy.12.refs_0_, s32[8]{0:T(128)} %refs_1_.5, bf16[1024,1024]{1,0:T(8,128)(2,1)} %refs_2_.5, bf16[4,128,128]{2,1,0:T(8,128)(2,1)} %get-tuple-element.45.refs_3_, ...), custom_call_target="tpu_custom_call" | custom-call | flops 2147483648 | bytes 6291456 | tf_op jit(solution)/shard_map/polar/pallas_call | solution.py:95
  76.1 5.3 %collective-permute-start.21 = (bf16[4,128,128]{2,1,0:T(8,128)(2,1)}, bf16[4,128,128]{2,1,0:T(8,128)(2,1)S(1)}, u32[]{:S(2)}, u32[]{:S(2)}) collective-permute-start(bf16[4,128,128]{2,1,0:T(8,128)(2,1)} %get-tuple-element.50), channel_id=1, source_target_pairs={{0,2},{1,3},{2,4},{3,5},{4,6},{5,7},{6,0},{7,1},{8,10},{9,11},{10,... | collective-permute-start | bytes 393224 | tf_op jit(solution)/shard_map/ppermute | solution.py:177
  81.5 2.0 %collective-permute-start.22 = (bf16[4,128,128]{2,1,0:T(8,128)(2,1)}, bf16[4,128,128]{2,1,0:T(8,128)(2,1)S(1)}, u32[]{:S(2)}, u32[]{:S(2)}) collective-permute-start(bf16[4,128,128]{2,1,0:T(8,128)(2,1)} %get-tuple-element.51), channel_id=1, source_target_pairs={{0,4},{1,5},{2,6},{3,7},{4,0},{5,1},{6,2},{7,3},{8,12},{9,13},{10,... | collective-permute-start | bytes 393224 | tf_op jit(solution)/shard_map/ppermute | solution.py:177
  83.9 6.8 %polar.4 = (bf16[4,128,128]{2,1,0:T(8,128)(2,1)}, bf16[4,128,128]{2,1,0:T(8,128)(2,1)}, bf16[4,128,128]{2,1,0:T(8,128)(2,1)}, bf16[4,128,128]{2,1,0:T(8,128)(2,1)}) custom-call(s32[8,4]{1,0:T(8,128)} %copy.12.refs_0_, s32[8]{0:T(128)} %refs_1_.5, bf16[1024,1024]{1,0:T(8,128)(2,1)} %refs_2_.5, bf16[4,128,128]{2,1,0:T(8,128)(2,1)} %get-tuple-element.37.refs_3_, ...), custom_call_target="tpu_custom_call" | custom-call | flops 2147483648 | bytes 6291456 | tf_op jit(solution)/shard_map/polar/pallas_call | solution.py:95
  93.2 7.0 %polar.3 = (bf16[4,128,128]{2,1,0:T(8,128)(2,1)}, bf16[4,128,128]{2,1,0:T(8,128)(2,1)}, bf16[4,128,128]{2,1,0:T(8,128)(2,1)}, bf16[4,128,128]{2,1,0:T(8,128)(2,1)}) custom-call(s32[8,4]{1,0:T(8,128)} %copy.12.refs_0_, s32[8]{0:T(128)} %refs_1_.5, bf16[1024,1024]{1,0:T(8,128)(2,1)} %refs_2_.5, bf16[4,128,128]{2,1,0:T(8,128)(2,1)} %get-tuple-element.29.refs_3_, ...), custom_call_target="tpu_custom_call" | custom-call | flops 2147483648 | bytes 6291456 | tf_op jit(solution)/shard_map/polar/pallas_call | solution.py:95
  102.3 2.0 %collective-permute-start.8 = (bf16[4,128,128]{2,1,0:T(8,128)(2,1)}, bf16[4,128,128]{2,1,0:T(8,128)(2,1)S(1)}, u32[]{:S(2)}, u32[]{:S(2)}) collective-permute-start(bf16[4,128,128]{2,1,0:T(8,128)(2,1)} %get-tuple-element.35), channel_id=1, source_target_pairs={{0,4},{1,5},{2,6},{3,7},{4,0},{5,1},{6,2},{7,3},{8,12},{9,13},{10,... | collective-permute-start | bytes 393224 | tf_op jit(solution)/shard_map/ppermute | solution.py:177
  104.3 2.2 %collective-permute-start.9 = (bf16[4,128,128]{2,1,0:T(8,128)(2,1)}, bf16[4,128,128]{2,1,0:T(8,128)(2,1)S(1)}, u32[]{:S(2)}, u32[]{:S(2)}) collective-permute-start(bf16[4,128,128]{2,1,0:T(8,128)(2,1)} %get-tuple-element.36), channel_id=1, source_target_pairs={{0,6},{1,7},{2,0},{3,1},{4,2},{5,3},{6,4},{7,5},{8,14},{9,15},{10,... | collective-permute-start | bytes 393224 | tf_op jit(solution)/shard_map/ppermute | solution.py:177
  106.5 2.8 %collective-permute-done.16 = bf16[4,128,128]{2,1,0:T(8,128)(2,1)S(1)} collective-permute-done((bf16[4,128,128]{2,1,0:T(8,128)(2,1)S(1)}, bf16[4,128,128]{2,1,0:T(8,128)(2,1)S(1)}, u32[]{:S(2)}, u32[]{:S(2)}) %collective-permute-start.16) | collective-permute-done | bytes 131104 | tf_op jit(solution)/shard_map/ppermute | solution.py:177
  110.9 5.5 %collective-permute-done.8 = bf16[4,128,128]{2,1,0:T(8,128)(2,1)S(1)} collective-permute-done((bf16[4,128,128]{2,1,0:T(8,128)(2,1)}, bf16[4,128,128]{2,1,0:T(8,128)(2,1)S(1)}, u32[]{:S(2)}, u32[]{:S(2)}) %collective-permute-start.8) | collective-permute-done | bytes 131104 | tf_op jit(solution)/shard_map/ppermute | solution.py:177
  117.0 5.8 %chi.1 = f32[48,12]{1,0:T(8,128)} custom-call(bf16[48,512,128]{2,1,0:T(8,128)(2,1)} %bitcast.25, bf16[512,128]{1,0:T(8,128)(2,1)} %bitcast.33, bf16[512,128]{1,0:T(8,128)(2,1)} %bitcast.35, bf16[512,128]{1,0:T(8,128)(2,1)} %bitcast.36, bf16[512,128]{1,0:T(8,128)(2,1)} %bitcast.37, bf16[512,128]{1,0:T(8,128)(2,1)} %bitcast.30, bf16[512,128]{1,0:T(8,128)(2,1)} %bitcast.31, ...), custom_call_target="tpu_custom_call" | custom-call | flops 75497472 | bytes 7864320 | tf_op jit(solution)/shard_map/chi/pallas_call | solution.py:151
  123.6 10.5 %all_to_all.5 = f32[8,6,12]{2,1,0:T(8,128)S(1)} all-to-all(f32[8,6,12]{2,1,0:T(8,128)S(1)} %reshape.55), channel_id=1, replica_groups=mesh['aux'=4,'pair'=8] {'pair'}, dimensions={0} | all-to-all | bytes 4608 | tf_op jit(solution)/shard_map/all_to_all | solution.py:202
  (87 shorter events, 21.5 us)
Async XLA Ops:
  6.5 109.8 %all-gather.2.cloned.1.call-start = ((), (), s32[]{:S(2)}) async-start(), calls=%async_computation.1 | async-start | bytes 7864320 | tf_op jit(solution)/shard_map/all_gather | solution.py:192
  9.9 9.7 %collective-permute-start.17 = (bf16[4,128,128]{2,1,0:T(8,128)(2,1)}, bf16[4,128,128]{2,1,0:T(8,128)(2,1)S(1)}, u32[]{:S(2)}, u32[]{:S(2)}) collective-permute-start(bf16[4,128,128]{2,1,0:T(8,128)(2,1)} %get-tuple-element.46), channel_id=1, source_target_pairs={{0,2},{1,3},{2,4},{3,5},{4,6},{5,7},{6,0},{7,1},{8,10},{9,11},{10,... | collective-permute-start | bytes 393224 | tf_op jit(solution)/shard_map/ppermute | solution.py:177
  13.0 12.3 %collective-permute-start.18 = (bf16[4,128,128]{2,1,0:T(8,128)(2,1)}, bf16[4,128,128]{2,1,0:T(8,128)(2,1)S(1)}, u32[]{:S(2)}, u32[]{:S(2)}) collective-permute-start(bf16[4,128,128]{2,1,0:T(8,128)(2,1)} %get-tuple-element.47), channel_id=1, source_target_pairs={{0,4},{1,5},{2,6},{3,7},{4,0},{5,1},{6,2},{7,3},{8,12},{9,13},{10,... | collective-permute-start | bytes 393224 | tf_op jit(solution)/shard_map/ppermute | solution.py:177
  15.6 12.1 %collective-permute-start.19 = (bf16[4,128,128]{2,1,0:T(8,128)(2,1)}, bf16[4,128,128]{2,1,0:T(8,128)(2,1)S(1)}, u32[]{:S(2)}, u32[]{:S(2)}) collective-permute-start(bf16[4,128,128]{2,1,0:T(8,128)(2,1)} %get-tuple-element.48), channel_id=1, source_target_pairs={{0,6},{1,7},{2,0},{3,1},{4,2},{5,3},{6,4},{7,5},{8,14},{9,15},{10,... | collective-permute-start | bytes 393224 | tf_op jit(solution)/shard_map/ppermute | solution.py:177
  16.9 20.2 %collective-permute-start.10 = (bf16[4,128,128]{2,1,0:T(8,128)(2,1)}, bf16[4,128,128]{2,1,0:T(8,128)(2,1)S(1)}, u32[]{:S(2)}, u32[]{:S(2)}) collective-permute-start(bf16[4,128,128]{2,1,0:T(8,128)(2,1)} %get-tuple-element.38), channel_id=1, source_target_pairs={{0,2},{1,3},{2,4},{3,5},{4,6},{5,7},{6,0},{7,1},{8,10},{9,11},{10,... | collective-permute-start | bytes 393224 | tf_op jit(solution)/shard_map/ppermute | solution.py:177
  17.6 19.6 %collective-permute-start.11 = (bf16[4,128,128]{2,1,0:T(8,128)(2,1)}, bf16[4,128,128]{2,1,0:T(8,128)(2,1)S(1)}, u32[]{:S(2)}, u32[]{:S(2)}) collective-permute-start(bf16[4,128,128]{2,1,0:T(8,128)(2,1)} %get-tuple-element.39), channel_id=1, source_target_pairs={{0,4},{1,5},{2,6},{3,7},{4,0},{5,1},{6,2},{7,3},{8,12},{9,13},{10,... | collective-permute-start | bytes 393224 | tf_op jit(solution)/shard_map/ppermute | solution.py:177
  19.6 19.3 %collective-permute-start.12 = (bf16[4,128,128]{2,1,0:T(8,128)(2,1)}, bf16[4,128,128]{2,1,0:T(8,128)(2,1)S(1)}, u32[]{:S(2)}, u32[]{:S(2)}) collective-permute-start(bf16[4,128,128]{2,1,0:T(8,128)(2,1)} %get-tuple-element.40), channel_id=1, source_target_pairs={{0,6},{1,7},{2,0},{3,1},{4,2},{5,3},{6,4},{7,5},{8,14},{9,15},{10,... | collective-permute-start | bytes 393224 | tf_op jit(solution)/shard_map/ppermute | solution.py:177
  28.7 39.8 %collective-permute-start.20 = (bf16[4,4,128,128]{3,2,1,0:T(8,128)(2,1)S(1)}, bf16[4,4,128,128]{3,2,1,0:T(8,128)(2,1)S(1)}, u32[]{:S(2)}, u32[]{:S(2)}) collective-permute-start(bf16[4,4,128,128]{3,2,1,0:T(8,128)(2,1)S(1)} %pad_maximum_fusion.2), channel_id=1, source_target_pairs={{0,1},{1,0},{2,3},{3,2},{4,5},{5,4},{6,7},{7,6},{8,9},{9,8},{10,11... | collective-permute-start | bytes 1572872 | tf_op jit(solution)/shard_map/ppermute | solution.py:183
  31.7 11.0 %collective-permute-start = (bf16[4,128,128]{2,1,0:T(8,128)(2,1)}, bf16[4,128,128]{2,1,0:T(8,128)(2,1)S(1)}, u32[]{:S(2)}, u32[]{:S(2)}) collective-permute-start(bf16[4,128,128]{2,1,0:T(8,128)(2,1)} %get-tuple-element.30), channel_id=1, source_target_pairs={{0,2},{1,3},{2,4},{3,5},{4,6},{5,7},{6,0},{7,1},{8,10},{9,11},{10,... | collective-permute-start | bytes 393224 | tf_op jit(solution)/shard_map/ppermute | solution.py:177
  37.1 20.1 %collective-permute-start.4 = (bf16[128,1024]{1,0:T(8,128)(2,1)S(1)}, bf16[128,1024]{1,0:T(8,128)(2,1)S(1)}, u32[]{:S(2)}, u32[]{:S(2)}) collective-permute-start(bf16[128,1024]{1,0:T(8,128)(2,1)S(1)} %copy-done.21), channel_id=1, source_target_pairs={{0,2},{1,3},{2,4},{3,5},{4,6},{5,7},{6,0},{7,1},{8,10},{9,11},{10,... | collective-permute-start | bytes 786440 | tf_op jit(solution)/shard_map/ppermute | solution.py:177
  37.2 15.5 %collective-permute-start.1 = (bf16[4,128,128]{2,1,0:T(8,128)(2,1)}, bf16[4,128,128]{2,1,0:T(8,128)(2,1)S(1)}, u32[]{:S(2)}, u32[]{:S(2)}) collective-permute-start(bf16[4,128,128]{2,1,0:T(8,128)(2,1)} %get-tuple-element.31), channel_id=1, source_target_pairs={{0,4},{1,5},{2,6},{3,7},{4,0},{5,1},{6,2},{7,3},{8,12},{9,13},{10,... | collective-permute-start | bytes 393224 | tf_op jit(solution)/shard_map/ppermute | solution.py:177
  38.9 15.4 %collective-permute-start.2 = (bf16[4,128,128]{2,1,0:T(8,128)(2,1)}, bf16[4,128,128]{2,1,0:T(8,128)(2,1)S(1)}, u32[]{:S(2)}, u32[]{:S(2)}) collective-permute-start(bf16[4,128,128]{2,1,0:T(8,128)(2,1)} %get-tuple-element.32), channel_id=1, source_target_pairs={{0,6},{1,7},{2,0},{3,1},{4,2},{5,3},{6,4},{7,5},{8,14},{9,15},{10,... | collective-permute-start | bytes 393224 | tf_op jit(solution)/shard_map/ppermute | solution.py:177
  42.8 41.1 %collective-permute-start.13 = (bf16[4,4,128,128]{3,2,1,0:T(8,128)(2,1)S(1)}, bf16[4,4,128,128]{3,2,1,0:T(8,128)(2,1)}, u32[]{:S(2)}, u32[]{:S(2)}) collective-permute-start(bf16[4,4,128,128]{3,2,1,0:T(8,128)(2,1)S(1)} %pad_maximum_fusion.1), channel_id=1, source_target_pairs={{0,1},{1,0},{2,3},{3,2},{4,5},{5,4},{6,7},{7,6},{8,9},{9,8},{10,11... | collective-permute-start | bytes 1572872 | tf_op jit(solution)/shard_map/ppermute | solution.py:183
  52.7 15.7 %collective-permute-start.5 = (bf16[128,1024]{1,0:T(8,128)(2,1)S(1)}, bf16[128,1024]{1,0:T(8,128)(2,1)}, u32[]{:S(2)}, u32[]{:S(2)}) collective-permute-start(bf16[128,1024]{1,0:T(8,128)(2,1)S(1)} %copy-done.21), channel_id=1, source_target_pairs={{0,4},{1,5},{2,6},{3,7},{4,0},{5,1},{6,2},{7,3},{8,12},{9,13},{10,... | collective-permute-start | bytes 786440 | tf_op jit(solution)/shard_map/ppermute | solution.py:177
  54.4 14.1 %collective-permute-start.6 = (bf16[128,1024]{1,0:T(8,128)(2,1)S(1)}, bf16[128,1024]{1,0:T(8,128)(2,1)}, u32[]{:S(2)}, u32[]{:S(2)}) collective-permute-start(bf16[128,1024]{1,0:T(8,128)(2,1)S(1)} %copy-done.21), channel_id=1, source_target_pairs={{0,6},{1,7},{2,0},{3,1},{4,2},{5,3},{6,4},{7,5},{8,14},{9,15},{10,... | collective-permute-start | bytes 786440 | tf_op jit(solution)/shard_map/ppermute | solution.py:177
  57.9 34.3 %collective-permute-start.3 = (bf16[4,4,128,128]{3,2,1,0:T(8,128)(2,1)S(1)}, bf16[4,4,128,128]{3,2,1,0:T(8,128)(2,1)}, u32[]{:S(2)}, u32[]{:S(2)}) collective-permute-start(bf16[4,4,128,128]{3,2,1,0:T(8,128)(2,1)S(1)} %pad_maximum_fusion), channel_id=1, source_target_pairs={{0,1},{1,0},{2,3},{3,2},{4,5},{5,4},{6,7},{7,6},{8,9},{9,8},{10,11... | collective-permute-start | bytes 1572872 | tf_op jit(solution)/shard_map/ppermute | solution.py:183
  76.1 24.0 %collective-permute-start.21 = (bf16[4,128,128]{2,1,0:T(8,128)(2,1)}, bf16[4,128,128]{2,1,0:T(8,128)(2,1)S(1)}, u32[]{:S(2)}, u32[]{:S(2)}) collective-permute-start(bf16[4,128,128]{2,1,0:T(8,128)(2,1)} %get-tuple-element.50), channel_id=1, source_target_pairs={{0,2},{1,3},{2,4},{3,5},{4,6},{5,7},{6,0},{7,1},{8,10},{9,11},{10,... | collective-permute-start | bytes 393224 | tf_op jit(solution)/shard_map/ppermute | solution.py:177
  81.5 20.3 %collective-permute-start.22 = (bf16[4,128,128]{2,1,0:T(8,128)(2,1)}, bf16[4,128,128]{2,1,0:T(8,128)(2,1)S(1)}, u32[]{:S(2)}, u32[]{:S(2)}) collective-permute-start(bf16[4,128,128]{2,1,0:T(8,128)(2,1)} %get-tuple-element.51), channel_id=1, source_target_pairs={{0,4},{1,5},{2,6},{3,7},{4,0},{5,1},{6,2},{7,3},{8,12},{9,13},{10,... | collective-permute-start | bytes 393224 | tf_op jit(solution)/shard_map/ppermute | solution.py:177
  83.5 18.8 %collective-permute-start.23 = (bf16[4,128,128]{2,1,0:T(8,128)(2,1)}, bf16[4,128,128]{2,1,0:T(8,128)(2,1)S(1)}, u32[]{:S(2)}, u32[]{:S(2)}) collective-permute-start(bf16[4,128,128]{2,1,0:T(8,128)(2,1)} %get-tuple-element.52), channel_id=1, source_target_pairs={{0,6},{1,7},{2,0},{3,1},{4,2},{5,3},{6,4},{7,5},{8,14},{9,15},{10,... | collective-permute-start | bytes 393224 | tf_op jit(solution)/shard_map/ppermute | solution.py:177
  90.7 13.6 %collective-permute-start.14 = (bf16[4,128,128]{2,1,0:T(8,128)(2,1)}, bf16[4,128,128]{2,1,0:T(8,128)(2,1)S(1)}, u32[]{:S(2)}, u32[]{:S(2)}) collective-permute-start(bf16[4,128,128]{2,1,0:T(8,128)(2,1)} %get-tuple-element.42), channel_id=1, source_target_pairs={{0,2},{1,3},{2,4},{3,5},{4,6},{5,7},{6,0},{7,1},{8,10},{9,11},{10,... | collective-permute-start | bytes 393224 | tf_op jit(solution)/shard_map/ppermute | solution.py:177
  92.3 14.3 %collective-permute-start.15 = (bf16[4,128,128]{2,1,0:T(8,128)(2,1)}, bf16[4,128,128]{2,1,0:T(8,128)(2,1)S(1)}, u32[]{:S(2)}, u32[]{:S(2)}) collective-permute-start(bf16[4,128,128]{2,1,0:T(8,128)(2,1)} %get-tuple-element.43), channel_id=1, source_target_pairs={{0,4},{1,5},{2,6},{3,7},{4,0},{5,1},{6,2},{7,3},{8,12},{9,13},{10,... | collective-permute-start | bytes 393224 | tf_op jit(solution)/shard_map/ppermute | solution.py:177
  100.2 9.2 %collective-permute-start.16 = (bf16[4,128,128]{2,1,0:T(8,128)(2,1)S(1)}, bf16[4,128,128]{2,1,0:T(8,128)(2,1)S(1)}, u32[]{:S(2)}, u32[]{:S(2)}) collective-permute-start(bf16[4,128,128]{2,1,0:T(8,128)(2,1)S(1)} %copy-done.23), channel_id=1, source_target_pairs={{0,6},{1,7},{2,0},{3,1},{4,2},{5,3},{6,4},{7,5},{8,14},{9,15},{10,... | collective-permute-start | bytes 393224 | tf_op jit(solution)/shard_map/ppermute | solution.py:177
  102.3 14.0 %collective-permute-start.8 = (bf16[4,128,128]{2,1,0:T(8,128)(2,1)}, bf16[4,128,128]{2,1,0:T(8,128)(2,1)S(1)}, u32[]{:S(2)}, u32[]{:S(2)}) collective-permute-start(bf16[4,128,128]{2,1,0:T(8,128)(2,1)} %get-tuple-element.35), channel_id=1, source_target_pairs={{0,4},{1,5},{2,6},{3,7},{4,0},{5,1},{6,2},{7,3},{8,12},{9,13},{10,... | collective-permute-start | bytes 393224 | tf_op jit(solution)/shard_map/ppermute | solution.py:177
  104.3 12.0 %collective-permute-start.9 = (bf16[4,128,128]{2,1,0:T(8,128)(2,1)}, bf16[4,128,128]{2,1,0:T(8,128)(2,1)S(1)}, u32[]{:S(2)}, u32[]{:S(2)}) collective-permute-start(bf16[4,128,128]{2,1,0:T(8,128)(2,1)} %get-tuple-element.36), channel_id=1, source_target_pairs={{0,6},{1,7},{2,0},{3,1},{4,2},{5,3},{6,4},{7,5},{8,14},{9,15},{10,... | collective-permute-start | bytes 393224 | tf_op jit(solution)/shard_map/ppermute | solution.py:177
  (25 other events, 555.6 us)
Sparse Core Ops, SparseCore 0:
  8.9 49.0 all-gather.1

commit v2 on v0

v2 whole, which is shorter than its diff:
```python
import math

import jax
import jax.numpy as jnp
from jax import lax
from jax.experimental import pallas as pl
from jax.experimental.pallas import tpu as pltpu
from jax.sharding import PartitionSpec as P

F32 = jnp.float32
BF16 = jnp.bfloat16
VMEM = pl.BlockSpec(memory_space=pltpu.VMEM)
SMEM = pl.BlockSpec(memory_space=pltpu.SMEM)
MIB = 2**20
QUICK = pl.CostEstimate(flops=0, bytes_accessed=2**20, transcendentals=0)
LONG = pl.CostEstimate(flops=2 * 10**11, bytes_accessed=2**28, transcendentals=0)


def size_of(shapes):
    return sum(math.prod(s.shape) * s.dtype.itemsize for s in shapes)


def rows_at(index, extent):
    return pl.ds(pl.multiple_of(index * extent, extent), extent)


def split_kernel(groups, lows, chunk, shares, copied, tiles_ref, *rest):
    high = lax.axis_index("pair") // lows
    slots, width = tiles_ref.shape[1], tiles_ref.shape[2]
    outs = rest if chunk else rest[1:]
    for d in range(groups):
        outs[d][0:slots] = tiles_ref[chunk * groups + lax.rem(high + d, groups)]
    if chunk == 0:
        occ_ref, part = rest[0], width // shares
        share = lax.axis_index("aux") if shares > 1 else 0
        for d in range(1, groups):
            for j in range(occ_ref.shape[1] // width):
                at = j * part
                outs[d][slots + at // width, at % width : at % width + part, :] = occ_ref[
                    rows_at(share, part), j * width : (j + 1) * width
                ]
    for out, (low, high) in zip(outs[groups:], copied):
        out[...] = tiles_ref[low:high]


def split(tiles, occ, groups, lows, chunk, shares, copied=()):
    _, slots, width, _ = tiles.shape
    extra = occ.shape[1] // (width * shares) if chunk == 0 else 0
    shapes = [
        jax.ShapeDtypeStruct((slots + (extra if d else 0), width, width), tiles.dtype)
        for d in range(groups)
    ]
    shapes += [jax.ShapeDtypeStruct((h - l,) + tiles.shape[1:], tiles.dtype) for l, h in copied]
    args = [tiles] if chunk else [tiles, occ]
    whole = lambda shape: pl.BlockSpec(shape, lambda _: (0,) * len(shape))
    specs = [whole(a.shape) for a in args]
    if chunk == 0:
        specs[0] = whole((groups,) + tiles.shape[1:])
    out = pl.pallas_call(
        lambda *refs: split_kernel(groups, lows, chunk, shares, copied, *refs),
        grid=(1,),
        out_shape=shapes,
        in_specs=specs,
        out_specs=[whole(s.shape) for s in shapes],
        cost_estimate=LONG,
        name="split",
    )(*args)
    return list(out[:groups]), list(out[groups:])


def stack_kernel(groups, slots, *refs):
    pieces, outs = refs[:groups], refs[groups:]
    for d, piece in enumerate(pieces):
        outs[0][d] = piece[0:slots]
        if len(outs) > 1 and d > 0:
            outs[1][d - 1] = piece[slots:]


def stack(pieces, slots, cost):
    groups, width = len(pieces), pieces[0].shape[1]
    extra = pieces[-1].shape[0] - slots
    shapes = [jax.ShapeDtypeStruct((groups, slots, width, width), BF16)]
    if extra:
        shapes.append(jax.ShapeDtypeStruct((groups - 1, extra, width, width), BF16))
    return pl.pallas_call(
        lambda *refs: stack_kernel(groups, slots, *refs),
        out_shape=shapes,
        in_specs=[VMEM] * groups,
        out_specs=[VMEM] * len(shapes),
        cost_estimate=cost,
        name="stack",
    )(*pieces)


def polar_kernel(groups, lows, masks, cols_ref, live_ref, virt_ref, occ_ref, *rest):
    rest = list(rest)
    take = lambda n: [rest.pop(0) for _ in range(n)]
    own, others, shares, outs = take(groups), take(lows - 1), take(len(masks)), take(groups)
    half, lhs, full = rest
    slots, width = outs[0].shape[0], outs[0].shape[1]
    basis = virt_ref.shape[0]
    me = lax.axis_index("pair")
    high, low = me // lows, lax.rem(me, lows)

    for e in range(lows):
        for d in range(groups):
            tiles = own[d] if e == 0 else others[e - 1].at[d]
            row = lax.rem(high + groups - d, groups) * lows + lax.rem(low + lows - e, lows)
            alive = live_ref[row]

            def term(s):
                left = tiles[s]
                right = virt_ref[rows_at(cols_ref[row, s], width), :]
                if s + 1 < slots:
                    second = jnp.where(s + 1 < alive, tiles[s + 1], jnp.zeros_like(left))
                    left = jnp.concatenate([left, second], axis=1)
                    below = virt_ref[rows_at(cols_ref[row, s + 1], width), :]
                    right = jnp.concatenate([right, below], axis=0)
                return jnp.dot(left, right, preferred_element_type=F32)

            steps = list(range(0, slots, 2))
            for n in range(len(steps)):
                here = alive > steps[n]
                if n + 1 < len(steps):
                    here = jnp.logical_and(here, alive <= steps[n + 1])

                @pl.when(here)
                def _():
                    total = term(steps[0])
                    for s in steps[1 : n + 1]:
                        total += term(s)
                    half[rows_at(row, width), :] = total.astype(BF16)

    lhs[0:width, :] = occ_ref[...]
    for mask_list, share in zip(masks, shares):
        part = width // (len(masks) * len(mask_list))
        for k, mask in enumerate(mask_list):
            source = lax.axis_index("aux") ^ mask if part < width else 0
            for d in range(1, groups):
                base = (groups - d) * width
                for j in range(basis // width):
                    at = j * part
                    lhs[
                        pl.ds(pl.multiple_of(base + source * part, part), part),
                        j * width : (j + 1) * width,
                    ] = share[k, d - 1, at // width, at % width : at % width + part, :]
    wide = 2 * width
    for j in range(0, basis, wide):
        full[:, j : j + wide] = jnp.dot(
            lhs[...], half[:, j : j + wide], preferred_element_type=F32
        ).astype(BF16)
    for d in range(groups):
        row = lax.rem(high + d, groups) * lows + low
        alive = live_ref[row]
        for s in range(slots):
            tile = full[d * width : (d + 1) * width, rows_at(cols_ref[row, s], width)]
            outs[d][s] = jnp.where(s < alive, tile, jnp.zeros_like(tile))


def polar(cols, live, virt, occ, own, others, masks, shares):
    groups, lows = len(own), len(others) + 1
    slots, width = own[0].shape[0], own[0].shape[1]
    basis = virt.shape[0]
    shapes = [jax.ShapeDtypeStruct((slots, width, width), BF16)] * groups
    scratch = [(basis, basis), (groups * width, basis), (groups * width, basis)]
    arrays = [virt, occ, *own, *others, *shares]
    held = size_of(arrays) + size_of(shapes) + sum(2 * a * b for a, b in scratch)
    return pl.pallas_call(
        lambda *refs: polar_kernel(groups, lows, masks, *refs),
        out_shape=shapes,
        in_specs=[SMEM, SMEM] + [VMEM] * len(arrays),
        out_specs=[VMEM] * groups,
        scratch_shapes=[pltpu.VMEM(s, BF16) for s in scratch],
        compiler_params=pltpu.CompilerParams(vmem_limit_bytes=held + 12 * MIB),
        cost_estimate=LONG,
        name="polar",
    )(cols, live, *arrays)


def chi_kernel(groups, lows, chunks, factor, places, *rest):
    count = groups * len(chunks)
    everyone, pieces = rest[: len(places)], rest[len(places) : len(places) + count]
    prior, out = rest[len(places) + count : -1], rest[-1]
    _, rows, width = everyone[0].shape
    unit, local = out.shape[1], out.shape[2]
    high, aux = lax.axis_index("pair") // lows, lax.axis_index("aux")
    step = 16

    def pair(ref, r):
        halves = [ref[..., r + k * step : r + (k + 1) * step, :] for k in range(2)]
        return jnp.concatenate([x.reshape(-1, width) for x in halves], axis=1)

    rights = [
        jnp.concatenate([pair(ref, r) for ref in pieces], axis=0) for r in range(0, rows, 2 * step)
    ]

    def product(ref):
        total = jnp.zeros((ref.shape[0] * step, count * step), F32)
        for right, r in zip(rights, range(0, rows, 2 * step)):
            total += lax.dot_general(
                pair(ref, r), right, (((1,), (1,)), ((), ())), preferred_element_type=F32
            )
        row = lax.broadcasted_iota(jnp.int32, total.shape, 0) % step
        col = lax.broadcasted_iota(jnp.int32, total.shape, 1) % step
        total = jnp.where(row == col, total, 0.0).reshape(-1, step, total.shape[1])
        return jnp.sum(total, axis=1)

    for mask in sorted({m for m, _ in places}):
        mine = sorted((start, n) for n, (m, start) in enumerate(places) if m == mask)
        total = [product(everyone[n]) for _, n in mine]
        total = jnp.concatenate(total, axis=0) if len(total) > 1 else total[0]
        group = lax.broadcasted_iota(jnp.int32, total.shape, 1) // step
        place = lax.broadcasted_iota(jnp.int32, (local, local), 1)
        result = jnp.zeros((local, local), F32)
        for n in range(count):
            c, d = divmod(n, groups)
            q = chunks[c] * groups + lax.rem(high + groups - d, groups)
            value = jnp.sum(jnp.where(group == n, total, 0.0), axis=1, keepdims=True)
            result = jnp.where(place == q, value * factor, result)
        for u in range(local // unit):
            at = (aux ^ mask) * (local // unit) + u
            piece = result[u * unit : (u + 1) * unit]
            out[at] = piece + prior[0][at] if prior else piece


def chi(everyone, back, chunks, prior, groups, lows, local, unit, factor):
    pieces = [p for c in chunks for p in back[c]]
    slots, width = pieces[0].shape[0], pieces[0].shape[1]
    places = [place for place, _ in everyone]
    arrays = [e.reshape(-1, slots * width, width) for _, e in everyone]
    arrays += [p.reshape(slots * width, width) for p in pieces]
    if prior is not None:
        arrays.append(prior)
    count = sum(e.shape[0] for _, e in everyone)
    return pl.pallas_call(
        lambda *refs: chi_kernel(groups, lows, chunks, factor, places, *refs),
        out_shape=jax.ShapeDtypeStruct((count // unit, unit, local), F32),
        in_specs=[VMEM] * len(arrays),
        out_specs=VMEM,
        compiler_params=pltpu.CompilerParams(vmem_limit_bytes=size_of(arrays) + 12 * MIB),
        cost_estimate=LONG,
        name="chi",
    )(*arrays)


def per_device(three_centre, occ_green, virt_green, tile_cols, tile_live):
    local, slots, width, _ = three_centre.shape
    blocks, peers = lax.axis_size("pair"), lax.axis_size("aux")
    groups = math.gcd(local, blocks)
    lows = blocks // groups
    chunks = local // groups
    shares = peers if peers & (peers - 1) == 0 and blocks % peers == 0 else 1

    def along_high(array, d):
        moves = [
            (h * lows + l, (h + d) % groups * lows + l) for h in range(groups) for l in range(lows)
        ]
        return lax.ppermute(array, "pair", moves)

    def along_low(array, e):
        moves = [
            (h * lows + l, h * lows + (l + e) % lows) for h in range(groups) for l in range(lows)
        ]
        return lax.ppermute(array, "pair", moves)

    def swap(array, bit):
        return lax.ppermute(array, "aux", [(a, a ^ bit) for a in range(peers)])

    def shift(arrays, between=lambda: None):
        order = sorted(range(1, groups), key=lambda d: -min(d, groups - d))
        moved = {0: arrays[0]}
        for d in order:
            moved[d] = along_high(arrays[d], d)
            if d == order[0]:
                between()
        return [moved[d] for d in range(groups)]

    together = lax.optimization_barrier
    factor = 1.0 / (width * math.sqrt(slots * blocks))
    bits = [1 << n for n in reversed(range(peers.bit_length() - 1))]
    own, others, tiles, back = {}, {}, {}, {}
    parts, masks = [], [[0]]
    everyone = [((0, 0), three_centre)]
    part, per = None, local * peers // blocks
    unit = math.gcd(local, per)

    first_back = max(chunks, 3)
    cut = -(-local * 7 // 12) if chunks > 1 else local
    first, copies = split(three_centre, occ_green, groups, lows, 0, shares)
    sending = {0: first}
    for phase in range(first_back + chunks):

        def share_low():
            if phase - 1 in own:
                stacked, *extra = stack(own[phase - 1], slots, QUICK if phase == chunks else LONG)
                if extra:
                    parts[:] = [extra[0][None]]
                others[phase - 1] = [along_low(stacked, e) for e in range(1, lows)]

        if phase in sending:
            own[phase] = shift(sending.pop(phase), share_low)
        elif phase >= first_back:
            back[phase - first_back] = shift(tiles.pop(phase - first_back), share_low)
        else:
            share_low()
        if phase in (1, 2):
            for bit in bits[: len(bits) - 1] if phase == 1 else bits[len(bits) - 1 :]:
                parts, masks = parts + [swap(x, bit) for x in parts], masks + [[m[0] | bit] for m in masks]
        if phase + 1 < chunks:
            sending[phase + 1], more = split(
                three_centre, occ_green, groups, lows, phase + 1, shares,
                [(0, cut)] * (phase == 0) + [(cut, local)] * (phase + 2 == chunks),
            )
            copies = copies + more
        if phase == 0 and bits:
            first_part = swap(copies[0] if copies else three_centre, bits[0])
            everyone.append(((bits[0], 0), first_part))
            if len(bits) > 1:
                everyone.append(((bits[-1], 0), swap(three_centre, bits[-1])))
        if phase == first_back - 1 and bits and cut < local:
            everyone.append(((bits[0], cut), swap(copies[1], bits[0])))
        if phase - 2 in others:
            c, pieces = phase - 2, own[phase - 2]
            if phase == first_back - 1 + 1 and everyone[-1][0][1]:
                pieces = together((pieces, everyone[-1][1]))[0]
            tiles[c] = list(
                polar(tile_cols, tile_live, virt_green, occ_green, pieces, others.pop(c), masks, parts)
            )
        if phase == first_back + chunks - 1:
            for bit in bits[1:]:
                for (mask, start), array in list(everyone):
                    if (mask ^ bit, start) not in dict(everyone):
                        array = together((array, back[chunks - 2]))[0]
                        everyone.append(((mask ^ bit, start), swap(array, bit)))
            if chunks > 1:
                part = chi(
                    everyone, back, list(range(chunks - 1)), None, groups, lows, local, unit, factor
                )
        done = {}
        if phase == 0 and len(bits) > 1:
            done[2] = everyone[2][1]
        if phase == 1 and bits:
            done[1] = everyone[1][1]
        live = (three_centre, sending, copies, own if phase < first_back else {}, tiles, back, parts, part, done)
        three_centre, sending, copies, kept, tiles, back, parts, part, done = together(live)
        own = kept or own
        for n, array in done.items():
            everyone[n] = (everyone[n][0], array)
    part = chi(everyone, back, [chunks - 1], part, groups, lows, local, unit, factor)
    part = part.reshape(blocks, per, local)
    return jnp.sum(lax.all_to_all(part, "pair", 0, 0, tiled=True), axis=0)


def solution(mesh):
    placed = (P("aux", "pair", None, None), P("pair", None), P(), P(), P())
    return jax.shard_map(
        per_device, mesh=mesh, in_specs=placed, out_specs=P("pair", "aux"), check_vma=False
    )
```

time: 296 us -> 112 us (0.38)
  waiting for transfers between devices: 209 us -> 18.9 us
  Pallas kernels: 0 us -> 39.9 us
  starting transfers between devices: 0.05 us -> 39.9 us
  local copies, waits for them, and re-layouts: 24 us -> 0.11 us
  matrix products: 23.2 us -> 0 us
  between operations: 15.6 us -> 0.1 us
  blocking collectives: 19.7 us -> 11.7 us
  other arithmetic: 4.04 us -> 0.6 us
    reduce_scatter x1 -> x0, waiting for transfers between devices: 208 us -> none  [per_device(): lax.psum_scatter(jnp.einsum('bta,tqbc->tqac', occ_cols, picked, preferred...]
    pallas_call x0 -> x11, Pallas kernels: none -> 39.9 us  [the longest x3 18.3 us: polar(): pl.pallas_call(lambda *refs: polar_kernel(groups, lows, masks, *refs), ou...]
    ppermute x0 -> x29, starting transfers between devices: none -> 39.9 us  [the longest x18 30.6 us: along_high(): return lax.ppermute(array, 'pair', moves)]
    dot_general x3 -> x0, matrix products: 23.2 us -> none  [the longest x1 9.75 us: per_device(): jnp.einsum('bta,tqbc->tqac', occ_cols, picked, preferred_element_type=jnp...]
    unnamed x1 -> x0, blocking collectives: 19.7 us -> none
    ppermute x0 -> x29, waiting for transfers between devices: none -> 18.9 us  [the longest x18 13.1 us: along_high(): return lax.ppermute(array, 'pair', moves)]
    all_to_all x0 -> x1, blocking collectives: none -> 11.7 us  [per_device(): return jnp.sum(lax.all_to_all(part, 'pair', 0, 0, tiled=True), axis=0)]
    gather x4 -> x0, local copies, waits for them, and re-layouts: 11.2 us -> none  [the longest x1 8.56 us: per_device(): picked = jnp.take(half, flat_cols, axis=0)]
  transfers between devices with their start and end apart: 2 -> 29, of which waited for: 1 -> 8; matrix products, arithmetic and copies ran while one was open for 3% -> 0% of each run, Pallas kernels for 0% -> 32%
where the time goes in v2:
time: 112 us; the launch traced here: 111 us
  starting transfers between devices  39.9 us (36%)
  Pallas kernels  39.9 us (36%)
  waiting for transfers between devices  18.9 us (17%)
  blocking collectives  11.7 us (10%)
    ppermute x18, starting transfers between devices, along_high(): return lax.ppermute(array, 'pair', moves)  30.6 us
    pallas_call x3, Pallas kernels, polar(): pl.pallas_call(lambda *refs: polar_kernel(groups, lows, masks, *refs), ou...  18.3 us
    ppermute x18, waiting for transfers between devices, along_high(): return lax.ppermute(array, 'pair', moves)  13.1 us
    all_to_all x1, blocking collectives, per_device(): return jnp.sum(lax.all_to_all(part, 'pair', 0, 0, tiled=True), axis=0)  11.7 us
    pallas_call x2, Pallas kernels, chi(): pl.pallas_call(lambda *refs: chi_kernel(groups, lows, chunks, factor, pla...  8.16 us
    pallas_call x3, Pallas kernels, split(): pl.pallas_call(lambda *refs: split_kernel(groups, lows, chunk, shares, co...  7.24 us
    pallas_call x3, Pallas kernels, stack(): pl.pallas_call(lambda *refs: stack_kernel(groups, slots, *refs), out_shap...  6.21 us
    ppermute x8, starting transfers between devices, swap(): return lax.ppermute(array, 'aux', [(a, a ^ bit) for a in range(peers)])  4.68 us
  transfers between devices with their start and end apart: 29, of which 8 were waited for; matrix products, arithmetic and copies ran while one was open for 0% of the time, Pallas kernels for 32%

profile of v2, /device:TPU:0, one launch (start us, length us, event | category | flops | bytes accessed | tf_op | source)
XLA Modules:
  0.0 111.2 jit_solution(13346404611253924115)
XLA Ops:
  0.5 2.0 %split.4 = (bf16[4,128,128]{2,1,0:T(8,128)(2,1)}, bf16[6,128,128]{2,1,0:T(8,128)(2,1)}, bf16[6,128,128]{2,1,0:T(8,128)(2,1)}, bf16[6,128,128]{2,1,0:T(8,128)(2,1)}) custom-call(bf16[12,4,128,128]{3,2,1,0:T(8,128)(2,1)} %refs_0_.7, bf16[128,1024]{1,0:T(8,128)(2,1)} %refs_3_.5), custom_call_target="tpu_custom_call" | custom-call | flops 199999995904 | bytes 268435456 | tf_op jit(solution)/shard_map/split/pallas_call | solution.py:59
  2.5 2.6 %collective-permute-start = (bf16[6,128,128]{2,1,0:T(8,128)(2,1)}, bf16[6,128,128]{2,1,0:T(8,128)(2,1)}, u32[]{:S(2)}, u32[]{:S(2)}) collective-permute-start(bf16[6,128,128]{2,1,0:T(8,128)(2,1)} %get-tuple-element.116), channel_id=1, source_target_pairs={{0,2},{1,3},{2,4},{3,5},{4,6},{5,7},{6,0},{7,1},{8,10},{9,11},{10,... | collective-permute-start | bytes 589832 | tf_op jit(solution)/shard_map/ppermute | solution.py:258
  5.1 2.6 %collective-permute-start.1 = (bf16[6,128,128]{2,1,0:T(8,128)(2,1)}, bf16[6,128,128]{2,1,0:T(8,128)(2,1)}, u32[]{:S(2)}, u32[]{:S(2)}) collective-permute-start(bf16[6,128,128]{2,1,0:T(8,128)(2,1)} %get-tuple-element.117), channel_id=1, source_target_pairs={{0,4},{1,5},{2,6},{3,7},{4,0},{5,1},{6,2},{7,3},{8,12},{9,13},{10,... | collective-permute-start | bytes 589832 | tf_op jit(solution)/shard_map/ppermute | solution.py:258
  9.0 2.7 %split.3 = (bf16[4,128,128]{2,1,0:T(8,128)(2,1)}, bf16[4,128,128]{2,1,0:T(8,128)(2,1)}, bf16[4,128,128]{2,1,0:T(8,128)(2,1)}, bf16[4,128,128]{2,1,0:T(8,128)(2,1)}, bf16[7,4,128,128]{3,2,1,0:T(8,128)(2,1)}) custom-call(bf16[12,4,128,128]{3,2,1,0:T(8,128)(2,1)} %refs_0_.7), custom_call_target="tpu_custom_call" | custom-call | flops 199999995904 | bytes 268435456 | tf_op jit(solution)/shard_map/split/pallas_call | solution.py:59
  13.3 8.2 %collective-permute-done.1.refs_2_.refs_6_ = bf16[6,128,128]{2,1,0:T(8,128)(2,1)} collective-permute-done((bf16[6,128,128]{2,1,0:T(8,128)(2,1)}, bf16[6,128,128]{2,1,0:T(8,128)(2,1)}, u32[]{:S(2)}, u32[]{:S(2)}) %collective-permute-start.1) | collective-permute-done | bytes 196640 | tf_op jit(solution)/shard_map/ppermute | solution.py:258
  21.5 4.7 %collective-permute-start.4 = (bf16[4,128,128]{2,1,0:T(8,128)(2,1)}, bf16[4,128,128]{2,1,0:T(8,128)(2,1)}, u32[]{:S(2)}, u32[]{:S(2)}) collective-permute-start(bf16[4,128,128]{2,1,0:T(8,128)(2,1)} %get-tuple-element.130), channel_id=1, source_target_pairs={{0,2},{1,3},{2,4},{3,5},{4,6},{5,7},{6,0},{7,1},{8,10},{9,11},{10,... | collective-permute-start | bytes 393224 | tf_op jit(solution)/shard_map/ppermute | solution.py:258
  28.6 2.1 %stack.3 = (bf16[4,4,128,128]{3,2,1,0:T(8,128)(2,1)}, bf16[3,2,128,128]{3,2,1,0:T(8,128)(2,1)}) custom-call(bf16[4,128,128]{2,1,0:T(8,128)(2,1)} %get-tuple-element.137.refs_0_.refs_4_, bf16[6,128,128]{2,1,0:T(8,128)(2,1)} %collective-permute-done.refs_1_.refs_5_, bf16[6,128,128]{2,1,0:T(8,128)(2,1)} %collective-permute-done.1.refs_2_.refs_6_, ...), custom_call_target="tpu_custom_call" | custom-call | flops 199999995904 | bytes 268435456 | tf_op jit(solution)/shard_map/stack/pallas_call | solution.py:85
  32.1 2.5 %split.5 = (bf16[4,128,128]{2,1,0:T(8,128)(2,1)}, bf16[4,128,128]{2,1,0:T(8,128)(2,1)}, bf16[4,128,128]{2,1,0:T(8,128)(2,1)}, bf16[4,128,128]{2,1,0:T(8,128)(2,1)}, bf16[5,4,128,128]{3,2,1,0:T(8,128)(2,1)}) custom-call(bf16[12,4,128,128]{3,2,1,0:T(8,128)(2,1)} %refs_0_.7), custom_call_target="tpu_custom_call" | custom-call | flops 199999995904 | bytes 268435456 | tf_op jit(solution)/shard_map/split/pallas_call | solution.py:59
  38.2 1.8 %collective-permute-start.10 = (bf16[4,128,128]{2,1,0:T(8,128)(2,1)}, bf16[4,128,128]{2,1,0:T(8,128)(2,1)}, u32[]{:S(2)}, u32[]{:S(2)}) collective-permute-start(bf16[4,128,128]{2,1,0:T(8,128)(2,1)} %get-tuple-element.146), channel_id=1, source_target_pairs={{0,2},{1,3},{2,4},{3,5},{4,6},{5,7},{6,0},{7,1},{8,10},{9,11},{10,... | collective-permute-start | bytes 393224 | tf_op jit(solution)/shard_map/ppermute | solution.py:258
  39.9 1.7 %collective-permute-start.11 = (bf16[4,128,128]{2,1,0:T(8,128)(2,1)}, bf16[4,128,128]{2,1,0:T(8,128)(2,1)}, u32[]{:S(2)}, u32[]{:S(2)}) collective-permute-start(bf16[4,128,128]{2,1,0:T(8,128)(2,1)} %get-tuple-element.147), channel_id=1, source_target_pairs={{0,4},{1,5},{2,6},{3,7},{4,0},{5,1},{6,2},{7,3},{8,12},{9,13},{10,... | collective-permute-start | bytes 393224 | tf_op jit(solution)/shard_map/ppermute | solution.py:258
  42.1 2.1 %stack.5 = bf16[4,4,128,128]{3,2,1,0:T(8,128)(2,1)} custom-call(bf16[4,128,128]{2,1,0:T(8,128)(2,1)} %get-tuple-element.164.refs_0_.refs_4_, bf16[4,128,128]{2,1,0:T(8,128)(2,1)} %collective-permute-done.4.refs_1_.refs_5_, bf16[4,128,128]{2,1,0:T(8,128)(2,1)} %collective-permute-done.5.refs_2_.refs_6_, ...), custom_call_target="tpu_custom_call" | custom-call | flops 199999995904 | bytes 268435456 | tf_op jit(solution)/shard_map/stack/pallas_call | solution.py:85
  46.5 1.8 %collective-permute-done.13.refs_8_ = bf16[4,4,128,128]{3,2,1,0:T(8,128)(2,1)} collective-permute-done((bf16[4,4,128,128]{3,2,1,0:T(8,128)(2,1)}, bf16[4,4,128,128]{3,2,1,0:T(8,128)(2,1)}, u32[]{:S(2)}, u32[]{:S(2)}) %collective-permute-start.13) | collective-permute-done | bytes 524320 | tf_op jit(solution)/shard_map/ppermute | solution.py:264
  48.6 6.1 %polar.3 = (bf16[4,128,128]{2,1,0:T(8,128)(2,1)S(1)}, bf16[4,128,128]{2,1,0:T(8,128)(2,1)}, bf16[4,128,128]{2,1,0:T(8,128)(2,1)}, bf16[4,128,128]{2,1,0:T(8,128)(2,1)}) custom-call(s32[8,4]{1,0:T(8,128)S(1)} %copy.8.refs_0_, s32[8]{0:T(128)S(1)} %copy-done.4, bf16[1024,1024]{1,0:T(8,128)(2,1)S(1)} %copy-done.1, bf16[128,1024]{1,0:T(8,128)(2,1)S(1)} %copy-done.3, ...), custom_call_target="tpu_custom_call" | custom-call | flops 199999995904 | bytes 268435456 | tf_op jit(solution)/shard_map/polar/pallas_call | solution.py:168
  57.0 1.8 %collective-permute-start.20 = (bf16[4,128,128]{2,1,0:T(8,128)(2,1)}, bf16[4,128,128]{2,1,0:T(8,128)(2,1)}, u32[]{:S(2)}, u32[]{:S(2)}) collective-permute-start(bf16[4,128,128]{2,1,0:T(8,128)(2,1)} %get-tuple-element.179), channel_id=1, source_target_pairs={{0,6},{1,7},{2,0},{3,1},{4,2},{5,3},{6,4},{7,5},{8,14},{9,15},{10,... | collective-permute-start | bytes 393224 | tf_op jit(solution)/shard_map/ppermute | solution.py:258
  58.8 2.0 %stack.4 = bf16[4,4,128,128]{3,2,1,0:T(8,128)(2,1)} custom-call(bf16[4,128,128]{2,1,0:T(8,128)(2,1)} %get-tuple-element.156.refs_0_.refs_4_, bf16[4,128,128]{2,1,0:T(8,128)(2,1)} %collective-permute-done.10.refs_1_.refs_5_, bf16[4,128,128]{2,1,0:T(8,128)(2,1)} %collective-permute-done.11.refs_2_.refs_6_, ...), custom_call_target="tpu_custom_call" | custom-call | bytes 1048576 | tf_op jit(solution)/shard_map/stack/pallas_call | solution.py:85
  60.8 2.3 %collective-permute-done.9 = bf16[5,4,128,128]{3,2,1,0:T(8,128)(2,1)} collective-permute-done((bf16[5,4,128,128]{3,2,1,0:T(8,128)(2,1)}, bf16[5,4,128,128]{3,2,1,0:T(8,128)(2,1)}, u32[]{:S(2)}, u32[]{:S(2)}) %collective-permute-start.9) | collective-permute-done | bytes 655392 | tf_op jit(solution)/shard_map/ppermute | solution.py:267
  64.6 6.0 %polar.4 = (bf16[4,128,128]{2,1,0:T(8,128)(2,1)S(1)}, bf16[4,128,128]{2,1,0:T(8,128)(2,1)}, bf16[4,128,128]{2,1,0:T(8,128)(2,1)}, bf16[4,128,128]{2,1,0:T(8,128)(2,1)}) custom-call(s32[8,4]{1,0:T(8,128)S(1)} %copy.8.refs_0_, s32[8]{0:T(128)S(1)} %copy-done.4, bf16[1024,1024]{1,0:T(8,128)(2,1)S(1)} %copy-done.1, bf16[128,1024]{1,0:T(8,128)(2,1)S(1)} %copy-done.3, ...), custom_call_target="tpu_custom_call" | custom-call | flops 199999995904 | bytes 268435456 | tf_op jit(solution)/shard_map/polar/pallas_call | solution.py:168
  70.9 2.0 %collective-permute-start.22 = (bf16[4,128,128]{2,1,0:T(8,128)(2,1)}, bf16[4,128,128]{2,1,0:T(8,128)(2,1)}, u32[]{:S(2)}, u32[]{:S(2)}) collective-permute-start(bf16[4,128,128]{2,1,0:T(8,128)(2,1)} %get-tuple-element.194), channel_id=1, source_target_pairs={{0,4},{1,5},{2,6},{3,7},{4,0},{5,1},{6,2},{7,3},{8,12},{9,13},{10,... | collective-permute-start | bytes 393224 | tf_op jit(solution)/shard_map/ppermute | solution.py:258
  74.5 6.2 %polar.5 = (bf16[4,128,128]{2,1,0:T(8,128)(2,1)S(1)}, bf16[4,128,128]{2,1,0:T(8,128)(2,1)}, bf16[4,128,128]{2,1,0:T(8,128)(2,1)}, bf16[4,128,128]{2,1,0:T(8,128)(2,1)}) custom-call(s32[8,4]{1,0:T(8,128)S(1)} %copy.8.refs_0_, s32[8]{0:T(128)S(1)} %copy-done.4, bf16[1024,1024]{1,0:T(8,128)(2,1)S(1)} %copy-done.1, bf16[128,1024]{1,0:T(8,128)(2,1)S(1)} %copy-done.3, ...), custom_call_target="tpu_custom_call" | custom-call | flops 199999995904 | bytes 268435456 | tf_op jit(solution)/shard_map/polar/pallas_call | solution.py:168
  81.8 2.4 %collective-permute-start.26 = (bf16[4,128,128]{2,1,0:T(8,128)(2,1)}, bf16[4,128,128]{2,1,0:T(8,128)(2,1)}, u32[]{:S(2)}, u32[]{:S(2)}) collective-permute-start(bf16[4,128,128]{2,1,0:T(8,128)(2,1)} %get-tuple-element.207), channel_id=1, source_target_pairs={{0,2},{1,3},{2,4},{3,5},{4,6},{5,7},{6,0},{7,1},{8,10},{9,11},{10,... | collective-permute-start | bytes 393224 | tf_op jit(solution)/shard_map/ppermute | solution.py:258
  86.7 4.4 %chi.2.refs_10_ = f32[8,6,12]{2,1,0:T(8,128)S(1)} custom-call(bf16[12,512,128]{2,1,0:T(8,128)(2,1)S(1)} %bitcast.19, bf16[7,512,128]{2,1,0:T(8,128)(2,1)} %bitcast.2.refs_1_, bf16[12,512,128]{2,1,0:T(8,128)(2,1)} %bitcast.3.refs_2_, bf16[5,512,128]{2,1,0:T(8,128)(2,1)} %bitcast.4.refs_3_, bf16[7,512,128]{2,1,0:T(8,128)(2,1)S(1)} %bitcast.21, ...), custom_call_target="tpu_custom_call" | custom-call | flops 199999995904 | bytes 268435456 | tf_op jit(solution)/shard_map/chi/pallas_call | solution.py:235
  91.1 4.0 %collective-permute-done.27 = bf16[4,128,128]{2,1,0:T(8,128)(2,1)} collective-permute-done((bf16[4,128,128]{2,1,0:T(8,128)(2,1)}, bf16[4,128,128]{2,1,0:T(8,128)(2,1)}, u32[]{:S(2)}, u32[]{:S(2)}) %collective-permute-start.27) | collective-permute-done | bytes 131104 | tf_op jit(solution)/shard_map/ppermute | solution.py:258
  95.1 3.8 %chi.3 = f32[8,6,12]{2,1,0:T(8,128)S(1)} custom-call(bf16[12,512,128]{2,1,0:T(8,128)(2,1)S(1)} %bitcast.20, bf16[7,512,128]{2,1,0:T(8,128)(2,1)} %bitcast.2.refs_1_, bf16[12,512,128]{2,1,0:T(8,128)(2,1)} %bitcast.3.refs_2_, bf16[5,512,128]{2,1,0:T(8,128)(2,1)} %bitcast.4.refs_3_, bf16[7,512,128]{2,1,0:T(8,128)(2,1)S(1)} %bitcast.22, ...), custom_call_target="tpu_custom_call" | custom-call | flops 199999995904 | bytes 268435456 | tf_op jit(solution)/shard_map/chi/pallas_call | solution.py:235
  98.9 11.7 %all_to_all.5 = f32[8,6,12]{2,1,0:T(8,128)S(1)} all-to-all(f32[8,6,12]{2,1,0:T(8,128)S(1)} %chi.3), channel_id=1, replica_groups=mesh['aux'=4,'pair'=8] {'pair'}, dimensions={0} | all-to-all | bytes 4608 | tf_op jit(solution)/shard_map/all_to_all | solution.py:351
  (64 shorter events, 23.7 us)
Async XLA Ops:
  0.0 21.5 %collective-permute-start.3 = (bf16[12,4,128,128]{3,2,1,0:T(8,128)(2,1)}, bf16[12,4,128,128]{3,2,1,0:T(8,128)(2,1)}, u32[]{:S(2)}, u32[]{:S(2)}) collective-permute-start(bf16[12,4,128,128]{3,2,1,0:T(8,128)(2,1)} %refs_0_.7), channel_id=1, source_target_pairs={{0,8},{8,0},{16,24},{24,16},{1,9},{9,1},{17,25},{25,17},{2,10},{10... | collective-permute-start | bytes 4718600 | tf_op jit(solution)/shard_map/ppermute | solution.py:267
  2.5 10.8 %collective-permute-start = (bf16[6,128,128]{2,1,0:T(8,128)(2,1)}, bf16[6,128,128]{2,1,0:T(8,128)(2,1)}, u32[]{:S(2)}, u32[]{:S(2)}) collective-permute-start(bf16[6,128,128]{2,1,0:T(8,128)(2,1)} %get-tuple-element.116), channel_id=1, source_target_pairs={{0,2},{1,3},{2,4},{3,5},{4,6},{5,7},{6,0},{7,1},{8,10},{9,11},{10,... | collective-permute-start | bytes 589832 | tf_op jit(solution)/shard_map/ppermute | solution.py:258
  5.1 16.4 %collective-permute-start.1 = (bf16[6,128,128]{2,1,0:T(8,128)(2,1)}, bf16[6,128,128]{2,1,0:T(8,128)(2,1)}, u32[]{:S(2)}, u32[]{:S(2)}) collective-permute-start(bf16[6,128,128]{2,1,0:T(8,128)(2,1)} %get-tuple-element.117), channel_id=1, source_target_pairs={{0,4},{1,5},{2,6},{3,7},{4,0},{5,1},{6,2},{7,3},{8,12},{9,13},{10,... | collective-permute-start | bytes 589832 | tf_op jit(solution)/shard_map/ppermute | solution.py:258
  7.6 13.9 %collective-permute-start.2 = (bf16[6,128,128]{2,1,0:T(8,128)(2,1)}, bf16[6,128,128]{2,1,0:T(8,128)(2,1)}, u32[]{:S(2)}, u32[]{:S(2)}) collective-permute-start(bf16[6,128,128]{2,1,0:T(8,128)(2,1)} %get-tuple-element.118), channel_id=1, source_target_pairs={{0,6},{1,7},{2,0},{3,1},{4,2},{5,3},{6,4},{7,5},{8,14},{9,15},{10,... | collective-permute-start | bytes 589832 | tf_op jit(solution)/shard_map/ppermute | solution.py:258
  11.7 23.1 %collective-permute-start.8 = (bf16[7,4,128,128]{3,2,1,0:T(8,128)(2,1)}, bf16[7,4,128,128]{3,2,1,0:T(8,128)(2,1)}, u32[]{:S(2)}, u32[]{:S(2)}) collective-permute-start(bf16[7,4,128,128]{3,2,1,0:T(8,128)(2,1)} %get-tuple-element.114), channel_id=1, source_target_pairs={{0,16},{8,24},{16,0},{24,8},{1,17},{9,25},{17,1},{25,9},{2,18},{10... | collective-permute-start | bytes 2752520 | tf_op jit(solution)/shard_map/ppermute | solution.py:267
  21.5 14.8 %collective-permute-start.4 = (bf16[4,128,128]{2,1,0:T(8,128)(2,1)}, bf16[4,128,128]{2,1,0:T(8,128)(2,1)}, u32[]{:S(2)}, u32[]{:S(2)}) collective-permute-start(bf16[4,128,128]{2,1,0:T(8,128)(2,1)} %get-tuple-element.130), channel_id=1, source_target_pairs={{0,2},{1,3},{2,4},{3,5},{4,6},{5,7},{6,0},{7,1},{8,10},{9,11},{10,... | collective-permute-start | bytes 393224 | tf_op jit(solution)/shard_map/ppermute | solution.py:258
  26.2 10.4 %collective-permute-start.5 = (bf16[4,128,128]{2,1,0:T(8,128)(2,1)}, bf16[4,128,128]{2,1,0:T(8,128)(2,1)}, u32[]{:S(2)}, u32[]{:S(2)}) collective-permute-start(bf16[4,128,128]{2,1,0:T(8,128)(2,1)} %get-tuple-element.131), channel_id=1, source_target_pairs={{0,4},{1,5},{2,6},{3,7},{4,0},{5,1},{6,2},{7,3},{8,12},{9,13},{10,... | collective-permute-start | bytes 393224 | tf_op jit(solution)/shard_map/ppermute | solution.py:258
  27.8 8.9 %collective-permute-start.6 = (bf16[4,128,128]{2,1,0:T(8,128)(2,1)}, bf16[4,128,128]{2,1,0:T(8,128)(2,1)}, u32[]{:S(2)}, u32[]{:S(2)}) collective-permute-start(bf16[4,128,128]{2,1,0:T(8,128)(2,1)} %get-tuple-element.132), channel_id=1, source_target_pairs={{0,6},{1,7},{2,0},{3,1},{4,2},{5,3},{6,4},{7,5},{8,14},{9,15},{10,... | collective-permute-start | bytes 393224 | tf_op jit(solution)/shard_map/ppermute | solution.py:258
  34.8 13.5 %collective-permute-start.13 = (bf16[4,4,128,128]{3,2,1,0:T(8,128)(2,1)}, bf16[4,4,128,128]{3,2,1,0:T(8,128)(2,1)}, u32[]{:S(2)}, u32[]{:S(2)}) collective-permute-start(bf16[4,4,128,128]{3,2,1,0:T(8,128)(2,1)} %get-tuple-element.149), channel_id=1, source_target_pairs={{0,1},{1,0},{2,3},{3,2},{4,5},{5,4},{6,7},{7,6},{8,9},{9,8},{10,11... | collective-permute-start | bytes 1572872 | tf_op jit(solution)/shard_map/ppermute | solution.py:264
  38.2 16.4 %collective-permute-start.10 = (bf16[4,128,128]{2,1,0:T(8,128)(2,1)}, bf16[4,128,128]{2,1,0:T(8,128)(2,1)}, u32[]{:S(2)}, u32[]{:S(2)}) collective-permute-start(bf16[4,128,128]{2,1,0:T(8,128)(2,1)} %get-tuple-element.146), channel_id=1, source_target_pairs={{0,2},{1,3},{2,4},{3,5},{4,6},{5,7},{6,0},{7,1},{8,10},{9,11},{10,... | collective-permute-start | bytes 393224 | tf_op jit(solution)/shard_map/ppermute | solution.py:258
  39.9 14.7 %collective-permute-start.11 = (bf16[4,128,128]{2,1,0:T(8,128)(2,1)}, bf16[4,128,128]{2,1,0:T(8,128)(2,1)}, u32[]{:S(2)}, u32[]{:S(2)}) collective-permute-start(bf16[4,128,128]{2,1,0:T(8,128)(2,1)} %get-tuple-element.147), channel_id=1, source_target_pairs={{0,4},{1,5},{2,6},{3,7},{4,0},{5,1},{6,2},{7,3},{8,12},{9,13},{10,... | collective-permute-start | bytes 393224 | tf_op jit(solution)/shard_map/ppermute | solution.py:258
  44.3 10.4 %collective-permute-start.12 = (bf16[4,128,128]{2,1,0:T(8,128)(2,1)}, bf16[4,128,128]{2,1,0:T(8,128)(2,1)}, u32[]{:S(2)}, u32[]{:S(2)}) collective-permute-start(bf16[4,128,128]{2,1,0:T(8,128)(2,1)} %get-tuple-element.148), channel_id=1, source_target_pairs={{0,6},{1,7},{2,0},{3,1},{4,2},{5,3},{6,4},{7,5},{8,14},{9,15},{10,... | collective-permute-start | bytes 393224 | tf_op jit(solution)/shard_map/ppermute | solution.py:258
  45.0 19.6 %collective-permute-start.17 = (bf16[4,4,128,128]{3,2,1,0:T(8,128)(2,1)}, bf16[4,4,128,128]{3,2,1,0:T(8,128)(2,1)}, u32[]{:S(2)}, u32[]{:S(2)}) collective-permute-start(bf16[4,4,128,128]{3,2,1,0:T(8,128)(2,1)} %stack.5), channel_id=1, source_target_pairs={{0,1},{1,0},{2,3},{3,2},{4,5},{5,4},{6,7},{7,6},{8,9},{9,8},{10,11... | collective-permute-start | bytes 1572872 | tf_op jit(solution)/shard_map/ppermute | solution.py:264
  48.3 14.8 %collective-permute-start.9 = (bf16[5,4,128,128]{3,2,1,0:T(8,128)(2,1)}, bf16[5,4,128,128]{3,2,1,0:T(8,128)(2,1)}, u32[]{:S(2)}, u32[]{:S(2)}) collective-permute-start(bf16[5,4,128,128]{3,2,1,0:T(8,128)(2,1)} %get-tuple-element.136), channel_id=1, source_target_pairs={{0,16},{8,24},{16,0},{24,8},{1,17},{9,25},{17,1},{25,9},{2,18},{10... | collective-permute-start | bytes 1966088 | tf_op jit(solution)/shard_map/ppermute | solution.py:267
  54.6 15.9 %collective-permute-start.18 = (bf16[4,128,128]{2,1,0:T(8,128)(2,1)}, bf16[4,128,128]{2,1,0:T(8,128)(2,1)}, u32[]{:S(2)}, u32[]{:S(2)}) collective-permute-start(bf16[4,128,128]{2,1,0:T(8,128)(2,1)} %get-tuple-element.177), channel_id=1, source_target_pairs={{0,2},{1,3},{2,4},{3,5},{4,6},{5,7},{6,0},{7,1},{8,10},{9,11},{10,... | collective-permute-start | bytes 393224 | tf_op jit(solution)/shard_map/ppermute | solution.py:258
  55.5 15.1 %collective-permute-start.19 = (bf16[4,128,128]{2,1,0:T(8,128)(2,1)}, bf16[4,128,128]{2,1,0:T(8,128)(2,1)}, u32[]{:S(2)}, u32[]{:S(2)}) collective-permute-start(bf16[4,128,128]{2,1,0:T(8,128)(2,1)} %get-tuple-element.178), channel_id=1, source_target_pairs={{0,4},{1,5},{2,6},{3,7},{4,0},{5,1},{6,2},{7,3},{8,12},{9,13},{10,... | collective-permute-start | bytes 393224 | tf_op jit(solution)/shard_map/ppermute | solution.py:258
  57.0 13.6 %collective-permute-start.20 = (bf16[4,128,128]{2,1,0:T(8,128)(2,1)}, bf16[4,128,128]{2,1,0:T(8,128)(2,1)}, u32[]{:S(2)}, u32[]{:S(2)}) collective-permute-start(bf16[4,128,128]{2,1,0:T(8,128)(2,1)} %get-tuple-element.179), channel_id=1, source_target_pairs={{0,6},{1,7},{2,0},{3,1},{4,2},{5,3},{6,4},{7,5},{8,14},{9,15},{10,... | collective-permute-start | bytes 393224 | tf_op jit(solution)/shard_map/ppermute | solution.py:258
  63.1 11.4 %collective-permute-start.16 = (bf16[4,4,128,128]{3,2,1,0:T(8,128)(2,1)}, bf16[4,4,128,128]{3,2,1,0:T(8,128)(2,1)}, u32[]{:S(2)}, u32[]{:S(2)}) collective-permute-start(bf16[4,4,128,128]{3,2,1,0:T(8,128)(2,1)} %stack.4), channel_id=1, source_target_pairs={{0,1},{1,0},{2,3},{3,2},{4,5},{5,4},{6,7},{7,6},{8,9},{9,8},{10,11... | collective-permute-start | bytes 1572872 | tf_op jit(solution)/shard_map/ppermute | solution.py:264
  70.6 10.1 %collective-permute-start.21 = (bf16[4,128,128]{2,1,0:T(8,128)(2,1)}, bf16[4,128,128]{2,1,0:T(8,128)(2,1)}, u32[]{:S(2)}, u32[]{:S(2)}) collective-permute-start(bf16[4,128,128]{2,1,0:T(8,128)(2,1)} %get-tuple-element.193), channel_id=1, source_target_pairs={{0,2},{1,3},{2,4},{3,5},{4,6},{5,7},{6,0},{7,1},{8,10},{9,11},{10,... | collective-permute-start | bytes 393224 | tf_op jit(solution)/shard_map/ppermute | solution.py:258
  70.9 10.5 %collective-permute-start.22 = (bf16[4,128,128]{2,1,0:T(8,128)(2,1)}, bf16[4,128,128]{2,1,0:T(8,128)(2,1)}, u32[]{:S(2)}, u32[]{:S(2)}) collective-permute-start(bf16[4,128,128]{2,1,0:T(8,128)(2,1)} %get-tuple-element.194), channel_id=1, source_target_pairs={{0,4},{1,5},{2,6},{3,7},{4,0},{5,1},{6,2},{7,3},{8,12},{9,13},{10,... | collective-permute-start | bytes 393224 | tf_op jit(solution)/shard_map/ppermute | solution.py:258
  72.8 8.5 %collective-permute-start.23 = (bf16[4,128,128]{2,1,0:T(8,128)(2,1)}, bf16[4,128,128]{2,1,0:T(8,128)(2,1)}, u32[]{:S(2)}, u32[]{:S(2)}) collective-permute-start(bf16[4,128,128]{2,1,0:T(8,128)(2,1)} %get-tuple-element.195), channel_id=1, source_target_pairs={{0,6},{1,7},{2,0},{3,1},{4,2},{5,3},{6,4},{7,5},{8,14},{9,15},{10,... | collective-permute-start | bytes 393224 | tf_op jit(solution)/shard_map/ppermute | solution.py:258
  81.8 9.3 %collective-permute-start.26 = (bf16[4,128,128]{2,1,0:T(8,128)(2,1)}, bf16[4,128,128]{2,1,0:T(8,128)(2,1)}, u32[]{:S(2)}, u32[]{:S(2)}) collective-permute-start(bf16[4,128,128]{2,1,0:T(8,128)(2,1)} %get-tuple-element.207), channel_id=1, source_target_pairs={{0,2},{1,3},{2,4},{3,5},{4,6},{5,7},{6,0},{7,1},{8,10},{9,11},{10,... | collective-permute-start | bytes 393224 | tf_op jit(solution)/shard_map/ppermute | solution.py:258
  84.3 10.8 %collective-permute-start.27 = (bf16[4,128,128]{2,1,0:T(8,128)(2,1)}, bf16[4,128,128]{2,1,0:T(8,128)(2,1)}, u32[]{:S(2)}, u32[]{:S(2)}) collective-permute-start(bf16[4,128,128]{2,1,0:T(8,128)(2,1)} %get-tuple-element.208), channel_id=1, source_target_pairs={{0,4},{1,5},{2,6},{3,7},{4,0},{5,1},{6,2},{7,3},{8,12},{9,13},{10,... | collective-permute-start | bytes 393224 | tf_op jit(solution)/shard_map/ppermute | solution.py:258
  85.7 9.3 %collective-permute-start.28 = (bf16[4,128,128]{2,1,0:T(8,128)(2,1)}, bf16[4,128,128]{2,1,0:T(8,128)(2,1)}, u32[]{:S(2)}, u32[]{:S(2)}) collective-permute-start(bf16[4,128,128]{2,1,0:T(8,128)(2,1)} %get-tuple-element.209), channel_id=1, source_target_pairs={{0,6},{1,7},{2,0},{3,1},{4,2},{5,3},{6,4},{7,5},{8,14},{9,15},{10,... | collective-permute-start | bytes 393224 | tf_op jit(solution)/shard_map/ppermute | solution.py:258
  (13 other events, 92.4 us)

commit v3 on v2

--- a/solution.py
+++ b/solution.py
@@ -12,8 +12,8 @@
 VMEM = pl.BlockSpec(memory_space=pltpu.VMEM)
 SMEM = pl.BlockSpec(memory_space=pltpu.SMEM)
 MIB = 2**20
-QUICK = pl.CostEstimate(flops=0, bytes_accessed=2**20, transcendentals=0)
-LONG = pl.CostEstimate(flops=2 * 10**11, bytes_accessed=2**28, transcendentals=0)
+LONG = pl.CostEstimate(flops=2 * 10**11, bytes_accessed=2**20, transcendentals=0)
+QUICK = pl.CostEstimate(flops=1, bytes_accessed=2**20, transcendentals=0)
 
 
 def size_of(shapes):
@@ -96,40 +96,22 @@
     rest = list(rest)
     take = lambda n: [rest.pop(0) for _ in range(n)]
     own, others, shares, outs = take(groups), take(lows - 1), take(len(masks)), take(groups)
-    half, lhs, full = rest
+    dense, lhs, half, full = rest
     slots, width = outs[0].shape[0], outs[0].shape[1]
     basis = virt_ref.shape[0]
     me = lax.axis_index("pair")
     high, low = me // lows, lax.rem(me, lows)
 
+    dense[...] = jnp.zeros_like(dense)
     for e in range(lows):
         for d in range(groups):
             tiles = own[d] if e == 0 else others[e - 1].at[d]
             row = lax.rem(high + groups - d, groups) * lows + lax.rem(low + lows - e, lows)
-            alive = live_ref[row]
-
-            def term(s):
-                left = tiles[s]
-                right = virt_ref[rows_at(cols_ref[row, s], width), :]
-                if s + 1 < slots:
-                    second = jnp.where(s + 1 < alive, tiles[s + 1], jnp.zeros_like(left))
-                    left = jnp.concatenate([left, second], axis=1)
-                    below = virt_ref[rows_at(cols_ref[row, s + 1], width), :]
-                    right = jnp.concatenate([right, below], axis=0)
-                return jnp.dot(left, right, preferred_element_type=F32)
-
-            steps = list(range(0, slots, 2))
-            for n in range(len(steps)):
-                here = alive > steps[n]
-                if n + 1 < len(steps):
-                    here = jnp.logical_and(here, alive <= steps[n + 1])
-
-                @pl.when(here)
+            for s in range(slots):
+
+                @pl.when(s < live_ref[row])
                 def _():
-                    total = term(steps[0])
-                    for s in steps[1 : n + 1]:
-                        total += term(s)
-                    half[rows_at(row, width), :] = total.astype(BF16)
+                    dense[rows_at(row, width), rows_at(cols_ref[row, s], width)] = tiles[s]
 
     lhs[0:width, :] = occ_ref[...]
     for mask_list, share in zip(masks, shares):
@@ -145,10 +127,11 @@
                         j * width : (j + 1) * width,
                     ] = share[k, d - 1, at // width, at % width : at % width + part, :]
     wide = 2 * width
-    for j in range(0, basis, wide):
-        full[:, j : j + wide] = jnp.dot(
-            lhs[...], half[:, j : j + wide], preferred_element_type=F32
-        ).astype(BF16)
+    for source, by, into in ((lhs, dense, half), (half, virt_ref, full)):
+        for j in range(0, basis, wide):
+            into[:, j : j + wide] = jnp.dot(
+                source[...], by[:, j : j + wide], preferred_element_type=F32
+            ).astype(BF16)
     for d in range(groups):
         row = lax.rem(high + d, groups) * lows + low
         alive = live_ref[row]
@@ -162,7 +145,7 @@
     slots, width = own[0].shape[0], own[0].shape[1]
     basis = virt.shape[0]
     shapes = [jax.ShapeDtypeStruct((slots, width, width), BF16)] * groups
-    scratch = [(basis, basis), (groups * width, basis), (groups * width, basis)]
+    scratch = [(basis, basis)] + [(groups * width, basis)] * 3
     arrays = [virt, occ, *own, *others, *shares]
     held = size_of(arrays) + size_of(shapes) + sum(2 * a * b for a, b in scratch)
     return pl.pallas_call(
@@ -177,10 +160,13 @@
     )(cols, live, *arrays)
 
 
-def chi_kernel(groups, lows, chunks, factor, places, *rest):
+def chi_kernel(groups, lows, chunks, factor, places, keep, *rest):
     count = groups * len(chunks)
     everyone, pieces = rest[: len(places)], rest[len(places) : len(places) + count]
-    prior, out = rest[len(places) + count : -1], rest[-1]
+    kept = rest[len(rest) - len(places) :] if keep else ()
+    prior, out = rest[len(places) + count : -1 - len(kept)], rest[-1 - len(kept)]
+    for ref, copy in zip(everyone, kept):
+        copy[...] = ref[...]
     _, rows, width = everyone[0].shape
     unit, local = out.shape[1], out.shape[2]
     high, aux = lax.axis_index("pair") // lows, lax.axis_index("aux")
@@ -223,7 +209,7 @@
             out[at] = piece + prior[0][at] if prior else piece
 
 
-def chi(everyone, back, chunks, prior, groups, lows, local, unit, factor):
+def chi(everyone, back, chunks, prior, groups, lows, local, unit, factor, keep=False):
     pieces = [p for c in chunks for p in back[c]]
     slots, width = pieces[0].shape[0], pieces[0].shape[1]
     places = [place for place, _ in everyone]
@@ -232,15 +218,17 @@
     if prior is not None:
         arrays.append(prior)
     count = sum(e.shape[0] for _, e in everyone)
-    return pl.pallas_call(
-        lambda *refs: chi_kernel(groups, lows, chunks, factor, places, *refs),
-        out_shape=jax.ShapeDtypeStruct((count // unit, unit, local), F32),
+    part, *kept = pl.pallas_call(
+        lambda *refs: chi_kernel(groups, lows, chunks, factor, places, keep, *refs),
+        out_shape=[jax.ShapeDtypeStruct((count // unit, unit, local), F32)]
+        + [pltpu.VMEM(a.shape, a.dtype) for a in arrays[: len(places)] if keep],
         in_specs=[VMEM] * len(arrays),
-        out_specs=VMEM,
+        out_specs=[VMEM] * (1 + len(places) * keep),
         compiler_params=pltpu.CompilerParams(vmem_limit_bytes=size_of(arrays) + 12 * MIB),
         cost_estimate=LONG,
         name="chi",
     )(*arrays)
+    return part, [(place, e) for place, e in zip(places, kept)] if keep else everyone
 
 
 def per_device(three_centre, occ_green, virt_green, tile_cols, tile_live):
@@ -306,12 +294,11 @@
         if phase in (1, 2):
             for bit in bits[: len(bits) - 1] if phase == 1 else bits[len(bits) - 1 :]:
                 parts, masks = parts + [swap(x, bit) for x in parts], masks + [[m[0] | bit] for m in masks]
-        if phase + 1 < chunks:
-            sending[phase + 1], more = split(
-                three_centre, occ_green, groups, lows, phase + 1, shares,
-                [(0, cut)] * (phase == 0) + [(cut, local)] * (phase + 2 == chunks),
-            )
-            copies = copies + more
+        for c in range(1, chunks):
+            if phase == c - 1:
+                runs = ([(0, cut)] * (c == 1) + [(cut, local)] * (c == chunks - 1)) * (cut < local)
+                sending[c], more = split(three_centre, occ_green, groups, lows, c, shares, runs)
+                copies = copies + more
         if phase == 0 and bits:
             first_part = swap(copies[0] if copies else three_centre, bits[0])
             everyone.append(((bits[0], 0), first_part))
@@ -333,8 +320,8 @@
                         array = together((array, back[chunks - 2]))[0]
                         everyone.append(((mask ^ bit, start), swap(array, bit)))
             if chunks > 1:
-                part = chi(
-                    everyone, back, list(range(chunks - 1)), None, groups, lows, local, unit, factor
+                part, everyone = chi(
+                    everyone, back, list(range(chunks - 1)), None, groups, lows, local, unit, factor, True
                 )
         done = {}
         if phase == 0 and len(bits) > 1:
@@ -346,7 +333,7 @@
         own = kept or own
         for n, array in done.items():
             everyone[n] = (everyone[n][0], array)
-    part = chi(everyone, back, [chunks - 1], part, groups, lows, local, unit, factor)
+    part, _ = chi(everyone, back, [chunks - 1], part, groups, lows, local, unit, factor)
     part = part.reshape(blocks, per, local)
     return jnp.sum(lax.all_to_all(part, "pair", 0, 0, tiled=True), axis=0)
 

time: 112 us -> 110 us (0.982)
  Pallas kernels: 39.9 us -> 37.3 us
  waiting for transfers between devices: 18.9 us -> 20.1 us
    pallas_call x3, Pallas kernels: 18.3 us -> 16.1 us  [polar(): pl.pallas_call(lambda *refs: polar_kernel(groups, lows, masks, *refs), ou...]
  transfers between devices with their start and end apart: 29 -> 29, of which waited for: 8 -> 9; matrix products, arithmetic and copies ran while one was open for 0% -> 0% of each run, Pallas kernels for 32% -> 31%
where the time goes in v3:
time: 110 us
  starting transfers between devices  39.8 us (36%)
  Pallas kernels  37.3 us (34%)
  waiting for transfers between devices  20.1 us (18%)
  blocking collectives  11.9 us (11%)
    ppermute x18, starting transfers between devices, along_high(): return lax.ppermute(array, 'pair', moves)  30.7 us
    pallas_call x3, Pallas kernels, polar(): pl.pallas_call(lambda *refs: polar_kernel(groups, lows, masks, *refs), ou...  16.1 us
    ppermute x18, waiting for transfers between devices, along_high(): return lax.ppermute(array, 'pair', moves)  13 us
    all_to_all x1, blocking collectives, per_device(): return jnp.sum(lax.all_to_all(part, 'pair', 0, 0, tiled=True), axis=0)  11.9 us
    pallas_call x2, Pallas kernels, chi(): pl.pallas_call(lambda *refs: chi_kernel(groups, lows, chunks, factor, pla...  7.74 us
    pallas_call x3, Pallas kernels, split(): pl.pallas_call(lambda *refs: split_kernel(groups, lows, chunk, shares, co...  7.18 us
    pallas_call x3, Pallas kernels, stack(): pl.pallas_call(lambda *refs: stack_kernel(groups, slots, *refs), out_shap...  6.3 us
    ppermute x8, waiting for transfers between devices, swap(): return lax.ppermute(array, 'aux', [(a, a ^ bit) for a in range(peers)])  4.71 us
  transfers between devices with their start and end apart: 29, of which 9 were waited for; matrix products, arithmetic and copies ran while one was open for 0% of the time, Pallas kernels for 31%

profile of v3, /device:TPU:0, one launch (start us, length us, event | category | flops | bytes accessed | tf_op | source)
XLA Modules:
  0.0 109.9 jit_solution(16819632752799038605)
XLA Ops:
  0.5 2.0 %split.4 = (bf16[4,128,128]{2,1,0:T(8,128)(2,1)}, bf16[6,128,128]{2,1,0:T(8,128)(2,1)}, bf16[6,128,128]{2,1,0:T(8,128)(2,1)}, bf16[6,128,128]{2,1,0:T(8,128)(2,1)}) custom-call(bf16[12,4,128,128]{3,2,1,0:T(8,128)(2,1)} %refs_0_.7, bf16[128,1024]{1,0:T(8,128)(2,1)} %refs_3_.5), custom_call_target="tpu_custom_call" | custom-call | flops 199999995904 | bytes 1048576 | tf_op jit(solution)/shard_map/split/pallas_call | solution.py:59
  2.5 2.6 %collective-permute-start = (bf16[6,128,128]{2,1,0:T(8,128)(2,1)}, bf16[6,128,128]{2,1,0:T(8,128)(2,1)}, u32[]{:S(2)}, u32[]{:S(2)}) collective-permute-start(bf16[6,128,128]{2,1,0:T(8,128)(2,1)} %get-tuple-element.123), channel_id=1, source_target_pairs={{0,2},{1,3},{2,4},{3,5},{4,6},{5,7},{6,0},{7,1},{8,10},{9,11},{10,... | collective-permute-start | bytes 589832 | tf_op jit(solution)/shard_map/ppermute | solution.py:246
  5.1 2.6 %collective-permute-start.1 = (bf16[6,128,128]{2,1,0:T(8,128)(2,1)}, bf16[6,128,128]{2,1,0:T(8,128)(2,1)}, u32[]{:S(2)}, u32[]{:S(2)}) collective-permute-start(bf16[6,128,128]{2,1,0:T(8,128)(2,1)} %get-tuple-element.124), channel_id=1, source_target_pairs={{0,4},{1,5},{2,6},{3,7},{4,0},{5,1},{6,2},{7,3},{8,12},{9,13},{10,... | collective-permute-start | bytes 589832 | tf_op jit(solution)/shard_map/ppermute | solution.py:246
  9.0 2.7 %split.3 = (bf16[4,128,128]{2,1,0:T(8,128)(2,1)}, bf16[4,128,128]{2,1,0:T(8,128)(2,1)}, bf16[4,128,128]{2,1,0:T(8,128)(2,1)}, bf16[4,128,128]{2,1,0:T(8,128)(2,1)}, bf16[7,4,128,128]{3,2,1,0:T(8,128)(2,1)}) custom-call(bf16[12,4,128,128]{3,2,1,0:T(8,128)(2,1)} %refs_0_.7), custom_call_target="tpu_custom_call" | custom-call | flops 199999995904 | bytes 1048576 | tf_op jit(solution)/shard_map/split/pallas_call | solution.py:59
  13.3 8.2 %collective-permute-done.1.refs_2_.refs_6_ = bf16[6,128,128]{2,1,0:T(8,128)(2,1)} collective-permute-done((bf16[6,128,128]{2,1,0:T(8,128)(2,1)}, bf16[6,128,128]{2,1,0:T(8,128)(2,1)}, u32[]{:S(2)}, u32[]{:S(2)}) %collective-permute-start.1) | collective-permute-done | bytes 196640 | tf_op jit(solution)/shard_map/ppermute | solution.py:246
  21.5 4.7 %collective-permute-start.4 = (bf16[4,128,128]{2,1,0:T(8,128)(2,1)}, bf16[4,128,128]{2,1,0:T(8,128)(2,1)}, u32[]{:S(2)}, u32[]{:S(2)}) collective-permute-start(bf16[4,128,128]{2,1,0:T(8,128)(2,1)} %get-tuple-element.137), channel_id=1, source_target_pairs={{0,2},{1,3},{2,4},{3,5},{4,6},{5,7},{6,0},{7,1},{8,10},{9,11},{10,... | collective-permute-start | bytes 393224 | tf_op jit(solution)/shard_map/ppermute | solution.py:246
  28.6 2.2 %stack.3 = (bf16[4,4,128,128]{3,2,1,0:T(8,128)(2,1)}, bf16[3,2,128,128]{3,2,1,0:T(8,128)(2,1)}) custom-call(bf16[4,128,128]{2,1,0:T(8,128)(2,1)} %get-tuple-element.144.refs_0_.refs_4_, bf16[6,128,128]{2,1,0:T(8,128)(2,1)} %collective-permute-done.refs_1_.refs_5_, bf16[6,128,128]{2,1,0:T(8,128)(2,1)} %collective-permute-done.1.refs_2_.refs_6_, ...), custom_call_target="tpu_custom_call" | custom-call | flops 199999995904 | bytes 1048576 | tf_op jit(solution)/shard_map/stack/pallas_call | solution.py:85
  32.2 2.5 %split.5 = (bf16[4,128,128]{2,1,0:T(8,128)(2,1)}, bf16[4,128,128]{2,1,0:T(8,128)(2,1)}, bf16[4,128,128]{2,1,0:T(8,128)(2,1)}, bf16[4,128,128]{2,1,0:T(8,128)(2,1)}, bf16[5,4,128,128]{3,2,1,0:T(8,128)(2,1)}) custom-call(bf16[12,4,128,128]{3,2,1,0:T(8,128)(2,1)} %refs_0_.7), custom_call_target="tpu_custom_call" | custom-call | flops 199999995904 | bytes 1048576 | tf_op jit(solution)/shard_map/split/pallas_call | solution.py:59
  38.1 1.8 %collective-permute-start.10 = (bf16[4,128,128]{2,1,0:T(8,128)(2,1)}, bf16[4,128,128]{2,1,0:T(8,128)(2,1)}, u32[]{:S(2)}, u32[]{:S(2)}) collective-permute-start(bf16[4,128,128]{2,1,0:T(8,128)(2,1)} %get-tuple-element.153), channel_id=1, source_target_pairs={{0,2},{1,3},{2,4},{3,5},{4,6},{5,7},{6,0},{7,1},{8,10},{9,11},{10,... | collective-permute-start | bytes 393224 | tf_op jit(solution)/shard_map/ppermute | solution.py:246
  39.9 1.7 %collective-permute-start.11 = (bf16[4,128,128]{2,1,0:T(8,128)(2,1)}, bf16[4,128,128]{2,1,0:T(8,128)(2,1)}, u32[]{:S(2)}, u32[]{:S(2)}) collective-permute-start(bf16[4,128,128]{2,1,0:T(8,128)(2,1)} %get-tuple-element.154), channel_id=1, source_target_pairs={{0,4},{1,5},{2,6},{3,7},{4,0},{5,1},{6,2},{7,3},{8,12},{9,13},{10,... | collective-permute-start | bytes 393224 | tf_op jit(solution)/shard_map/ppermute | solution.py:246
  42.1 2.1 %stack.5 = bf16[4,4,128,128]{3,2,1,0:T(8,128)(2,1)} custom-call(bf16[4,128,128]{2,1,0:T(8,128)(2,1)} %get-tuple-element.171.refs_0_.refs_4_, bf16[4,128,128]{2,1,0:T(8,128)(2,1)} %collective-permute-done.4.refs_1_.refs_5_, bf16[4,128,128]{2,1,0:T(8,128)(2,1)} %collective-permute-done.5.refs_2_.refs_6_, ...), custom_call_target="tpu_custom_call" | custom-call | flops 199999995904 | bytes 1048576 | tf_op jit(solution)/shard_map/stack/pallas_call | solution.py:85
  46.5 2.0 %collective-permute-done.13.refs_8_ = bf16[4,4,128,128]{3,2,1,0:T(8,128)(2,1)} collective-permute-done((bf16[4,4,128,128]{3,2,1,0:T(8,128)(2,1)}, bf16[4,4,128,128]{3,2,1,0:T(8,128)(2,1)}, u32[]{:S(2)}, u32[]{:S(2)}) %collective-permute-start.13) | collective-permute-done | bytes 524320 | tf_op jit(solution)/shard_map/ppermute | solution.py:252
  48.6 5.4 %polar.3 = (bf16[4,128,128]{2,1,0:T(8,128)(2,1)S(1)}, bf16[4,128,128]{2,1,0:T(8,128)(2,1)}, bf16[4,128,128]{2,1,0:T(8,128)(2,1)}, bf16[4,128,128]{2,1,0:T(8,128)(2,1)}) custom-call(s32[8,4]{1,0:T(8,128)S(1)} %copy.8.refs_0_, s32[8]{0:T(128)S(1)} %copy-done.4, bf16[1024,1024]{1,0:T(8,128)(2,1)S(1)} %copy-done.1, bf16[128,1024]{1,0:T(8,128)(2,1)S(1)} %copy-done.3, ...), custom_call_target="tpu_custom_call" | custom-call | flops 199999995904 | bytes 1048576 | tf_op jit(solution)/shard_map/polar/pallas_call | solution.py:151
  58.0 2.0 %stack.4 = bf16[4,4,128,128]{3,2,1,0:T(8,128)(2,1)} custom-call(bf16[4,128,128]{2,1,0:T(8,128)(2,1)} %get-tuple-element.163.refs_0_.refs_4_, bf16[4,128,128]{2,1,0:T(8,128)(2,1)} %collective-permute-done.10.refs_1_.refs_5_, bf16[4,128,128]{2,1,0:T(8,128)(2,1)} %collective-permute-done.11.refs_2_.refs_6_, ...), custom_call_target="tpu_custom_call" | custom-call | flops 1 | bytes 1048576 | tf_op jit(solution)/shard_map/stack/pallas_call | solution.py:85
  60.1 3.3 %collective-permute-done.9 = bf16[5,4,128,128]{3,2,1,0:T(8,128)(2,1)} collective-permute-done((bf16[5,4,128,128]{3,2,1,0:T(8,128)(2,1)}, bf16[5,4,128,128]{3,2,1,0:T(8,128)(2,1)}, u32[]{:S(2)}, u32[]{:S(2)}) %collective-permute-start.9) | collective-permute-done | bytes 655392 | tf_op jit(solution)/shard_map/ppermute | solution.py:255
  64.8 5.3 %polar.4 = (bf16[4,128,128]{2,1,0:T(8,128)(2,1)S(1)}, bf16[4,128,128]{2,1,0:T(8,128)(2,1)}, bf16[4,128,128]{2,1,0:T(8,128)(2,1)}, bf16[4,128,128]{2,1,0:T(8,128)(2,1)}) custom-call(s32[8,4]{1,0:T(8,128)S(1)} %copy.8.refs_0_, s32[8]{0:T(128)S(1)} %copy-done.4, bf16[1024,1024]{1,0:T(8,128)(2,1)S(1)} %copy-done.1, bf16[128,1024]{1,0:T(8,128)(2,1)S(1)} %copy-done.3, ...), custom_call_target="tpu_custom_call" | custom-call | flops 199999995904 | bytes 1048576 | tf_op jit(solution)/shard_map/polar/pallas_call | solution.py:151
  70.3 2.0 %collective-permute-start.22 = (bf16[4,128,128]{2,1,0:T(8,128)(2,1)}, bf16[4,128,128]{2,1,0:T(8,128)(2,1)}, u32[]{:S(2)}, u32[]{:S(2)}) collective-permute-start(bf16[4,128,128]{2,1,0:T(8,128)(2,1)} %get-tuple-element.201), channel_id=1, source_target_pairs={{0,4},{1,5},{2,6},{3,7},{4,0},{5,1},{6,2},{7,3},{8,12},{9,13},{10,... | collective-permute-start | bytes 393224 | tf_op jit(solution)/shard_map/ppermute | solution.py:246
  72.2 1.8 %collective-permute-start.23 = (bf16[4,128,128]{2,1,0:T(8,128)(2,1)}, bf16[4,128,128]{2,1,0:T(8,128)(2,1)}, u32[]{:S(2)}, u32[]{:S(2)}) collective-permute-start(bf16[4,128,128]{2,1,0:T(8,128)(2,1)} %get-tuple-element.202), channel_id=1, source_target_pairs={{0,6},{1,7},{2,0},{3,1},{4,2},{5,3},{6,4},{7,5},{8,14},{9,15},{10,... | collective-permute-start | bytes 393224 | tf_op jit(solution)/shard_map/ppermute | solution.py:246
  74.4 5.4 %polar.5 = (bf16[4,128,128]{2,1,0:T(8,128)(2,1)S(1)}, bf16[4,128,128]{2,1,0:T(8,128)(2,1)}, bf16[4,128,128]{2,1,0:T(8,128)(2,1)}, bf16[4,128,128]{2,1,0:T(8,128)(2,1)}) custom-call(s32[8,4]{1,0:T(8,128)S(1)} %copy.8.refs_0_, s32[8]{0:T(128)S(1)} %copy-done.4, bf16[1024,1024]{1,0:T(8,128)(2,1)S(1)} %copy-done.1, bf16[128,1024]{1,0:T(8,128)(2,1)S(1)} %copy-done.3, ...), custom_call_target="tpu_custom_call" | custom-call | flops 199999995904 | bytes 1048576 | tf_op jit(solution)/shard_map/polar/pallas_call | solution.py:151
  81.3 2.6 %collective-permute-start.26 = (bf16[4,128,128]{2,1,0:T(8,128)(2,1)}, bf16[4,128,128]{2,1,0:T(8,128)(2,1)}, u32[]{:S(2)}, u32[]{:S(2)}) collective-permute-start(bf16[4,128,128]{2,1,0:T(8,128)(2,1)} %get-tuple-element.220), channel_id=1, source_target_pairs={{0,2},{1,3},{2,4},{3,5},{4,6},{5,7},{6,0},{7,1},{8,10},{9,11},{10,... | collective-permute-start | bytes 393224 | tf_op jit(solution)/shard_map/ppermute | solution.py:246
  86.3 4.9 %chi.2 = (f32[8,6,12]{2,1,0:T(8,128)S(1)}, bf16[12,512,128]{2,1,0:T(8,128)(2,1)S(1)}, bf16[7,512,128]{2,1,0:T(8,128)(2,1)S(1)}, bf16[12,512,128]{2,1,0:T(8,128)(...) custom-call(bf16[12,512,128]{2,1,0:T(8,128)(2,1)S(1)} %bitcast.19, ...), custom_call_target="tpu_custom_call" | custom-call | flops 199999995904 | bytes 1048576 | tf_op jit(solution)/shard_map/chi/pallas_call | solution.py:221
  91.2 3.3 %collective-permute-done.27 = bf16[4,128,128]{2,1,0:T(8,128)(2,1)} collective-permute-done((bf16[4,128,128]{2,1,0:T(8,128)(2,1)}, bf16[4,128,128]{2,1,0:T(8,128)(2,1)}, u32[]{:S(2)}, u32[]{:S(2)}) %collective-permute-start.27) | collective-permute-done | bytes 131104 | tf_op jit(solution)/shard_map/ppermute | solution.py:246
  94.5 2.9 %chi.3 = f32[8,6,12]{2,1,0:T(8,128)S(1)} custom-call(bf16[12,512,128]{2,1,0:T(8,128)(2,1)S(1)} %get-tuple-element.213.refs_0_, bf16[7,512,128]{2,1,0:T(8,128)(2,1)S(1)} %get-tuple-element.214.refs_1_, bf16[12,512,128]{2,1,0:T(8,128)(2,1)S(1)} %get-tuple-element.215.refs_2_, bf16[5,512,128]{2,1,0:T(8,128)(2,1)S(1)} %get-tuple-element.216.refs_3_, ...), custom_call_target="tpu_custom_call" | custom-call | flops 199999995904 | bytes 1048576 | tf_op jit(solution)/shard_map/chi/pallas_call | solution.py:221
  97.4 11.9 %all_to_all.5 = f32[8,6,12]{2,1,0:T(8,128)S(1)} all-to-all(f32[8,6,12]{2,1,0:T(8,128)S(1)} %chi.3), channel_id=1, replica_groups=mesh['aux'=4,'pair'=8] {'pair'}, dimensions={0} | all-to-all | bytes 4608 | tf_op jit(solution)/shard_map/all_to_all | solution.py:338
  (64 shorter events, 24.1 us)
Async XLA Ops:
  0.0 21.5 %collective-permute-start.3 = (bf16[12,4,128,128]{3,2,1,0:T(8,128)(2,1)}, bf16[12,4,128,128]{3,2,1,0:T(8,128)(2,1)}, u32[]{:S(2)}, u32[]{:S(2)}) collective-permute-start(bf16[12,4,128,128]{3,2,1,0:T(8,128)(2,1)} %refs_0_.7), channel_id=1, source_target_pairs={{0,8},{8,0},{16,24},{24,16},{1,9},{9,1},{17,25},{25,17},{2,10},{10... | collective-permute-start | bytes 4718600 | tf_op jit(solution)/shard_map/ppermute | solution.py:255
  2.5 10.8 %collective-permute-start = (bf16[6,128,128]{2,1,0:T(8,128)(2,1)}, bf16[6,128,128]{2,1,0:T(8,128)(2,1)}, u32[]{:S(2)}, u32[]{:S(2)}) collective-permute-start(bf16[6,128,128]{2,1,0:T(8,128)(2,1)} %get-tuple-element.123), channel_id=1, source_target_pairs={{0,2},{1,3},{2,4},{3,5},{4,6},{5,7},{6,0},{7,1},{8,10},{9,11},{10,... | collective-permute-start | bytes 589832 | tf_op jit(solution)/shard_map/ppermute | solution.py:246
  5.1 16.4 %collective-permute-start.1 = (bf16[6,128,128]{2,1,0:T(8,128)(2,1)}, bf16[6,128,128]{2,1,0:T(8,128)(2,1)}, u32[]{:S(2)}, u32[]{:S(2)}) collective-permute-start(bf16[6,128,128]{2,1,0:T(8,128)(2,1)} %get-tuple-element.124), channel_id=1, source_target_pairs={{0,4},{1,5},{2,6},{3,7},{4,0},{5,1},{6,2},{7,3},{8,12},{9,13},{10,... | collective-permute-start | bytes 589832 | tf_op jit(solution)/shard_map/ppermute | solution.py:246
  7.6 13.9 %collective-permute-start.2 = (bf16[6,128,128]{2,1,0:T(8,128)(2,1)}, bf16[6,128,128]{2,1,0:T(8,128)(2,1)}, u32[]{:S(2)}, u32[]{:S(2)}) collective-permute-start(bf16[6,128,128]{2,1,0:T(8,128)(2,1)} %get-tuple-element.125), channel_id=1, source_target_pairs={{0,6},{1,7},{2,0},{3,1},{4,2},{5,3},{6,4},{7,5},{8,14},{9,15},{10,... | collective-permute-start | bytes 589832 | tf_op jit(solution)/shard_map/ppermute | solution.py:246
  11.7 23.1 %collective-permute-start.8 = (bf16[7,4,128,128]{3,2,1,0:T(8,128)(2,1)}, bf16[7,4,128,128]{3,2,1,0:T(8,128)(2,1)}, u32[]{:S(2)}, u32[]{:S(2)}) collective-permute-start(bf16[7,4,128,128]{3,2,1,0:T(8,128)(2,1)} %get-tuple-element.121), channel_id=1, source_target_pairs={{0,16},{8,24},{16,0},{24,8},{1,17},{9,25},{17,1},{25,9},{2,18},{10... | collective-permute-start | bytes 2752520 | tf_op jit(solution)/shard_map/ppermute | solution.py:255
  21.5 14.7 %collective-permute-start.4 = (bf16[4,128,128]{2,1,0:T(8,128)(2,1)}, bf16[4,128,128]{2,1,0:T(8,128)(2,1)}, u32[]{:S(2)}, u32[]{:S(2)}) collective-permute-start(bf16[4,128,128]{2,1,0:T(8,128)(2,1)} %get-tuple-element.137), channel_id=1, source_target_pairs={{0,2},{1,3},{2,4},{3,5},{4,6},{5,7},{6,0},{7,1},{8,10},{9,11},{10,... | collective-permute-start | bytes 393224 | tf_op jit(solution)/shard_map/ppermute | solution.py:246
  26.2 10.4 %collective-permute-start.5 = (bf16[4,128,128]{2,1,0:T(8,128)(2,1)}, bf16[4,128,128]{2,1,0:T(8,128)(2,1)}, u32[]{:S(2)}, u32[]{:S(2)}) collective-permute-start(bf16[4,128,128]{2,1,0:T(8,128)(2,1)} %get-tuple-element.138), channel_id=1, source_target_pairs={{0,4},{1,5},{2,6},{3,7},{4,0},{5,1},{6,2},{7,3},{8,12},{9,13},{10,... | collective-permute-start | bytes 393224 | tf_op jit(solution)/shard_map/ppermute | solution.py:246
  27.8 8.9 %collective-permute-start.6 = (bf16[4,128,128]{2,1,0:T(8,128)(2,1)}, bf16[4,128,128]{2,1,0:T(8,128)(2,1)}, u32[]{:S(2)}, u32[]{:S(2)}) collective-permute-start(bf16[4,128,128]{2,1,0:T(8,128)(2,1)} %get-tuple-element.139), channel_id=1, source_target_pairs={{0,6},{1,7},{2,0},{3,1},{4,2},{5,3},{6,4},{7,5},{8,14},{9,15},{10,... | collective-permute-start | bytes 393224 | tf_op jit(solution)/shard_map/ppermute | solution.py:246
  34.7 13.7 %collective-permute-start.13 = (bf16[4,4,128,128]{3,2,1,0:T(8,128)(2,1)}, bf16[4,4,128,128]{3,2,1,0:T(8,128)(2,1)}, u32[]{:S(2)}, u32[]{:S(2)}) collective-permute-start(bf16[4,4,128,128]{3,2,1,0:T(8,128)(2,1)} %get-tuple-element.156), channel_id=1, source_target_pairs={{0,1},{1,0},{2,3},{3,2},{4,5},{5,4},{6,7},{7,6},{8,9},{9,8},{10,11... | collective-permute-start | bytes 1572872 | tf_op jit(solution)/shard_map/ppermute | solution.py:252
  38.1 15.9 %collective-permute-start.10 = (bf16[4,128,128]{2,1,0:T(8,128)(2,1)}, bf16[4,128,128]{2,1,0:T(8,128)(2,1)}, u32[]{:S(2)}, u32[]{:S(2)}) collective-permute-start(bf16[4,128,128]{2,1,0:T(8,128)(2,1)} %get-tuple-element.153), channel_id=1, source_target_pairs={{0,2},{1,3},{2,4},{3,5},{4,6},{5,7},{6,0},{7,1},{8,10},{9,11},{10,... | collective-permute-start | bytes 393224 | tf_op jit(solution)/shard_map/ppermute | solution.py:246
  39.9 14.1 %collective-permute-start.11 = (bf16[4,128,128]{2,1,0:T(8,128)(2,1)}, bf16[4,128,128]{2,1,0:T(8,128)(2,1)}, u32[]{:S(2)}, u32[]{:S(2)}) collective-permute-start(bf16[4,128,128]{2,1,0:T(8,128)(2,1)} %get-tuple-element.154), channel_id=1, source_target_pairs={{0,4},{1,5},{2,6},{3,7},{4,0},{5,1},{6,2},{7,3},{8,12},{9,13},{10,... | collective-permute-start | bytes 393224 | tf_op jit(solution)/shard_map/ppermute | solution.py:246
  44.3 9.8 %collective-permute-start.12 = (bf16[4,128,128]{2,1,0:T(8,128)(2,1)}, bf16[4,128,128]{2,1,0:T(8,128)(2,1)}, u32[]{:S(2)}, u32[]{:S(2)}) collective-permute-start(bf16[4,128,128]{2,1,0:T(8,128)(2,1)} %get-tuple-element.155), channel_id=1, source_target_pairs={{0,6},{1,7},{2,0},{3,1},{4,2},{5,3},{6,4},{7,5},{8,14},{9,15},{10,... | collective-permute-start | bytes 393224 | tf_op jit(solution)/shard_map/ppermute | solution.py:246
  45.0 19.9 %collective-permute-start.17 = (bf16[4,4,128,128]{3,2,1,0:T(8,128)(2,1)}, bf16[4,4,128,128]{3,2,1,0:T(8,128)(2,1)}, u32[]{:S(2)}, u32[]{:S(2)}) collective-permute-start(bf16[4,4,128,128]{3,2,1,0:T(8,128)(2,1)} %stack.5), channel_id=1, source_target_pairs={{0,1},{1,0},{2,3},{3,2},{4,5},{5,4},{6,7},{7,6},{8,9},{9,8},{10,11... | collective-permute-start | bytes 1572872 | tf_op jit(solution)/shard_map/ppermute | solution.py:252
  48.5 14.8 %collective-permute-start.9 = (bf16[5,4,128,128]{3,2,1,0:T(8,128)(2,1)}, bf16[5,4,128,128]{3,2,1,0:T(8,128)(2,1)}, u32[]{:S(2)}, u32[]{:S(2)}) collective-permute-start(bf16[5,4,128,128]{3,2,1,0:T(8,128)(2,1)} %get-tuple-element.143), channel_id=1, source_target_pairs={{0,16},{8,24},{16,0},{24,8},{1,17},{9,25},{17,1},{25,9},{2,18},{10... | collective-permute-start | bytes 1966088 | tf_op jit(solution)/shard_map/ppermute | solution.py:255
  54.0 16.1 %collective-permute-start.18 = (bf16[4,128,128]{2,1,0:T(8,128)(2,1)}, bf16[4,128,128]{2,1,0:T(8,128)(2,1)}, u32[]{:S(2)}, u32[]{:S(2)}) collective-permute-start(bf16[4,128,128]{2,1,0:T(8,128)(2,1)} %get-tuple-element.184), channel_id=1, source_target_pairs={{0,2},{1,3},{2,4},{3,5},{4,6},{5,7},{6,0},{7,1},{8,10},{9,11},{10,... | collective-permute-start | bytes 393224 | tf_op jit(solution)/shard_map/ppermute | solution.py:246
  54.8 15.4 %collective-permute-start.19 = (bf16[4,128,128]{2,1,0:T(8,128)(2,1)}, bf16[4,128,128]{2,1,0:T(8,128)(2,1)}, u32[]{:S(2)}, u32[]{:S(2)}) collective-permute-start(bf16[4,128,128]{2,1,0:T(8,128)(2,1)} %get-tuple-element.185), channel_id=1, source_target_pairs={{0,4},{1,5},{2,6},{3,7},{4,0},{5,1},{6,2},{7,3},{8,12},{9,13},{10,... | collective-permute-start | bytes 393224 | tf_op jit(solution)/shard_map/ppermute | solution.py:246
  56.4 13.7 %collective-permute-start.20 = (bf16[4,128,128]{2,1,0:T(8,128)(2,1)}, bf16[4,128,128]{2,1,0:T(8,128)(2,1)}, u32[]{:S(2)}, u32[]{:S(2)}) collective-permute-start(bf16[4,128,128]{2,1,0:T(8,128)(2,1)} %get-tuple-element.186), channel_id=1, source_target_pairs={{0,6},{1,7},{2,0},{3,1},{4,2},{5,3},{6,4},{7,5},{8,14},{9,15},{10,... | collective-permute-start | bytes 393224 | tf_op jit(solution)/shard_map/ppermute | solution.py:246
  63.3 11.1 %collective-permute-start.16 = (bf16[4,4,128,128]{3,2,1,0:T(8,128)(2,1)}, bf16[4,4,128,128]{3,2,1,0:T(8,128)(2,1)}, u32[]{:S(2)}, u32[]{:S(2)}) collective-permute-start(bf16[4,4,128,128]{3,2,1,0:T(8,128)(2,1)} %stack.4), channel_id=1, source_target_pairs={{0,1},{1,0},{2,3},{3,2},{4,5},{5,4},{6,7},{7,6},{8,9},{9,8},{10,11... | collective-permute-start | bytes 1572872 | tf_op jit(solution)/shard_map/ppermute | solution.py:252
  70.2 9.6 %collective-permute-start.21 = (bf16[4,128,128]{2,1,0:T(8,128)(2,1)}, bf16[4,128,128]{2,1,0:T(8,128)(2,1)}, u32[]{:S(2)}, u32[]{:S(2)}) collective-permute-start(bf16[4,128,128]{2,1,0:T(8,128)(2,1)} %get-tuple-element.200), channel_id=1, source_target_pairs={{0,2},{1,3},{2,4},{3,5},{4,6},{5,7},{6,0},{7,1},{8,10},{9,11},{10,... | collective-permute-start | bytes 393224 | tf_op jit(solution)/shard_map/ppermute | solution.py:246
  70.3 10.5 %collective-permute-start.22 = (bf16[4,128,128]{2,1,0:T(8,128)(2,1)}, bf16[4,128,128]{2,1,0:T(8,128)(2,1)}, u32[]{:S(2)}, u32[]{:S(2)}) collective-permute-start(bf16[4,128,128]{2,1,0:T(8,128)(2,1)} %get-tuple-element.201), channel_id=1, source_target_pairs={{0,4},{1,5},{2,6},{3,7},{4,0},{5,1},{6,2},{7,3},{8,12},{9,13},{10,... | collective-permute-start | bytes 393224 | tf_op jit(solution)/shard_map/ppermute | solution.py:246
  72.2 8.5 %collective-permute-start.23 = (bf16[4,128,128]{2,1,0:T(8,128)(2,1)}, bf16[4,128,128]{2,1,0:T(8,128)(2,1)}, u32[]{:S(2)}, u32[]{:S(2)}) collective-permute-start(bf16[4,128,128]{2,1,0:T(8,128)(2,1)} %get-tuple-element.202), channel_id=1, source_target_pairs={{0,6},{1,7},{2,0},{3,1},{4,2},{5,3},{6,4},{7,5},{8,14},{9,15},{10,... | collective-permute-start | bytes 393224 | tf_op jit(solution)/shard_map/ppermute | solution.py:246
  81.3 9.9 %collective-permute-start.26 = (bf16[4,128,128]{2,1,0:T(8,128)(2,1)}, bf16[4,128,128]{2,1,0:T(8,128)(2,1)}, u32[]{:S(2)}, u32[]{:S(2)}) collective-permute-start(bf16[4,128,128]{2,1,0:T(8,128)(2,1)} %get-tuple-element.220), channel_id=1, source_target_pairs={{0,2},{1,3},{2,4},{3,5},{4,6},{5,7},{6,0},{7,1},{8,10},{9,11},{10,... | collective-permute-start | bytes 393224 | tf_op jit(solution)/shard_map/ppermute | solution.py:246
  83.9 10.6 %collective-permute-start.27 = (bf16[4,128,128]{2,1,0:T(8,128)(2,1)}, bf16[4,128,128]{2,1,0:T(8,128)(2,1)}, u32[]{:S(2)}, u32[]{:S(2)}) collective-permute-start(bf16[4,128,128]{2,1,0:T(8,128)(2,1)} %get-tuple-element.221), channel_id=1, source_target_pairs={{0,4},{1,5},{2,6},{3,7},{4,0},{5,1},{6,2},{7,3},{8,12},{9,13},{10,... | collective-permute-start | bytes 393224 | tf_op jit(solution)/shard_map/ppermute | solution.py:246
  85.2 9.3 %collective-permute-start.28 = (bf16[4,128,128]{2,1,0:T(8,128)(2,1)}, bf16[4,128,128]{2,1,0:T(8,128)(2,1)}, u32[]{:S(2)}, u32[]{:S(2)}) collective-permute-start(bf16[4,128,128]{2,1,0:T(8,128)(2,1)} %get-tuple-element.222), channel_id=1, source_target_pairs={{0,6},{1,7},{2,0},{3,1},{4,2},{5,3},{6,4},{7,5},{8,14},{9,15},{10,... | collective-permute-start | bytes 393224 | tf_op jit(solution)/shard_map/ppermute | solution.py:246
  (13 other events, 92.3 us)

commit v4 on v3

--- a/solution.py
+++ b/solution.py
@@ -255,11 +255,11 @@
         return lax.ppermute(array, "aux", [(a, a ^ bit) for a in range(peers)])
 
     def shift(arrays, between=lambda: None):
-        order = sorted(range(1, groups), key=lambda d: -min(d, groups - d))
+        order = sorted(range(1, groups), key=lambda d: (min(d, groups - d), -d))
         moved = {0: arrays[0]}
         for d in order:
             moved[d] = along_high(arrays[d], d)
-            if d == order[0]:
+            if d == order[-1]:
                 between()
         return [moved[d] for d in range(groups)]
 

time: 110 us -> 110 us (level)
  no operation moved by 1% of the time
where the time goes in v4:
time: 110 us
  starting transfers between devices  39.8 us (36%)
  Pallas kernels  37.3 us (34%)
  waiting for transfers between devices  20.1 us (18%)
  blocking collectives  11.9 us (11%)
    ppermute x18, starting transfers between devices, along_high(): return lax.ppermute(array, 'pair', moves)  30.7 us
    pallas_call x3, Pallas kernels, polar(): pl.pallas_call(lambda *refs: polar_kernel(groups, lows, masks, *refs), ou...  16.1 us
    ppermute x18, waiting for transfers between devices, along_high(): return lax.ppermute(array, 'pair', moves)  13 us
    all_to_all x1, blocking collectives, per_device(): return jnp.sum(lax.all_to_all(part, 'pair', 0, 0, tiled=True), axis=0)  11.9 us
    pallas_call x2, Pallas kernels, chi(): pl.pallas_call(lambda *refs: chi_kernel(groups, lows, chunks, factor, pla...  7.75 us
    pallas_call x3, Pallas kernels, split(): pl.pallas_call(lambda *refs: split_kernel(groups, lows, chunk, shares, co...  7.18 us
    pallas_call x3, Pallas kernels, stack(): pl.pallas_call(lambda *refs: stack_kernel(groups, slots, *refs), out_shap...  6.3 us
    ppermute x8, waiting for transfers between devices, swap(): return lax.ppermute(array, 'aux', [(a, a ^ bit) for a in range(peers)])  4.71 us
  transfers between devices with their start and end apart: 29, of which 9 were waited for; matrix products, arithmetic and copies ran while one was open for 0% of the time, Pallas kernels for 31%

profile of v4, /device:TPU:0, one launch (start us, length us, event | category | flops | bytes accessed | tf_op | source)
XLA Modules:
  0.0 109.9 jit_solution(16819632752799038605)
XLA Ops:
  0.5 2.0 %split.4 = (bf16[4,128,128]{2,1,0:T(8,128)(2,1)}, bf16[6,128,128]{2,1,0:T(8,128)(2,1)}, bf16[6,128,128]{2,1,0:T(8,128)(2,1)}, bf16[6,128,128]{2,1,0:T(8,128)(2,1)}) custom-call(bf16[12,4,128,128]{3,2,1,0:T(8,128)(2,1)} %refs_0_.7, bf16[128,1024]{1,0:T(8,128)(2,1)} %refs_3_.5), custom_call_target="tpu_custom_call" | custom-call | flops 199999995904 | bytes 1048576 | tf_op jit(solution)/shard_map/split/pallas_call | solution.py:59
  2.5 2.6 %collective-permute-start = (bf16[6,128,128]{2,1,0:T(8,128)(2,1)}, bf16[6,128,128]{2,1,0:T(8,128)(2,1)}, u32[]{:S(2)}, u32[]{:S(2)}) collective-permute-start(bf16[6,128,128]{2,1,0:T(8,128)(2,1)} %get-tuple-element.123), channel_id=1, source_target_pairs={{0,2},{1,3},{2,4},{3,5},{4,6},{5,7},{6,0},{7,1},{8,10},{9,11},{10,... | collective-permute-start | bytes 589832 | tf_op jit(solution)/shard_map/ppermute | solution.py:246
  5.1 2.6 %collective-permute-start.1 = (bf16[6,128,128]{2,1,0:T(8,128)(2,1)}, bf16[6,128,128]{2,1,0:T(8,128)(2,1)}, u32[]{:S(2)}, u32[]{:S(2)}) collective-permute-start(bf16[6,128,128]{2,1,0:T(8,128)(2,1)} %get-tuple-element.124), channel_id=1, source_target_pairs={{0,4},{1,5},{2,6},{3,7},{4,0},{5,1},{6,2},{7,3},{8,12},{9,13},{10,... | collective-permute-start | bytes 589832 | tf_op jit(solution)/shard_map/ppermute | solution.py:246
  9.0 2.7 %split.3 = (bf16[4,128,128]{2,1,0:T(8,128)(2,1)}, bf16[4,128,128]{2,1,0:T(8,128)(2,1)}, bf16[4,128,128]{2,1,0:T(8,128)(2,1)}, bf16[4,128,128]{2,1,0:T(8,128)(2,1)}, bf16[7,4,128,128]{3,2,1,0:T(8,128)(2,1)}) custom-call(bf16[12,4,128,128]{3,2,1,0:T(8,128)(2,1)} %refs_0_.7), custom_call_target="tpu_custom_call" | custom-call | flops 199999995904 | bytes 1048576 | tf_op jit(solution)/shard_map/split/pallas_call | solution.py:59
  13.3 8.2 %collective-permute-done.1.refs_2_.refs_6_ = bf16[6,128,128]{2,1,0:T(8,128)(2,1)} collective-permute-done((bf16[6,128,128]{2,1,0:T(8,128)(2,1)}, bf16[6,128,128]{2,1,0:T(8,128)(2,1)}, u32[]{:S(2)}, u32[]{:S(2)}) %collective-permute-start.1) | collective-permute-done | bytes 196640 | tf_op jit(solution)/shard_map/ppermute | solution.py:246
  21.5 4.7 %collective-permute-start.4 = (bf16[4,128,128]{2,1,0:T(8,128)(2,1)}, bf16[4,128,128]{2,1,0:T(8,128)(2,1)}, u32[]{:S(2)}, u32[]{:S(2)}) collective-permute-start(bf16[4,128,128]{2,1,0:T(8,128)(2,1)} %get-tuple-element.137), channel_id=1, source_target_pairs={{0,2},{1,3},{2,4},{3,5},{4,6},{5,7},{6,0},{7,1},{8,10},{9,11},{10,... | collective-permute-start | bytes 393224 | tf_op jit(solution)/shard_map/ppermute | solution.py:246
  28.6 2.2 %stack.3 = (bf16[4,4,128,128]{3,2,1,0:T(8,128)(2,1)}, bf16[3,2,128,128]{3,2,1,0:T(8,128)(2,1)}) custom-call(bf16[4,128,128]{2,1,0:T(8,128)(2,1)} %get-tuple-element.144.refs_0_.refs_4_, bf16[6,128,128]{2,1,0:T(8,128)(2,1)} %collective-permute-done.refs_1_.refs_5_, bf16[6,128,128]{2,1,0:T(8,128)(2,1)} %collective-permute-done.1.refs_2_.refs_6_, ...), custom_call_target="tpu_custom_call" | custom-call | flops 199999995904 | bytes 1048576 | tf_op jit(solution)/shard_map/stack/pallas_call | solution.py:85
  32.2 2.5 %split.5 = (bf16[4,128,128]{2,1,0:T(8,128)(2,1)}, bf16[4,128,128]{2,1,0:T(8,128)(2,1)}, bf16[4,128,128]{2,1,0:T(8,128)(2,1)}, bf16[4,128,128]{2,1,0:T(8,128)(2,1)}, bf16[5,4,128,128]{3,2,1,0:T(8,128)(2,1)}) custom-call(bf16[12,4,128,128]{3,2,1,0:T(8,128)(2,1)} %refs_0_.7), custom_call_target="tpu_custom_call" | custom-call | flops 199999995904 | bytes 1048576 | tf_op jit(solution)/shard_map/split/pallas_call | solution.py:59
  38.1 1.8 %collective-permute-start.10 = (bf16[4,128,128]{2,1,0:T(8,128)(2,1)}, bf16[4,128,128]{2,1,0:T(8,128)(2,1)}, u32[]{:S(2)}, u32[]{:S(2)}) collective-permute-start(bf16[4,128,128]{2,1,0:T(8,128)(2,1)} %get-tuple-element.153), channel_id=1, source_target_pairs={{0,2},{1,3},{2,4},{3,5},{4,6},{5,7},{6,0},{7,1},{8,10},{9,11},{10,... | collective-permute-start | bytes 393224 | tf_op jit(solution)/shard_map/ppermute | solution.py:246
  39.9 1.7 %collective-permute-start.11 = (bf16[4,128,128]{2,1,0:T(8,128)(2,1)}, bf16[4,128,128]{2,1,0:T(8,128)(2,1)}, u32[]{:S(2)}, u32[]{:S(2)}) collective-permute-start(bf16[4,128,128]{2,1,0:T(8,128)(2,1)} %get-tuple-element.154), channel_id=1, source_target_pairs={{0,4},{1,5},{2,6},{3,7},{4,0},{5,1},{6,2},{7,3},{8,12},{9,13},{10,... | collective-permute-start | bytes 393224 | tf_op jit(solution)/shard_map/ppermute | solution.py:246
  42.1 2.1 %stack.5 = bf16[4,4,128,128]{3,2,1,0:T(8,128)(2,1)} custom-call(bf16[4,128,128]{2,1,0:T(8,128)(2,1)} %get-tuple-element.171.refs_0_.refs_4_, bf16[4,128,128]{2,1,0:T(8,128)(2,1)} %collective-permute-done.4.refs_1_.refs_5_, bf16[4,128,128]{2,1,0:T(8,128)(2,1)} %collective-permute-done.5.refs_2_.refs_6_, ...), custom_call_target="tpu_custom_call" | custom-call | flops 199999995904 | bytes 1048576 | tf_op jit(solution)/shard_map/stack/pallas_call | solution.py:85
  46.5 2.0 %collective-permute-done.13.refs_8_ = bf16[4,4,128,128]{3,2,1,0:T(8,128)(2,1)} collective-permute-done((bf16[4,4,128,128]{3,2,1,0:T(8,128)(2,1)}, bf16[4,4,128,128]{3,2,1,0:T(8,128)(2,1)}, u32[]{:S(2)}, u32[]{:S(2)}) %collective-permute-start.13) | collective-permute-done | bytes 524320 | tf_op jit(solution)/shard_map/ppermute | solution.py:252
  48.6 5.4 %polar.3 = (bf16[4,128,128]{2,1,0:T(8,128)(2,1)S(1)}, bf16[4,128,128]{2,1,0:T(8,128)(2,1)}, bf16[4,128,128]{2,1,0:T(8,128)(2,1)}, bf16[4,128,128]{2,1,0:T(8,128)(2,1)}) custom-call(s32[8,4]{1,0:T(8,128)S(1)} %copy.8.refs_0_, s32[8]{0:T(128)S(1)} %copy-done.4, bf16[1024,1024]{1,0:T(8,128)(2,1)S(1)} %copy-done.1, bf16[128,1024]{1,0:T(8,128)(2,1)S(1)} %copy-done.3, ...), custom_call_target="tpu_custom_call" | custom-call | flops 199999995904 | bytes 1048576 | tf_op jit(solution)/shard_map/polar/pallas_call | solution.py:151
  58.1 2.0 %stack.4 = bf16[4,4,128,128]{3,2,1,0:T(8,128)(2,1)} custom-call(bf16[4,128,128]{2,1,0:T(8,128)(2,1)} %get-tuple-element.163.refs_0_.refs_4_, bf16[4,128,128]{2,1,0:T(8,128)(2,1)} %collective-permute-done.10.refs_1_.refs_5_, bf16[4,128,128]{2,1,0:T(8,128)(2,1)} %collective-permute-done.11.refs_2_.refs_6_, ...), custom_call_target="tpu_custom_call" | custom-call | flops 1 | bytes 1048576 | tf_op jit(solution)/shard_map/stack/pallas_call | solution.py:85
  60.1 3.2 %collective-permute-done.9 = bf16[5,4,128,128]{3,2,1,0:T(8,128)(2,1)} collective-permute-done((bf16[5,4,128,128]{3,2,1,0:T(8,128)(2,1)}, bf16[5,4,128,128]{3,2,1,0:T(8,128)(2,1)}, u32[]{:S(2)}, u32[]{:S(2)}) %collective-permute-start.9) | collective-permute-done | bytes 655392 | tf_op jit(solution)/shard_map/ppermute | solution.py:255
  64.8 5.3 %polar.4 = (bf16[4,128,128]{2,1,0:T(8,128)(2,1)S(1)}, bf16[4,128,128]{2,1,0:T(8,128)(2,1)}, bf16[4,128,128]{2,1,0:T(8,128)(2,1)}, bf16[4,128,128]{2,1,0:T(8,128)(2,1)}) custom-call(s32[8,4]{1,0:T(8,128)S(1)} %copy.8.refs_0_, s32[8]{0:T(128)S(1)} %copy-done.4, bf16[1024,1024]{1,0:T(8,128)(2,1)S(1)} %copy-done.1, bf16[128,1024]{1,0:T(8,128)(2,1)S(1)} %copy-done.3, ...), custom_call_target="tpu_custom_call" | custom-call | flops 199999995904 | bytes 1048576 | tf_op jit(solution)/shard_map/polar/pallas_call | solution.py:151
  70.3 2.0 %collective-permute-start.22 = (bf16[4,128,128]{2,1,0:T(8,128)(2,1)}, bf16[4,128,128]{2,1,0:T(8,128)(2,1)}, u32[]{:S(2)}, u32[]{:S(2)}) collective-permute-start(bf16[4,128,128]{2,1,0:T(8,128)(2,1)} %get-tuple-element.201), channel_id=1, source_target_pairs={{0,4},{1,5},{2,6},{3,7},{4,0},{5,1},{6,2},{7,3},{8,12},{9,13},{10,... | collective-permute-start | bytes 393224 | tf_op jit(solution)/shard_map/ppermute | solution.py:246
  72.2 1.8 %collective-permute-start.23 = (bf16[4,128,128]{2,1,0:T(8,128)(2,1)}, bf16[4,128,128]{2,1,0:T(8,128)(2,1)}, u32[]{:S(2)}, u32[]{:S(2)}) collective-permute-start(bf16[4,128,128]{2,1,0:T(8,128)(2,1)} %get-tuple-element.202), channel_id=1, source_target_pairs={{0,6},{1,7},{2,0},{3,1},{4,2},{5,3},{6,4},{7,5},{8,14},{9,15},{10,... | collective-permute-start | bytes 393224 | tf_op jit(solution)/shard_map/ppermute | solution.py:246
  74.4 5.4 %polar.5 = (bf16[4,128,128]{2,1,0:T(8,128)(2,1)S(1)}, bf16[4,128,128]{2,1,0:T(8,128)(2,1)}, bf16[4,128,128]{2,1,0:T(8,128)(2,1)}, bf16[4,128,128]{2,1,0:T(8,128)(2,1)}) custom-call(s32[8,4]{1,0:T(8,128)S(1)} %copy.8.refs_0_, s32[8]{0:T(128)S(1)} %copy-done.4, bf16[1024,1024]{1,0:T(8,128)(2,1)S(1)} %copy-done.1, bf16[128,1024]{1,0:T(8,128)(2,1)S(1)} %copy-done.3, ...), custom_call_target="tpu_custom_call" | custom-call | flops 199999995904 | bytes 1048576 | tf_op jit(solution)/shard_map/polar/pallas_call | solution.py:151
  81.3 2.6 %collective-permute-start.26 = (bf16[4,128,128]{2,1,0:T(8,128)(2,1)}, bf16[4,128,128]{2,1,0:T(8,128)(2,1)}, u32[]{:S(2)}, u32[]{:S(2)}) collective-permute-start(bf16[4,128,128]{2,1,0:T(8,128)(2,1)} %get-tuple-element.220), channel_id=1, source_target_pairs={{0,2},{1,3},{2,4},{3,5},{4,6},{5,7},{6,0},{7,1},{8,10},{9,11},{10,... | collective-permute-start | bytes 393224 | tf_op jit(solution)/shard_map/ppermute | solution.py:246
  86.3 4.9 %chi.2 = (f32[8,6,12]{2,1,0:T(8,128)S(1)}, bf16[12,512,128]{2,1,0:T(8,128)(2,1)S(1)}, bf16[7,512,128]{2,1,0:T(8,128)(2,1)S(1)}, bf16[12,512,128]{2,1,0:T(8,128)(...) custom-call(bf16[12,512,128]{2,1,0:T(8,128)(2,1)S(1)} %bitcast.19, ...), custom_call_target="tpu_custom_call" | custom-call | flops 199999995904 | bytes 1048576 | tf_op jit(solution)/shard_map/chi/pallas_call | solution.py:221
  91.2 3.3 %collective-permute-done.27 = bf16[4,128,128]{2,1,0:T(8,128)(2,1)} collective-permute-done((bf16[4,128,128]{2,1,0:T(8,128)(2,1)}, bf16[4,128,128]{2,1,0:T(8,128)(2,1)}, u32[]{:S(2)}, u32[]{:S(2)}) %collective-permute-start.27) | collective-permute-done | bytes 131104 | tf_op jit(solution)/shard_map/ppermute | solution.py:246
  94.5 2.9 %chi.3 = f32[8,6,12]{2,1,0:T(8,128)S(1)} custom-call(bf16[12,512,128]{2,1,0:T(8,128)(2,1)S(1)} %get-tuple-element.213.refs_0_, bf16[7,512,128]{2,1,0:T(8,128)(2,1)S(1)} %get-tuple-element.214.refs_1_, bf16[12,512,128]{2,1,0:T(8,128)(2,1)S(1)} %get-tuple-element.215.refs_2_, bf16[5,512,128]{2,1,0:T(8,128)(2,1)S(1)} %get-tuple-element.216.refs_3_, ...), custom_call_target="tpu_custom_call" | custom-call | flops 199999995904 | bytes 1048576 | tf_op jit(solution)/shard_map/chi/pallas_call | solution.py:221
  97.4 11.9 %all_to_all.5 = f32[8,6,12]{2,1,0:T(8,128)S(1)} all-to-all(f32[8,6,12]{2,1,0:T(8,128)S(1)} %chi.3), channel_id=1, replica_groups=mesh['aux'=4,'pair'=8] {'pair'}, dimensions={0} | all-to-all | bytes 4608 | tf_op jit(solution)/shard_map/all_to_all | solution.py:338
  (64 shorter events, 24.1 us)
Async XLA Ops:
  0.0 21.5 %collective-permute-start.3 = (bf16[12,4,128,128]{3,2,1,0:T(8,128)(2,1)}, bf16[12,4,128,128]{3,2,1,0:T(8,128)(2,1)}, u32[]{:S(2)}, u32[]{:S(2)}) collective-permute-start(bf16[12,4,128,128]{3,2,1,0:T(8,128)(2,1)} %refs_0_.7), channel_id=1, source_target_pairs={{0,8},{8,0},{16,24},{24,16},{1,9},{9,1},{17,25},{25,17},{2,10},{10... | collective-permute-start | bytes 4718600 | tf_op jit(solution)/shard_map/ppermute | solution.py:255
  2.5 10.8 %collective-permute-start = (bf16[6,128,128]{2,1,0:T(8,128)(2,1)}, bf16[6,128,128]{2,1,0:T(8,128)(2,1)}, u32[]{:S(2)}, u32[]{:S(2)}) collective-permute-start(bf16[6,128,128]{2,1,0:T(8,128)(2,1)} %get-tuple-element.123), channel_id=1, source_target_pairs={{0,2},{1,3},{2,4},{3,5},{4,6},{5,7},{6,0},{7,1},{8,10},{9,11},{10,... | collective-permute-start | bytes 589832 | tf_op jit(solution)/shard_map/ppermute | solution.py:246
  5.1 16.4 %collective-permute-start.1 = (bf16[6,128,128]{2,1,0:T(8,128)(2,1)}, bf16[6,128,128]{2,1,0:T(8,128)(2,1)}, u32[]{:S(2)}, u32[]{:S(2)}) collective-permute-start(bf16[6,128,128]{2,1,0:T(8,128)(2,1)} %get-tuple-element.124), channel_id=1, source_target_pairs={{0,4},{1,5},{2,6},{3,7},{4,0},{5,1},{6,2},{7,3},{8,12},{9,13},{10,... | collective-permute-start | bytes 589832 | tf_op jit(solution)/shard_map/ppermute | solution.py:246
  7.6 13.9 %collective-permute-start.2 = (bf16[6,128,128]{2,1,0:T(8,128)(2,1)}, bf16[6,128,128]{2,1,0:T(8,128)(2,1)}, u32[]{:S(2)}, u32[]{:S(2)}) collective-permute-start(bf16[6,128,128]{2,1,0:T(8,128)(2,1)} %get-tuple-element.125), channel_id=1, source_target_pairs={{0,6},{1,7},{2,0},{3,1},{4,2},{5,3},{6,4},{7,5},{8,14},{9,15},{10,... | collective-permute-start | bytes 589832 | tf_op jit(solution)/shard_map/ppermute | solution.py:246
  11.7 23.1 %collective-permute-start.8 = (bf16[7,4,128,128]{3,2,1,0:T(8,128)(2,1)}, bf16[7,4,128,128]{3,2,1,0:T(8,128)(2,1)}, u32[]{:S(2)}, u32[]{:S(2)}) collective-permute-start(bf16[7,4,128,128]{3,2,1,0:T(8,128)(2,1)} %get-tuple-element.121), channel_id=1, source_target_pairs={{0,16},{8,24},{16,0},{24,8},{1,17},{9,25},{17,1},{25,9},{2,18},{10... | collective-permute-start | bytes 2752520 | tf_op jit(solution)/shard_map/ppermute | solution.py:255
  21.5 14.7 %collective-permute-start.4 = (bf16[4,128,128]{2,1,0:T(8,128)(2,1)}, bf16[4,128,128]{2,1,0:T(8,128)(2,1)}, u32[]{:S(2)}, u32[]{:S(2)}) collective-permute-start(bf16[4,128,128]{2,1,0:T(8,128)(2,1)} %get-tuple-element.137), channel_id=1, source_target_pairs={{0,2},{1,3},{2,4},{3,5},{4,6},{5,7},{6,0},{7,1},{8,10},{9,11},{10,... | collective-permute-start | bytes 393224 | tf_op jit(solution)/shard_map/ppermute | solution.py:246
  26.2 10.4 %collective-permute-start.5 = (bf16[4,128,128]{2,1,0:T(8,128)(2,1)}, bf16[4,128,128]{2,1,0:T(8,128)(2,1)}, u32[]{:S(2)}, u32[]{:S(2)}) collective-permute-start(bf16[4,128,128]{2,1,0:T(8,128)(2,1)} %get-tuple-element.138), channel_id=1, source_target_pairs={{0,4},{1,5},{2,6},{3,7},{4,0},{5,1},{6,2},{7,3},{8,12},{9,13},{10,... | collective-permute-start | bytes 393224 | tf_op jit(solution)/shard_map/ppermute | solution.py:246
  27.8 8.9 %collective-permute-start.6 = (bf16[4,128,128]{2,1,0:T(8,128)(2,1)}, bf16[4,128,128]{2,1,0:T(8,128)(2,1)}, u32[]{:S(2)}, u32[]{:S(2)}) collective-permute-start(bf16[4,128,128]{2,1,0:T(8,128)(2,1)} %get-tuple-element.139), channel_id=1, source_target_pairs={{0,6},{1,7},{2,0},{3,1},{4,2},{5,3},{6,4},{7,5},{8,14},{9,15},{10,... | collective-permute-start | bytes 393224 | tf_op jit(solution)/shard_map/ppermute | solution.py:246
  34.7 13.7 %collective-permute-start.13 = (bf16[4,4,128,128]{3,2,1,0:T(8,128)(2,1)}, bf16[4,4,128,128]{3,2,1,0:T(8,128)(2,1)}, u32[]{:S(2)}, u32[]{:S(2)}) collective-permute-start(bf16[4,4,128,128]{3,2,1,0:T(8,128)(2,1)} %get-tuple-element.156), channel_id=1, source_target_pairs={{0,1},{1,0},{2,3},{3,2},{4,5},{5,4},{6,7},{7,6},{8,9},{9,8},{10,11... | collective-permute-start | bytes 1572872 | tf_op jit(solution)/shard_map/ppermute | solution.py:252
  38.1 15.9 %collective-permute-start.10 = (bf16[4,128,128]{2,1,0:T(8,128)(2,1)}, bf16[4,128,128]{2,1,0:T(8,128)(2,1)}, u32[]{:S(2)}, u32[]{:S(2)}) collective-permute-start(bf16[4,128,128]{2,1,0:T(8,128)(2,1)} %get-tuple-element.153), channel_id=1, source_target_pairs={{0,2},{1,3},{2,4},{3,5},{4,6},{5,7},{6,0},{7,1},{8,10},{9,11},{10,... | collective-permute-start | bytes 393224 | tf_op jit(solution)/shard_map/ppermute | solution.py:246
  39.9 14.1 %collective-permute-start.11 = (bf16[4,128,128]{2,1,0:T(8,128)(2,1)}, bf16[4,128,128]{2,1,0:T(8,128)(2,1)}, u32[]{:S(2)}, u32[]{:S(2)}) collective-permute-start(bf16[4,128,128]{2,1,0:T(8,128)(2,1)} %get-tuple-element.154), channel_id=1, source_target_pairs={{0,4},{1,5},{2,6},{3,7},{4,0},{5,1},{6,2},{7,3},{8,12},{9,13},{10,... | collective-permute-start | bytes 393224 | tf_op jit(solution)/shard_map/ppermute | solution.py:246
  44.3 9.8 %collective-permute-start.12 = (bf16[4,128,128]{2,1,0:T(8,128)(2,1)}, bf16[4,128,128]{2,1,0:T(8,128)(2,1)}, u32[]{:S(2)}, u32[]{:S(2)}) collective-permute-start(bf16[4,128,128]{2,1,0:T(8,128)(2,1)} %get-tuple-element.155), channel_id=1, source_target_pairs={{0,6},{1,7},{2,0},{3,1},{4,2},{5,3},{6,4},{7,5},{8,14},{9,15},{10,... | collective-permute-start | bytes 393224 | tf_op jit(solution)/shard_map/ppermute | solution.py:246
  45.0 19.9 %collective-permute-start.17 = (bf16[4,4,128,128]{3,2,1,0:T(8,128)(2,1)}, bf16[4,4,128,128]{3,2,1,0:T(8,128)(2,1)}, u32[]{:S(2)}, u32[]{:S(2)}) collective-permute-start(bf16[4,4,128,128]{3,2,1,0:T(8,128)(2,1)} %stack.5), channel_id=1, source_target_pairs={{0,1},{1,0},{2,3},{3,2},{4,5},{5,4},{6,7},{7,6},{8,9},{9,8},{10,11... | collective-permute-start | bytes 1572872 | tf_op jit(solution)/shard_map/ppermute | solution.py:252
  48.5 14.8 %collective-permute-start.9 = (bf16[5,4,128,128]{3,2,1,0:T(8,128)(2,1)}, bf16[5,4,128,128]{3,2,1,0:T(8,128)(2,1)}, u32[]{:S(2)}, u32[]{:S(2)}) collective-permute-start(bf16[5,4,128,128]{3,2,1,0:T(8,128)(2,1)} %get-tuple-element.143), channel_id=1, source_target_pairs={{0,16},{8,24},{16,0},{24,8},{1,17},{9,25},{17,1},{25,9},{2,18},{10... | collective-permute-start | bytes 1966088 | tf_op jit(solution)/shard_map/ppermute | solution.py:255
  54.0 16.1 %collective-permute-start.18 = (bf16[4,128,128]{2,1,0:T(8,128)(2,1)}, bf16[4,128,128]{2,1,0:T(8,128)(2,1)}, u32[]{:S(2)}, u32[]{:S(2)}) collective-permute-start(bf16[4,128,128]{2,1,0:T(8,128)(2,1)} %get-tuple-element.184), channel_id=1, source_target_pairs={{0,2},{1,3},{2,4},{3,5},{4,6},{5,7},{6,0},{7,1},{8,10},{9,11},{10,... | collective-permute-start | bytes 393224 | tf_op jit(solution)/shard_map/ppermute | solution.py:246
  54.8 15.4 %collective-permute-start.19 = (bf16[4,128,128]{2,1,0:T(8,128)(2,1)}, bf16[4,128,128]{2,1,0:T(8,128)(2,1)}, u32[]{:S(2)}, u32[]{:S(2)}) collective-permute-start(bf16[4,128,128]{2,1,0:T(8,128)(2,1)} %get-tuple-element.185), channel_id=1, source_target_pairs={{0,4},{1,5},{2,6},{3,7},{4,0},{5,1},{6,2},{7,3},{8,12},{9,13},{10,... | collective-permute-start | bytes 393224 | tf_op jit(solution)/shard_map/ppermute | solution.py:246
  56.4 13.7 %collective-permute-start.20 = (bf16[4,128,128]{2,1,0:T(8,128)(2,1)}, bf16[4,128,128]{2,1,0:T(8,128)(2,1)}, u32[]{:S(2)}, u32[]{:S(2)}) collective-permute-start(bf16[4,128,128]{2,1,0:T(8,128)(2,1)} %get-tuple-element.186), channel_id=1, source_target_pairs={{0,6},{1,7},{2,0},{3,1},{4,2},{5,3},{6,4},{7,5},{8,14},{9,15},{10,... | collective-permute-start | bytes 393224 | tf_op jit(solution)/shard_map/ppermute | solution.py:246
  63.3 11.1 %collective-permute-start.16 = (bf16[4,4,128,128]{3,2,1,0:T(8,128)(2,1)}, bf16[4,4,128,128]{3,2,1,0:T(8,128)(2,1)}, u32[]{:S(2)}, u32[]{:S(2)}) collective-permute-start(bf16[4,4,128,128]{3,2,1,0:T(8,128)(2,1)} %stack.4), channel_id=1, source_target_pairs={{0,1},{1,0},{2,3},{3,2},{4,5},{5,4},{6,7},{7,6},{8,9},{9,8},{10,11... | collective-permute-start | bytes 1572872 | tf_op jit(solution)/shard_map/ppermute | solution.py:252
  70.2 9.6 %collective-permute-start.21 = (bf16[4,128,128]{2,1,0:T(8,128)(2,1)}, bf16[4,128,128]{2,1,0:T(8,128)(2,1)}, u32[]{:S(2)}, u32[]{:S(2)}) collective-permute-start(bf16[4,128,128]{2,1,0:T(8,128)(2,1)} %get-tuple-element.200), channel_id=1, source_target_pairs={{0,2},{1,3},{2,4},{3,5},{4,6},{5,7},{6,0},{7,1},{8,10},{9,11},{10,... | collective-permute-start | bytes 393224 | tf_op jit(solution)/shard_map/ppermute | solution.py:246
  70.3 10.5 %collective-permute-start.22 = (bf16[4,128,128]{2,1,0:T(8,128)(2,1)}, bf16[4,128,128]{2,1,0:T(8,128)(2,1)}, u32[]{:S(2)}, u32[]{:S(2)}) collective-permute-start(bf16[4,128,128]{2,1,0:T(8,128)(2,1)} %get-tuple-element.201), channel_id=1, source_target_pairs={{0,4},{1,5},{2,6},{3,7},{4,0},{5,1},{6,2},{7,3},{8,12},{9,13},{10,... | collective-permute-start | bytes 393224 | tf_op jit(solution)/shard_map/ppermute | solution.py:246
  72.2 8.5 %collective-permute-start.23 = (bf16[4,128,128]{2,1,0:T(8,128)(2,1)}, bf16[4,128,128]{2,1,0:T(8,128)(2,1)}, u32[]{:S(2)}, u32[]{:S(2)}) collective-permute-start(bf16[4,128,128]{2,1,0:T(8,128)(2,1)} %get-tuple-element.202), channel_id=1, source_target_pairs={{0,6},{1,7},{2,0},{3,1},{4,2},{5,3},{6,4},{7,5},{8,14},{9,15},{10,... | collective-permute-start | bytes 393224 | tf_op jit(solution)/shard_map/ppermute | solution.py:246
  81.3 9.9 %collective-permute-start.26 = (bf16[4,128,128]{2,1,0:T(8,128)(2,1)}, bf16[4,128,128]{2,1,0:T(8,128)(2,1)}, u32[]{:S(2)}, u32[]{:S(2)}) collective-permute-start(bf16[4,128,128]{2,1,0:T(8,128)(2,1)} %get-tuple-element.220), channel_id=1, source_target_pairs={{0,2},{1,3},{2,4},{3,5},{4,6},{5,7},{6,0},{7,1},{8,10},{9,11},{10,... | collective-permute-start | bytes 393224 | tf_op jit(solution)/shard_map/ppermute | solution.py:246
  83.9 10.6 %collective-permute-start.27 = (bf16[4,128,128]{2,1,0:T(8,128)(2,1)}, bf16[4,128,128]{2,1,0:T(8,128)(2,1)}, u32[]{:S(2)}, u32[]{:S(2)}) collective-permute-start(bf16[4,128,128]{2,1,0:T(8,128)(2,1)} %get-tuple-element.221), channel_id=1, source_target_pairs={{0,4},{1,5},{2,6},{3,7},{4,0},{5,1},{6,2},{7,3},{8,12},{9,13},{10,... | collective-permute-start | bytes 393224 | tf_op jit(solution)/shard_map/ppermute | solution.py:246
  85.2 9.3 %collective-permute-start.28 = (bf16[4,128,128]{2,1,0:T(8,128)(2,1)}, bf16[4,128,128]{2,1,0:T(8,128)(2,1)}, u32[]{:S(2)}, u32[]{:S(2)}) collective-permute-start(bf16[4,128,128]{2,1,0:T(8,128)(2,1)} %get-tuple-element.222), channel_id=1, source_target_pairs={{0,6},{1,7},{2,0},{3,1},{4,2},{5,3},{6,4},{7,5},{8,14},{9,15},{10,... | collective-permute-start | bytes 393224 | tf_op jit(solution)/shard_map/ppermute | solution.py:246
  (13 other events, 92.3 us)

commit v5 on v4

--- a/solution.py
+++ b/solution.py
@@ -13,6 +13,7 @@
 SMEM = pl.BlockSpec(memory_space=pltpu.SMEM)
 MIB = 2**20
 LONG = pl.CostEstimate(flops=2 * 10**11, bytes_accessed=2**20, transcendentals=0)
+MIDDLE = pl.CostEstimate(flops=5 * 10**9, bytes_accessed=2**20, transcendentals=0)
 QUICK = pl.CostEstimate(flops=1, bytes_accessed=2**20, transcendentals=0)
 
 
@@ -225,7 +226,7 @@
         in_specs=[VMEM] * len(arrays),
         out_specs=[VMEM] * (1 + len(places) * keep),
         compiler_params=pltpu.CompilerParams(vmem_limit_bytes=size_of(arrays) + 12 * MIB),
-        cost_estimate=LONG,
+        cost_estimate=MIDDLE,
         name="chi",
     )(*arrays)
     return part, [(place, e) for place, e in zip(places, kept)] if keep else everyone

time: 110 us -> 109 us (level)
  Pallas kernels: 37.3 us -> 35.6 us
  transfers between devices with their start and end apart: 29 -> 29, of which waited for: 9 -> 8; matrix products, arithmetic and copies ran while one was open for 0% -> 0% of each run, Pallas kernels for 31% -> 31%
where the time goes in v5:
time: 109 us
  starting transfers between devices  40.1 us (37%)
  Pallas kernels  35.6 us (33%)
  waiting for transfers between devices  20.1 us (18%)
  blocking collectives  12 us (11%)
    ppermute x18, starting transfers between devices, along_high(): return lax.ppermute(array, 'pair', moves)  30.8 us
    pallas_call x3, Pallas kernels, polar(): pl.pallas_call(lambda *refs: polar_kernel(groups, lows, masks, *refs), ou...  15.4 us
    ppermute x18, waiting for transfers between devices, along_high(): return lax.ppermute(array, 'pair', moves)  13.2 us
    all_to_all x1, blocking collectives, per_device(): return jnp.sum(lax.all_to_all(part, 'pair', 0, 0, tiled=True), axis=0)  12 us
    pallas_call x3, Pallas kernels, split(): pl.pallas_call(lambda *refs: split_kernel(groups, lows, chunk, shares, co...  7.18 us
    pallas_call x2, Pallas kernels, chi(): pl.pallas_call(lambda *refs: chi_kernel(groups, lows, chunks, factor, pla...  6.75 us
    pallas_call x3, Pallas kernels, stack(): pl.pallas_call(lambda *refs: stack_kernel(groups, slots, *refs), out_shap...  6.24 us
    ppermute x8, starting transfers between devices, swap(): return lax.ppermute(array, 'aux', [(a, a ^ bit) for a in range(peers)])  4.68 us
  transfers between devices with their start and end apart: 29, of which 8 were waited for; matrix products, arithmetic and copies ran while one was open for 0% of the time, Pallas kernels for 31%

profile of v5, /device:TPU:0, one launch (start us, length us, event | category | flops | bytes accessed | tf_op | source)
XLA Modules:
  0.0 108.6 jit_solution(11763906799947715012)
XLA Ops:
  0.5 2.0 %split.4 = (bf16[4,128,128]{2,1,0:T(8,128)(2,1)}, bf16[6,128,128]{2,1,0:T(8,128)(2,1)}, bf16[6,128,128]{2,1,0:T(8,128)(2,1)}, bf16[6,128,128]{2,1,0:T(8,128)(2,1)}) custom-call(bf16[12,4,128,128]{3,2,1,0:T(8,128)(2,1)} %refs_0_.7, bf16[128,1024]{1,0:T(8,128)(2,1)} %refs_3_.5), custom_call_target="tpu_custom_call" | custom-call | flops 199999995904 | bytes 1048576 | tf_op jit(solution)/shard_map/split/pallas_call | solution.py:60
  2.5 2.6 %collective-permute-start = (bf16[6,128,128]{2,1,0:T(8,128)(2,1)}, bf16[6,128,128]{2,1,0:T(8,128)(2,1)}, u32[]{:S(2)}, u32[]{:S(2)}) collective-permute-start(bf16[6,128,128]{2,1,0:T(8,128)(2,1)} %get-tuple-element.123), channel_id=1, source_target_pairs={{0,2},{1,3},{2,4},{3,5},{4,6},{5,7},{6,0},{7,1},{8,10},{9,11},{10,... | collective-permute-start | bytes 589832 | tf_op jit(solution)/shard_map/ppermute | solution.py:247
  5.1 2.6 %collective-permute-start.1 = (bf16[6,128,128]{2,1,0:T(8,128)(2,1)}, bf16[6,128,128]{2,1,0:T(8,128)(2,1)}, u32[]{:S(2)}, u32[]{:S(2)}) collective-permute-start(bf16[6,128,128]{2,1,0:T(8,128)(2,1)} %get-tuple-element.124), channel_id=1, source_target_pairs={{0,4},{1,5},{2,6},{3,7},{4,0},{5,1},{6,2},{7,3},{8,12},{9,13},{10,... | collective-permute-start | bytes 589832 | tf_op jit(solution)/shard_map/ppermute | solution.py:247
  9.0 2.7 %split.3 = (bf16[4,128,128]{2,1,0:T(8,128)(2,1)}, bf16[4,128,128]{2,1,0:T(8,128)(2,1)}, bf16[4,128,128]{2,1,0:T(8,128)(2,1)}, bf16[4,128,128]{2,1,0:T(8,128)(2,1)}, bf16[7,4,128,128]{3,2,1,0:T(8,128)(2,1)}) custom-call(bf16[12,4,128,128]{3,2,1,0:T(8,128)(2,1)} %refs_0_.7), custom_call_target="tpu_custom_call" | custom-call | flops 199999995904 | bytes 1048576 | tf_op jit(solution)/shard_map/split/pallas_call | solution.py:60
  13.3 8.2 %collective-permute-done.1.refs_2_.refs_6_ = bf16[6,128,128]{2,1,0:T(8,128)(2,1)} collective-permute-done((bf16[6,128,128]{2,1,0:T(8,128)(2,1)}, bf16[6,128,128]{2,1,0:T(8,128)(2,1)}, u32[]{:S(2)}, u32[]{:S(2)}) %collective-permute-start.1) | collective-permute-done | bytes 196640 | tf_op jit(solution)/shard_map/ppermute | solution.py:247
  21.5 4.7 %collective-permute-start.4 = (bf16[4,128,128]{2,1,0:T(8,128)(2,1)}, bf16[4,128,128]{2,1,0:T(8,128)(2,1)}, u32[]{:S(2)}, u32[]{:S(2)}) collective-permute-start(bf16[4,128,128]{2,1,0:T(8,128)(2,1)} %get-tuple-element.137), channel_id=1, source_target_pairs={{0,2},{1,3},{2,4},{3,5},{4,6},{5,7},{6,0},{7,1},{8,10},{9,11},{10,... | collective-permute-start | bytes 393224 | tf_op jit(solution)/shard_map/ppermute | solution.py:247
  28.6 2.1 %stack.3 = (bf16[4,4,128,128]{3,2,1,0:T(8,128)(2,1)}, bf16[3,2,128,128]{3,2,1,0:T(8,128)(2,1)}) custom-call(bf16[4,128,128]{2,1,0:T(8,128)(2,1)} %get-tuple-element.144.refs_0_.refs_4_, bf16[6,128,128]{2,1,0:T(8,128)(2,1)} %collective-permute-done.refs_1_.refs_5_, bf16[6,128,128]{2,1,0:T(8,128)(2,1)} %collective-permute-done.1.refs_2_.refs_6_, ...), custom_call_target="tpu_custom_call" | custom-call | flops 199999995904 | bytes 1048576 | tf_op jit(solution)/shard_map/stack/pallas_call | solution.py:86
  32.2 2.5 %split.5 = (bf16[4,128,128]{2,1,0:T(8,128)(2,1)}, bf16[4,128,128]{2,1,0:T(8,128)(2,1)}, bf16[4,128,128]{2,1,0:T(8,128)(2,1)}, bf16[4,128,128]{2,1,0:T(8,128)(2,1)}, bf16[5,4,128,128]{3,2,1,0:T(8,128)(2,1)}) custom-call(bf16[12,4,128,128]{3,2,1,0:T(8,128)(2,1)} %refs_0_.7), custom_call_target="tpu_custom_call" | custom-call | flops 199999995904 | bytes 1048576 | tf_op jit(solution)/shard_map/split/pallas_call | solution.py:60
  38.1 1.8 %collective-permute-start.10 = (bf16[4,128,128]{2,1,0:T(8,128)(2,1)}, bf16[4,128,128]{2,1,0:T(8,128)(2,1)}, u32[]{:S(2)}, u32[]{:S(2)}) collective-permute-start(bf16[4,128,128]{2,1,0:T(8,128)(2,1)} %get-tuple-element.153), channel_id=1, source_target_pairs={{0,2},{1,3},{2,4},{3,5},{4,6},{5,7},{6,0},{7,1},{8,10},{9,11},{10,... | collective-permute-start | bytes 393224 | tf_op jit(solution)/shard_map/ppermute | solution.py:247
  42.1 2.1 %stack.5 = bf16[4,4,128,128]{3,2,1,0:T(8,128)(2,1)} custom-call(bf16[4,128,128]{2,1,0:T(8,128)(2,1)} %get-tuple-element.171.refs_0_.refs_4_, bf16[4,128,128]{2,1,0:T(8,128)(2,1)} %collective-permute-done.4.refs_1_.refs_5_, bf16[4,128,128]{2,1,0:T(8,128)(2,1)} %collective-permute-done.5.refs_2_.refs_6_, ...), custom_call_target="tpu_custom_call" | custom-call | flops 199999995904 | bytes 1048576 | tf_op jit(solution)/shard_map/stack/pallas_call | solution.py:86
  46.5 1.8 %collective-permute-done.13.refs_8_ = bf16[4,4,128,128]{3,2,1,0:T(8,128)(2,1)} collective-permute-done((bf16[4,4,128,128]{3,2,1,0:T(8,128)(2,1)}, bf16[4,4,128,128]{3,2,1,0:T(8,128)(2,1)}, u32[]{:S(2)}, u32[]{:S(2)}) %collective-permute-start.13) | collective-permute-done | bytes 524320 | tf_op jit(solution)/shard_map/ppermute | solution.py:253
  48.6 5.4 %polar.3 = (bf16[4,128,128]{2,1,0:T(8,128)(2,1)S(1)}, bf16[4,128,128]{2,1,0:T(8,128)(2,1)}, bf16[4,128,128]{2,1,0:T(8,128)(2,1)}, bf16[4,128,128]{2,1,0:T(8,128)(2,1)}) custom-call(s32[8,4]{1,0:T(8,128)S(1)} %copy.8.refs_0_, s32[8]{0:T(128)S(1)} %copy-done.4, bf16[1024,1024]{1,0:T(8,128)(2,1)S(1)} %copy-done.1, bf16[128,1024]{1,0:T(8,128)(2,1)S(1)} %copy-done.3, ...), custom_call_target="tpu_custom_call" | custom-call | flops 199999995904 | bytes 1048576 | tf_op jit(solution)/shard_map/polar/pallas_call | solution.py:152
  56.3 1.7 %collective-permute-start.20 = (bf16[4,128,128]{2,1,0:T(8,128)(2,1)}, bf16[4,128,128]{2,1,0:T(8,128)(2,1)}, u32[]{:S(2)}, u32[]{:S(2)}) collective-permute-start(bf16[4,128,128]{2,1,0:T(8,128)(2,1)} %get-tuple-element.186), channel_id=1, source_target_pairs={{0,6},{1,7},{2,0},{3,1},{4,2},{5,3},{6,4},{7,5},{8,14},{9,15},{10,... | collective-permute-start | bytes 393224 | tf_op jit(solution)/shard_map/ppermute | solution.py:247
  58.1 2.0 %stack.4 = bf16[4,4,128,128]{3,2,1,0:T(8,128)(2,1)} custom-call(bf16[4,128,128]{2,1,0:T(8,128)(2,1)} %get-tuple-element.163.refs_0_.refs_4_, bf16[4,128,128]{2,1,0:T(8,128)(2,1)} %collective-permute-done.10.refs_1_.refs_5_, bf16[4,128,128]{2,1,0:T(8,128)(2,1)} %collective-permute-done.11.refs_2_.refs_6_, ...), custom_call_target="tpu_custom_call" | custom-call | flops 1 | bytes 1048576 | tf_op jit(solution)/shard_map/stack/pallas_call | solution.py:86
  60.1 3.1 %collective-permute-done.9 = bf16[5,4,128,128]{3,2,1,0:T(8,128)(2,1)} collective-permute-done((bf16[5,4,128,128]{3,2,1,0:T(8,128)(2,1)}, bf16[5,4,128,128]{3,2,1,0:T(8,128)(2,1)}, u32[]{:S(2)}, u32[]{:S(2)}) %collective-permute-start.9) | collective-permute-done | bytes 655392 | tf_op jit(solution)/shard_map/ppermute | solution.py:256
  64.7 5.3 %polar.4 = (bf16[4,128,128]{2,1,0:T(8,128)(2,1)S(1)}, bf16[4,128,128]{2,1,0:T(8,128)(2,1)}, bf16[4,128,128]{2,1,0:T(8,128)(2,1)}, bf16[4,128,128]{2,1,0:T(8,128)(2,1)}) custom-call(s32[8,4]{1,0:T(8,128)S(1)} %copy.8.refs_0_, s32[8]{0:T(128)S(1)} %copy-done.4, bf16[1024,1024]{1,0:T(8,128)(2,1)S(1)} %copy-done.1, bf16[128,1024]{1,0:T(8,128)(2,1)S(1)} %copy-done.3, ...), custom_call_target="tpu_custom_call" | custom-call | flops 199999995904 | bytes 1048576 | tf_op jit(solution)/shard_map/polar/pallas_call | solution.py:152
  70.2 2.0 %collective-permute-start.22 = (bf16[4,128,128]{2,1,0:T(8,128)(2,1)}, bf16[4,128,128]{2,1,0:T(8,128)(2,1)}, u32[]{:S(2)}, u32[]{:S(2)}) collective-permute-start(bf16[4,128,128]{2,1,0:T(8,128)(2,1)} %get-tuple-element.201), channel_id=1, source_target_pairs={{0,4},{1,5},{2,6},{3,7},{4,0},{5,1},{6,2},{7,3},{8,12},{9,13},{10,... | collective-permute-start | bytes 393224 | tf_op jit(solution)/shard_map/ppermute | solution.py:247
  72.2 1.8 %collective-permute-start.23 = (bf16[4,128,128]{2,1,0:T(8,128)(2,1)}, bf16[4,128,128]{2,1,0:T(8,128)(2,1)}, u32[]{:S(2)}, u32[]{:S(2)}) collective-permute-start(bf16[4,128,128]{2,1,0:T(8,128)(2,1)} %get-tuple-element.202), channel_id=1, source_target_pairs={{0,6},{1,7},{2,0},{3,1},{4,2},{5,3},{6,4},{7,5},{8,14},{9,15},{10,... | collective-permute-start | bytes 393224 | tf_op jit(solution)/shard_map/ppermute | solution.py:247
  74.4 4.7 %polar.5 = (bf16[4,128,128]{2,1,0:T(8,128)(2,1)S(1)}, bf16[4,128,128]{2,1,0:T(8,128)(2,1)S(1)}, bf16[4,128,128]{2,1,0:T(8,128)(2,1)S(1)}, bf16[4,128,128]{2,1,0:T(8,128)(2,1)S(1)}) custom-call(s32[8,4]{1,0:T(8,128)S(1)} %copy.8.refs_0_, s32[8]{0:T(128)S(1)} %copy-done.4, bf16[1024,1024]{1,0:T(8,128)(2,1)S(1)} %copy-done.1, bf16[128,1024]{1,0:T(8,128)(2,1)S(1)} %copy-done.3, ...), custom_call_target="tpu_custom_call" | custom-call | flops 199999995904 | bytes 1048576 | tf_op jit(solution)/shard_map/polar/pallas_call | solution.py:152
  81.2 2.7 %collective-permute-start.26 = (bf16[4,128,128]{2,1,0:T(8,128)(2,1)S(1)}, bf16[4,128,128]{2,1,0:T(8,128)(2,1)S(1)}, u32[]{:S(2)}, u32[]{:S(2)}) collective-permute-start(bf16[4,128,128]{2,1,0:T(8,128)(2,1)S(1)} %get-tuple-element.220), channel_id=1, source_target_pairs={{0,2},{1,3},{2,4},{3,5},{4,6},{5,7},{6,0},{7,1},{8,10},{9,11},{10,... | collective-permute-start | bytes 393224 | tf_op jit(solution)/shard_map/ppermute | solution.py:247
  86.3 4.9 %chi.2 = (f32[8,6,12]{2,1,0:T(8,128)S(1)}, bf16[12,512,128]{2,1,0:T(8,128)(2,1)S(1)}, bf16[7,512,128]{2,1,0:T(8,128)(2,1)S(1)}, bf16[12,512,128]{2,1,0:T(8,128)(...) custom-call(bf16[12,512,128]{2,1,0:T(8,128)(2,1)S(1)} %bitcast.19, ...), custom_call_target="tpu_custom_call" | custom-call | flops 5000000000 | bytes 1048576 | tf_op jit(solution)/shard_map/chi/pallas_call | solution.py:222
  91.2 2.9 %collective-permute-done.27 = bf16[4,128,128]{2,1,0:T(8,128)(2,1)S(1)} collective-permute-done((bf16[4,128,128]{2,1,0:T(8,128)(2,1)S(1)}, bf16[4,128,128]{2,1,0:T(8,128)(2,1)S(1)}, u32[]{:S(2)}, u32[]{:S(2)}) %collective-permute-start.27) | collective-permute-done | bytes 131104 | tf_op jit(solution)/shard_map/ppermute | solution.py:247
  94.1 1.9 %chi.3 = f32[8,6,12]{2,1,0:T(8,128)S(1)} custom-call(bf16[12,512,128]{2,1,0:T(8,128)(2,1)S(1)} %get-tuple-element.213.refs_0_, bf16[7,512,128]{2,1,0:T(8,128)(2,1)S(1)} %get-tuple-element.214.refs_1_, bf16[12,512,128]{2,1,0:T(8,128)(2,1)S(1)} %get-tuple-element.215.refs_2_, bf16[5,512,128]{2,1,0:T(8,128)(2,1)S(1)} %get-tuple-element.216.refs_3_, ...), custom_call_target="tpu_custom_call" | custom-call | flops 5000000000 | bytes 1048576 | tf_op jit(solution)/shard_map/chi/pallas_call | solution.py:222
  96.0 12.0 %all_to_all.5 = f32[8,6,12]{2,1,0:T(8,128)S(1)} all-to-all(f32[8,6,12]{2,1,0:T(8,128)S(1)} %chi.3), channel_id=1, replica_groups=mesh['aux'=4,'pair'=8] {'pair'}, dimensions={0} | all-to-all | bytes 4608 | tf_op jit(solution)/shard_map/all_to_all | solution.py:339
  (64 shorter events, 24.9 us)
Async XLA Ops:
  0.0 21.5 %collective-permute-start.3 = (bf16[12,4,128,128]{3,2,1,0:T(8,128)(2,1)}, bf16[12,4,128,128]{3,2,1,0:T(8,128)(2,1)}, u32[]{:S(2)}, u32[]{:S(2)}) collective-permute-start(bf16[12,4,128,128]{3,2,1,0:T(8,128)(2,1)} %refs_0_.7), channel_id=1, source_target_pairs={{0,8},{8,0},{16,24},{24,16},{1,9},{9,1},{17,25},{25,17},{2,10},{10... | collective-permute-start | bytes 4718600 | tf_op jit(solution)/shard_map/ppermute | solution.py:256
  2.5 10.8 %collective-permute-start = (bf16[6,128,128]{2,1,0:T(8,128)(2,1)}, bf16[6,128,128]{2,1,0:T(8,128)(2,1)}, u32[]{:S(2)}, u32[]{:S(2)}) collective-permute-start(bf16[6,128,128]{2,1,0:T(8,128)(2,1)} %get-tuple-element.123), channel_id=1, source_target_pairs={{0,2},{1,3},{2,4},{3,5},{4,6},{5,7},{6,0},{7,1},{8,10},{9,11},{10,... | collective-permute-start | bytes 589832 | tf_op jit(solution)/shard_map/ppermute | solution.py:247
  5.1 16.4 %collective-permute-start.1 = (bf16[6,128,128]{2,1,0:T(8,128)(2,1)}, bf16[6,128,128]{2,1,0:T(8,128)(2,1)}, u32[]{:S(2)}, u32[]{:S(2)}) collective-permute-start(bf16[6,128,128]{2,1,0:T(8,128)(2,1)} %get-tuple-element.124), channel_id=1, source_target_pairs={{0,4},{1,5},{2,6},{3,7},{4,0},{5,1},{6,2},{7,3},{8,12},{9,13},{10,... | collective-permute-start | bytes 589832 | tf_op jit(solution)/shard_map/ppermute | solution.py:247
  7.7 13.9 %collective-permute-start.2 = (bf16[6,128,128]{2,1,0:T(8,128)(2,1)}, bf16[6,128,128]{2,1,0:T(8,128)(2,1)}, u32[]{:S(2)}, u32[]{:S(2)}) collective-permute-start(bf16[6,128,128]{2,1,0:T(8,128)(2,1)} %get-tuple-element.125), channel_id=1, source_target_pairs={{0,6},{1,7},{2,0},{3,1},{4,2},{5,3},{6,4},{7,5},{8,14},{9,15},{10,... | collective-permute-start | bytes 589832 | tf_op jit(solution)/shard_map/ppermute | solution.py:247
  11.7 23.0 %collective-permute-start.8 = (bf16[7,4,128,128]{3,2,1,0:T(8,128)(2,1)}, bf16[7,4,128,128]{3,2,1,0:T(8,128)(2,1)}, u32[]{:S(2)}, u32[]{:S(2)}) collective-permute-start(bf16[7,4,128,128]{3,2,1,0:T(8,128)(2,1)} %get-tuple-element.121), channel_id=1, source_target_pairs={{0,16},{8,24},{16,0},{24,8},{1,17},{9,25},{17,1},{25,9},{2,18},{10... | collective-permute-start | bytes 2752520 | tf_op jit(solution)/shard_map/ppermute | solution.py:256
  21.5 14.7 %collective-permute-start.4 = (bf16[4,128,128]{2,1,0:T(8,128)(2,1)}, bf16[4,128,128]{2,1,0:T(8,128)(2,1)}, u32[]{:S(2)}, u32[]{:S(2)}) collective-permute-start(bf16[4,128,128]{2,1,0:T(8,128)(2,1)} %get-tuple-element.137), channel_id=1, source_target_pairs={{0,2},{1,3},{2,4},{3,5},{4,6},{5,7},{6,0},{7,1},{8,10},{9,11},{10,... | collective-permute-start | bytes 393224 | tf_op jit(solution)/shard_map/ppermute | solution.py:247
  26.2 10.4 %collective-permute-start.5 = (bf16[4,128,128]{2,1,0:T(8,128)(2,1)}, bf16[4,128,128]{2,1,0:T(8,128)(2,1)}, u32[]{:S(2)}, u32[]{:S(2)}) collective-permute-start(bf16[4,128,128]{2,1,0:T(8,128)(2,1)} %get-tuple-element.138), channel_id=1, source_target_pairs={{0,4},{1,5},{2,6},{3,7},{4,0},{5,1},{6,2},{7,3},{8,12},{9,13},{10,... | collective-permute-start | bytes 393224 | tf_op jit(solution)/shard_map/ppermute | solution.py:247
  27.8 8.9 %collective-permute-start.6 = (bf16[4,128,128]{2,1,0:T(8,128)(2,1)}, bf16[4,128,128]{2,1,0:T(8,128)(2,1)}, u32[]{:S(2)}, u32[]{:S(2)}) collective-permute-start(bf16[4,128,128]{2,1,0:T(8,128)(2,1)} %get-tuple-element.139), channel_id=1, source_target_pairs={{0,6},{1,7},{2,0},{3,1},{4,2},{5,3},{6,4},{7,5},{8,14},{9,15},{10,... | collective-permute-start | bytes 393224 | tf_op jit(solution)/shard_map/ppermute | solution.py:247
  34.7 13.6 %collective-permute-start.13 = (bf16[4,4,128,128]{3,2,1,0:T(8,128)(2,1)}, bf16[4,4,128,128]{3,2,1,0:T(8,128)(2,1)}, u32[]{:S(2)}, u32[]{:S(2)}) collective-permute-start(bf16[4,4,128,128]{3,2,1,0:T(8,128)(2,1)} %get-tuple-element.156), channel_id=1, source_target_pairs={{0,1},{1,0},{2,3},{3,2},{4,5},{5,4},{6,7},{7,6},{8,9},{9,8},{10,11... | collective-permute-start | bytes 1572872 | tf_op jit(solution)/shard_map/ppermute | solution.py:253
  38.1 15.8 %collective-permute-start.10 = (bf16[4,128,128]{2,1,0:T(8,128)(2,1)}, bf16[4,128,128]{2,1,0:T(8,128)(2,1)}, u32[]{:S(2)}, u32[]{:S(2)}) collective-permute-start(bf16[4,128,128]{2,1,0:T(8,128)(2,1)} %get-tuple-element.153), channel_id=1, source_target_pairs={{0,2},{1,3},{2,4},{3,5},{4,6},{5,7},{6,0},{7,1},{8,10},{9,11},{10,... | collective-permute-start | bytes 393224 | tf_op jit(solution)/shard_map/ppermute | solution.py:247
  40.0 14.0 %collective-permute-start.11 = (bf16[4,128,128]{2,1,0:T(8,128)(2,1)}, bf16[4,128,128]{2,1,0:T(8,128)(2,1)}, u32[]{:S(2)}, u32[]{:S(2)}) collective-permute-start(bf16[4,128,128]{2,1,0:T(8,128)(2,1)} %get-tuple-element.154), channel_id=1, source_target_pairs={{0,4},{1,5},{2,6},{3,7},{4,0},{5,1},{6,2},{7,3},{8,12},{9,13},{10,... | collective-permute-start | bytes 393224 | tf_op jit(solution)/shard_map/ppermute | solution.py:247
  44.3 9.7 %collective-permute-start.12 = (bf16[4,128,128]{2,1,0:T(8,128)(2,1)}, bf16[4,128,128]{2,1,0:T(8,128)(2,1)}, u32[]{:S(2)}, u32[]{:S(2)}) collective-permute-start(bf16[4,128,128]{2,1,0:T(8,128)(2,1)} %get-tuple-element.155), channel_id=1, source_target_pairs={{0,6},{1,7},{2,0},{3,1},{4,2},{5,3},{6,4},{7,5},{8,14},{9,15},{10,... | collective-permute-start | bytes 393224 | tf_op jit(solution)/shard_map/ppermute | solution.py:247
  45.0 19.8 %collective-permute-start.17 = (bf16[4,4,128,128]{3,2,1,0:T(8,128)(2,1)}, bf16[4,4,128,128]{3,2,1,0:T(8,128)(2,1)}, u32[]{:S(2)}, u32[]{:S(2)}) collective-permute-start(bf16[4,4,128,128]{3,2,1,0:T(8,128)(2,1)} %stack.5), channel_id=1, source_target_pairs={{0,1},{1,0},{2,3},{3,2},{4,5},{5,4},{6,7},{7,6},{8,9},{9,8},{10,11... | collective-permute-start | bytes 1572872 | tf_op jit(solution)/shard_map/ppermute | solution.py:253
  48.3 14.9 %collective-permute-start.9 = (bf16[5,4,128,128]{3,2,1,0:T(8,128)(2,1)}, bf16[5,4,128,128]{3,2,1,0:T(8,128)(2,1)}, u32[]{:S(2)}, u32[]{:S(2)}) collective-permute-start(bf16[5,4,128,128]{3,2,1,0:T(8,128)(2,1)} %get-tuple-element.143), channel_id=1, source_target_pairs={{0,16},{8,24},{16,0},{24,8},{1,17},{9,25},{17,1},{25,9},{2,18},{10... | collective-permute-start | bytes 1966088 | tf_op jit(solution)/shard_map/ppermute | solution.py:256
  54.0 16.1 %collective-permute-start.18 = (bf16[4,128,128]{2,1,0:T(8,128)(2,1)}, bf16[4,128,128]{2,1,0:T(8,128)(2,1)}, u32[]{:S(2)}, u32[]{:S(2)}) collective-permute-start(bf16[4,128,128]{2,1,0:T(8,128)(2,1)} %get-tuple-element.184), channel_id=1, source_target_pairs={{0,2},{1,3},{2,4},{3,5},{4,6},{5,7},{6,0},{7,1},{8,10},{9,11},{10,... | collective-permute-start | bytes 393224 | tf_op jit(solution)/shard_map/ppermute | solution.py:247
  54.8 15.2 %collective-permute-start.19 = (bf16[4,128,128]{2,1,0:T(8,128)(2,1)}, bf16[4,128,128]{2,1,0:T(8,128)(2,1)}, u32[]{:S(2)}, u32[]{:S(2)}) collective-permute-start(bf16[4,128,128]{2,1,0:T(8,128)(2,1)} %get-tuple-element.185), channel_id=1, source_target_pairs={{0,4},{1,5},{2,6},{3,7},{4,0},{5,1},{6,2},{7,3},{8,12},{9,13},{10,... | collective-permute-start | bytes 393224 | tf_op jit(solution)/shard_map/ppermute | solution.py:247
  56.3 13.7 %collective-permute-start.20 = (bf16[4,128,128]{2,1,0:T(8,128)(2,1)}, bf16[4,128,128]{2,1,0:T(8,128)(2,1)}, u32[]{:S(2)}, u32[]{:S(2)}) collective-permute-start(bf16[4,128,128]{2,1,0:T(8,128)(2,1)} %get-tuple-element.186), channel_id=1, source_target_pairs={{0,6},{1,7},{2,0},{3,1},{4,2},{5,3},{6,4},{7,5},{8,14},{9,15},{10,... | collective-permute-start | bytes 393224 | tf_op jit(solution)/shard_map/ppermute | solution.py:247
  63.2 11.2 %collective-permute-start.16 = (bf16[4,4,128,128]{3,2,1,0:T(8,128)(2,1)}, bf16[4,4,128,128]{3,2,1,0:T(8,128)(2,1)}, u32[]{:S(2)}, u32[]{:S(2)}) collective-permute-start(bf16[4,4,128,128]{3,2,1,0:T(8,128)(2,1)} %stack.4), channel_id=1, source_target_pairs={{0,1},{1,0},{2,3},{3,2},{4,5},{5,4},{6,7},{7,6},{8,9},{9,8},{10,11... | collective-permute-start | bytes 1572872 | tf_op jit(solution)/shard_map/ppermute | solution.py:253
  70.1 9.0 %collective-permute-start.21 = (bf16[4,128,128]{2,1,0:T(8,128)(2,1)}, bf16[4,128,128]{2,1,0:T(8,128)(2,1)}, u32[]{:S(2)}, u32[]{:S(2)}) collective-permute-start(bf16[4,128,128]{2,1,0:T(8,128)(2,1)} %get-tuple-element.200), channel_id=1, source_target_pairs={{0,2},{1,3},{2,4},{3,5},{4,6},{5,7},{6,0},{7,1},{8,10},{9,11},{10,... | collective-permute-start | bytes 393224 | tf_op jit(solution)/shard_map/ppermute | solution.py:247
  70.2 10.5 %collective-permute-start.22 = (bf16[4,128,128]{2,1,0:T(8,128)(2,1)}, bf16[4,128,128]{2,1,0:T(8,128)(2,1)}, u32[]{:S(2)}, u32[]{:S(2)}) collective-permute-start(bf16[4,128,128]{2,1,0:T(8,128)(2,1)} %get-tuple-element.201), channel_id=1, source_target_pairs={{0,4},{1,5},{2,6},{3,7},{4,0},{5,1},{6,2},{7,3},{8,12},{9,13},{10,... | collective-permute-start | bytes 393224 | tf_op jit(solution)/shard_map/ppermute | solution.py:247
  72.2 8.5 %collective-permute-start.23 = (bf16[4,128,128]{2,1,0:T(8,128)(2,1)}, bf16[4,128,128]{2,1,0:T(8,128)(2,1)}, u32[]{:S(2)}, u32[]{:S(2)}) collective-permute-start(bf16[4,128,128]{2,1,0:T(8,128)(2,1)} %get-tuple-element.202), channel_id=1, source_target_pairs={{0,6},{1,7},{2,0},{3,1},{4,2},{5,3},{6,4},{7,5},{8,14},{9,15},{10,... | collective-permute-start | bytes 393224 | tf_op jit(solution)/shard_map/ppermute | solution.py:247
  81.2 10.0 %collective-permute-start.26 = (bf16[4,128,128]{2,1,0:T(8,128)(2,1)S(1)}, bf16[4,128,128]{2,1,0:T(8,128)(2,1)S(1)}, u32[]{:S(2)}, u32[]{:S(2)}) collective-permute-start(bf16[4,128,128]{2,1,0:T(8,128)(2,1)S(1)} %get-tuple-element.220), channel_id=1, source_target_pairs={{0,2},{1,3},{2,4},{3,5},{4,6},{5,7},{6,0},{7,1},{8,10},{9,11},{10,... | collective-permute-start | bytes 393224 | tf_op jit(solution)/shard_map/ppermute | solution.py:247
  83.9 10.2 %collective-permute-start.27 = (bf16[4,128,128]{2,1,0:T(8,128)(2,1)S(1)}, bf16[4,128,128]{2,1,0:T(8,128)(2,1)S(1)}, u32[]{:S(2)}, u32[]{:S(2)}) collective-permute-start(bf16[4,128,128]{2,1,0:T(8,128)(2,1)S(1)} %get-tuple-element.221), channel_id=1, source_target_pairs={{0,4},{1,5},{2,6},{3,7},{4,0},{5,1},{6,2},{7,3},{8,12},{9,13},{10,... | collective-permute-start | bytes 393224 | tf_op jit(solution)/shard_map/ppermute | solution.py:247
  85.1 9.0 %collective-permute-start.28 = (bf16[4,128,128]{2,1,0:T(8,128)(2,1)S(1)}, bf16[4,128,128]{2,1,0:T(8,128)(2,1)S(1)}, u32[]{:S(2)}, u32[]{:S(2)}) collective-permute-start(bf16[4,128,128]{2,1,0:T(8,128)(2,1)S(1)} %get-tuple-element.222), channel_id=1, source_target_pairs={{0,6},{1,7},{2,0},{3,1},{4,2},{5,3},{6,4},{7,5},{8,14},{9,15},{10,... | collective-permute-start | bytes 393224 | tf_op jit(solution)/shard_map/ppermute | solution.py:247
  (13 other events, 92.2 us)
